TPU v7x, 512 devices: a whole 4x4x16 slice. The times are simulated.
512 devices in a mesh: tm: 64 (over y, x, z_hi, core), section: 8 (over z_lo).
Axes of the slice: x: 4, y: 4, z: 16 (z_hi: 2, z_lo: 8; z = z_hi * 8 + z_lo), core: 2. Of those that a mesh axis runs over, the one named last changes fastest.
Arguments:
- layer_five: bfloat16 [16, 8192, 512], P('section', 'tm'), may hold values from -6 to 6
- conv_six: bfloat16 [1024, 512], P('tm'), may hold values from -0.1875 to 0.1875
- conv_seven: bfloat16 [1024, 512], P('tm'), may hold values from -0.1875 to 0.1875
- gains: float32 [3, 512], replicated, may hold values from 0.25 to 1.75
- biases: float32 [3, 512], replicated, may hold values from -1.5 to 1.5
- proj_weight: bfloat16 [512, 1920], P(None, 'section'), may hold values from -0.25 to 0.25
- feature_grad: bfloat16 [16, 2048, 1920], P(None, ('tm', 'section')), may hold values from -0.08984375 to 0.08984375
Outputs:
- grad_layer_five: bfloat16 [16, 8192, 512], P('section', 'tm')
- grad_conv_six: float32 [1024, 512], P('tm', 'section')
- grad_conv_seven: float32 [1024, 512], P('tm', 'section')
- grad_proj: float32 [512, 1920], P('tm', 'section')
- grad_gains: float32 [3, 512], replicated
- grad_biases: float32 [3, 512], replicated
All inputs are finite; a program needn't handle non-finite values.
Results may differ from a plain program's by a relative error of at most 0.023.
Values may be sent and summed in bfloat16 or wider, within the bound.
No kernel may reach another device: no remote copies, remote signals or barrier semaphores. Data moves between devices by JAX's collectives and lax.ppermute only.
A program may use at most 64 MiB of HBM per device.

v0:
```python
import jax
import jax.numpy as jnp
from jax import lax
from jax.sharding import PartitionSpec as P

norm_epsilon = 1e-05
half_root = 0.7071067811865476
inv_root_tau = 0.3989422804014327


def gelu_parts(preact):
    normal_cdf = 0.5 * (1.0 + lax.erf(preact * half_root))
    density = jnp.exp(-0.5 * preact * preact) * inv_root_tau
    return (preact * normal_cdf, normal_cdf + preact * density)


def norm_forward(hidden, gain_row, bias_row):
    average = jnp.mean(hidden, axis=-1, keepdims=True)
    centred = hidden - average
    inv_scale = lax.rsqrt(jnp.mean(centred * centred, axis=-1, keepdims=True) + norm_epsilon)
    normal_part = centred * inv_scale
    return (normal_part * gain_row + bias_row, normal_part, inv_scale)


def norm_backward(incoming, normal_part, inv_scale, gain_row):
    scaled = incoming * gain_row
    first_mean = jnp.mean(scaled, axis=-1, keepdims=True)
    second_mean = jnp.mean(scaled * normal_part, axis=-1, keepdims=True)
    return inv_scale * (scaled - first_mean - normal_part * second_mean)


def rounded(value):
    narrow = lax.optimization_barrier(value.astype(jnp.bfloat16))
    return narrow.astype(jnp.float32)


def weight_terms(inputs, grad_rows, utt_local):
    channels_in = inputs.shape[1]
    section_count = lax.axis_size("section")
    block_width = grad_rows.shape[1] // section_count
    own_inputs = inputs.reshape(utt_local, -1, channels_in)
    own_grads = grad_rows.reshape(utt_local, -1, grad_rows.shape[1])
    column_part = lax.all_to_all(own_grads, "section", split_axis=2, concat_axis=0, tiled=True)
    portion = lax.all_gather(own_inputs, "section", axis=0, tiled=True)
    sources = portion.shape[0] // utt_local
    portion_in = portion.reshape(sources, -1, channels_in)
    portion_grad = column_part.reshape(sources, -1, block_width)
    product = jnp.einsum(
        "srk,src->sck", portion_in, portion_grad, preferred_element_type=jnp.float32
    )
    return jnp.sum(rounded(product), axis=0)


def on_device(layer_five, conv_six, conv_seven, gains, biases, proj_weight, feature_grad):
    utt_local, positions, channels = layer_five.shape
    frames_local = positions // 4
    kernel_six, kernel_seven = (
        lax.all_gather(conv_six, "tm", axis=0, tiled=True),
        lax.all_gather(conv_seven, "tm", axis=0, tiled=True),
    )
    unf_six = layer_five.reshape(-1, 2 * channels)
    hid_six = jnp.dot(unf_six, kernel_six, preferred_element_type=jnp.float32)
    pre_six, part_six, scale_six = norm_forward(hid_six, gains[0], biases[0])
    act_six_f, deriv_six = gelu_parts(pre_six)
    act_six = act_six_f.astype(jnp.bfloat16)
    unf_seven = act_six.reshape(-1, 2 * channels)
    hid_seven = jnp.dot(unf_seven, kernel_seven, preferred_element_type=jnp.float32)
    pre_seven, part_seven, scale_seven = norm_forward(hid_seven, gains[1], biases[1])
    act_seven_f, deriv_seven = gelu_parts(pre_seven)
    act_seven = act_seven_f.astype(jnp.bfloat16)
    pre_feat, part_feat, scale_feat = norm_forward(
        act_seven.astype(jnp.float32), gains[2], biases[2]
    )
    normed = pre_feat.astype(jnp.bfloat16).reshape(utt_local, frames_local, channels)
    column_grad = lax.all_to_all(feature_grad, "section", split_axis=2, concat_axis=1, tiled=True)
    grad_part = column_grad
    proj_term = jnp.einsum(
        "ufc,ufp->pc",
        lax.all_gather(normed, "section", axis=0, tiled=True),
        grad_part,
        preferred_element_type=jnp.float32,
    )
    grad_part = column_grad
    product = jnp.einsum("ufp,cp->ufc", grad_part, proj_weight, preferred_element_type=jnp.float32)
    grad_normed = (
        lax.psum_scatter(
            rounded(product).astype(jnp.bfloat16), "section", scatter_dimension=0, tiled=True
        )
        .astype(jnp.float32)
        .reshape(-1, channels)
    )
    dact_seven = norm_backward(grad_normed, part_feat, scale_feat, gains[2])
    dpre_seven = dact_seven * deriv_seven
    dhid_seven = norm_backward(dpre_seven, part_seven, scale_seven, gains[1]).astype(jnp.bfloat16)
    term_seven = weight_terms(unf_seven, dhid_seven, utt_local)
    dact_six = lax.dot_general(
        dhid_seven, kernel_seven, (((1,), (1,)), ((), ())), preferred_element_type=jnp.float32
    ).reshape(-1, channels)
    dpre_six = dact_six * deriv_six
    dhid_six = norm_backward(dpre_six, part_six, scale_six, gains[0]).astype(jnp.bfloat16)
    term_six = weight_terms(unf_six, dhid_six, utt_local)
    grad_input = lax.dot_general(
        dhid_six, kernel_six, (((1,), (1,)), ((), ())), preferred_element_type=jnp.float32
    )
    grad_layer_five = grad_input.reshape(utt_local, positions, channels).astype(jnp.bfloat16)
    wide_seven, wide_six, wide_proj = (
        lax.psum_scatter(term_seven, "tm", scatter_dimension=1, tiled=True),
        lax.psum_scatter(term_six, "tm", scatter_dimension=1, tiled=True),
        lax.psum_scatter(proj_term, "tm", scatter_dimension=1, tiled=True),
    )
    gain_terms = jnp.stack(
        [
            jnp.sum(dpre_six * part_six, axis=0),
            jnp.sum(dpre_seven * part_seven, axis=0),
            jnp.sum(grad_normed * part_feat, axis=0),
        ]
    )
    bias_terms = jnp.stack(
        [jnp.sum(dpre_six, axis=0), jnp.sum(dpre_seven, axis=0), jnp.sum(grad_normed, axis=0)]
    )
    grad_gains, grad_biases = lax.psum((gain_terms, bias_terms), ("tm", "section"))
    return (grad_layer_five, wide_six.T, wide_seven.T, wide_proj.T, grad_gains, grad_biases)


def solution(mesh):
    return jax.shard_map(
        on_device,
        mesh=mesh,
        in_specs=(
            P("section", "tm", None),
            P("tm", None),
            P("tm", None),
            P(),
            P(),
            P(None, "section"),
            P(None, ("tm", "section"), None),
        ),
        out_specs=(
            P("section", "tm", None),
            P("tm", "section"),
            P("tm", "section"),
            P("tm", "section"),
            P(),
            P(),
        ),
        check_vma=False,
    )
```

profile of v0, /device:TPU:64, one launch (start us, length us, event | category | flops | bytes accessed | tf_op | source)
XLA Modules:
  0.0 2079.6 jit_solution(497287820516145287)
XLA Ops:
  8.1 2.9 copy.36
  10.9 2.1 reshape.139
  13.0 26.4 %all_to_all.48 = bf16[8,2,7680]{2,1,0:T(2,128)(2,1)S(1)} all-to-all(bf16[8,2,7680]{2,1,0:T(2,128)(2,1)S(1)} %reshape.139), channel_id=1, replica_groups=mesh['tm'=64,'section'=8] {'section'}, dimensions={0} | all-to-all | bytes 491520 | tf_op jit(solution)/shard_map/all_to_all | solution.py:75
  39.4 1.3 reshape.140
  40.7 1.1 copy.37
  41.8 0.2 all_to_all.38
  42.0 1.1 convolution_convert_fusion.2
  43.1 0.0 all-gather.5.cloned.1.call-start
  43.2 0.5 all-gather.5.cloned.1.call-update
  43.7 0.0 all-gather.7.cloned.1.call-start
  43.8 0.5 all-gather.7.cloned.1.call-update
  44.3 0.0 all-gather.9.cloned.1.call-start
  44.4 0.8 reshape_reshape.6
  45.2 0.0 all-gather.11.cloned.1.call-start
  45.2 0.1 reshape.120
  45.4 53.4 %reduce-scatter.11.cloned.1.call-done = bf16[2,32,512]{2,1,0:T(8,128)(2,1)} async-done(((bf16[16,32,512]{2,1,0:T(8,128)(2,1)}), bf16[2,32,512]{2,1,0:T(8,128)(2,1)}) %reduce-scatter.11.cloned.1.call-update) | async-done | bytes 65552 | tf_op jit(solution)/shard_map/reduce_scatter | solution.py:86
  98.8 0.9 convert_reduce_fusion.3
  99.7 0.1 div.45
  99.8 44.4 %all-gather.5.cloned.1.call-done = bf16[1024,512]{1,0:T(8,128)(2,1)} async-done(((bf16[16,512]{1,0:T(8,128)(2,1)}), bf16[1024,512]{1,0:T(8,128)(2,1)}) %all-gather.5.cloned.1.call-update) | async-done | bytes 1048592 | tf_op jit(solution)/shard_map/all_gather | solution.py:58
  144.3 1.6 fusion.30
  145.9 0.2 multiply_reduce_fusion.2
  146.1 0.2 multiply_convert_fusion.1
  146.3 0.7 reshape_reshape.7
  147.0 93.9 %all-gather.7.cloned.1.call-done = bf16[1024,512]{1,0:T(8,128)(2,1)} async-done(((bf16[16,512]{1,0:T(8,128)(2,1)}), bf16[1024,512]{1,0:T(8,128)(2,1)}) %all-gather.7.cloned.1.call-update) | async-done | bytes 1048592 | tf_op jit(solution)/shard_map/all_gather | solution.py:59
  241.0 1.7 fusion.31
  242.7 0.2 multiply_reduce_fusion.6
  242.9 0.2 convert_reduce_fusion.2
  243.1 0.2 fusion.19
  243.3 0.2 fusion.18
  243.6 0.0 reduce-scatter.17.cloned.1.call-start
  243.6 0.3 multiply_reduce_fusion.4
  244.0 0.1 multiply_convert_fusion.2
  244.1 0.4 fusion.32
  244.6 48.7 %all_gather.19 = bf16[16,32,512]{2,1,0:T(8,128)(2,1)S(1)} all-gather(bf16[2,32,512]{2,1,0:T(8,128)(2,1)S(1)} %bitcast.97), channel_id=1, replica_groups=mesh['tm'=64,'section'=8] {'section'}, dimensions={0}, use_global_device_ids=true | all-gather | bytes 589824 | tf_op jit(solution)/shard_map/all_gather | solution.py:79
  293.2 0.3 convolution_bitcast_fusion
  293.6 1.0 copy.53
  294.6 0.3 multiply_reduce_fusion
  295.0 0.1 multiply_convert_fusion
  295.1 0.2 copy.38
  295.3 0.9 reshape.141
  296.2 11.2 all-to-all-start.1
  307.4 0.2 copy.39
  307.5 0.9 reshape.143
  308.4 7.3 all-to-all-done.1
  315.8 6.3 all-to-all-start.2
  322.1 0.2 reshape.142
  322.3 0.1 reshape.125
  322.5 2.0 convolution_convert_fusion.1
  324.5 0.2 convert_reduce_fusion.1
  324.7 1.0 copy.49
  325.7 0.0 reduce-scatter.15.cloned.1.call-start
  325.8 4.5 all-to-all-done.2
  330.3 0.2 reshape.144
  330.5 0.1 copy.48
  330.7 43.2 %all-gather.11.cloned.1.call-done = bf16[16,32,1024]{2,1,0:T(8,128)(2,1)} async-done(((bf16[2,32,1024]{2,1,0:T(8,128)(2,1)}), bf16[16,32,1024]{2,1,0:T(8,128)(2,1)}) %all-gather.11.cloned.1.call-update) | async-done | bytes 1048592 | tf_op jit(solution)/shard_map/all_gather | solution.py:44
  373.8 1.8 convolution_convert_fusion
  375.6 0.2 convert_reduce_fusion
  375.8 1.0 copy.51
  376.9 0.5 convolution_convert_fusion.3
  377.3 0.8 convert_element_type.52
  378.2 107.0 %all-reduce = (f32[3,512]{1,0:T(4,128)}, f32[3,512]{1,0:T(4,128)}) all-reduce(f32[3,512]{1,0:T(4,128)S(1)} %pad_maximum_fusion, f32[3,512]{1,0:T(4,128)S(1)} %pad_maximum_fusion.1), channel_id=1, replica_groups=mesh['tm'=64,'section'=8] {'tm','section'}, use_global_device_ids=true, to_apply=%region_21.0 | all-reduce | flops 3072 | bytes 24576 | tf_op jit(solution)/shard_map/psum | solution.py:121
  485.2 463.1 %reduce-scatter.17.cloned.1.call-done = f32[8,240]{1,0:T(8,128)} async-done(((f32[512,240]{1,0:T(8,128)}), f32[8,240]{1,0:T(8,128)}) %reduce-scatter.17.cloned.1.call-update) | async-done | bytes 7696 | tf_op jit(solution)/shard_map/transpose | solution.py:122
  948.3 561.8 %reduce-scatter.13.cloned.1.call-done = f32[16,64]{1,0:T(8,128)} async-done(((f32[1024,64]{1,0:T(8,128)}), f32[16,64]{1,0:T(8,128)}) %reduce-scatter.13.cloned.1.call-update) | async-done | bytes 4112 | tf_op jit(solution)/shard_map/transpose | solution.py:122
  1510.1 562.0 %reduce-scatter.15.cloned.1.call-done = f32[16,64]{1,0:T(8,128)} async-done(((f32[1024,64]{1,0:T(8,128)}), f32[16,64]{1,0:T(8,128)}) %reduce-scatter.15.cloned.1.call-update) | async-done | bytes 4112 | tf_op jit(solution)/shard_map/transpose | solution.py:122
  (40 shorter events, 0.4 us)
Async XLA Ops:
  8.0 34.0 %copy-start = (bf16[512,240]{0,1:T(8,128)(2,1)S(1)}, bf16[512,240]{0,1:T(8,128)(2,1)}, u32[]{:S(2)}) copy-start(bf16[512,240]{0,1:T(8,128)(2,1)} %param.12) | copy-start | bytes 737284
  8.0 90.8 %reduce-scatter.11.cloned.1.call-start = ((), (), s32[]{:S(2)}) async-start(), calls=%async_computation.9 | async-start | bytes 589824 | tf_op jit(solution)/shard_map/reduce_scatter | solution.py:86
  40.7 3.6 copy-start.3
  41.8 3.5 copy-start.5
  41.8 3.5 copy-start.6
  43.1 101.1 %all-gather.5.cloned.1.call-start = ((), (), s32[]{:S(2)}) async-start(), calls=%async_computation.7 | async-start | bytes 1064960 | tf_op jit(solution)/shard_map/all_gather | solution.py:58
  43.7 197.2 %all-gather.7.cloned.1.call-start = ((), (), s32[]{:S(2)}) async-start(), calls=%async_computation.8 | async-start | bytes 1064960 | tf_op jit(solution)/shard_map/all_gather | solution.py:59
  44.3 278.2 %all-gather.9.cloned.1.call-start = ((), (), s32[]{:S(2)}) async-start(), calls=%async_computation.10 | async-start | bytes 2359296 | tf_op jit(solution)/shard_map/all_gather | solution.py:44
  45.2 328.7 %all-gather.11.cloned.1.call-start = ((), (), s32[]{:S(2)}) async-start(), calls=%async_computation.11 | async-start | bytes 1179648 | tf_op jit(solution)/shard_map/all_gather | solution.py:44
  99.8 143.5 %copy-start.4 = (bf16[2,32,512]{2,1,0:T(8,128)(2,1)S(1)}, bf16[2,32,512]{2,1,0:T(8,128)(2,1)}, u32[]{:S(2)}) copy-start(bf16[2,32,512]{2,1,0:T(8,128)(2,1)} %reduce-scatter.11.cloned.1.call-done) | copy-start | bytes 196612
  241.0 3.1 copy-start.2
  243.6 704.7 %reduce-scatter.17.cloned.1.call-start = ((), (), s32[]{:S(2)}) async-start(), calls=%async_computation.14 | async-start | bytes 532480 | tf_op jit(solution)/shard_map/transpose | solution.py:122
  296.2 19.6 all-to-all-start.1
  315.8 14.5 all-to-all-start.2
  322.1 1188.0 %reduce-scatter.13.cloned.1.call-start = ((), (), s32[]{:S(2)}) async-start(), calls=%async_computation.12 | async-start | bytes 532480 | tf_op jit(solution)/shard_map/transpose | solution.py:122
  325.7 1746.4 %reduce-scatter.15.cloned.1.call-start = ((), (), s32[]{:S(2)}) async-start(), calls=%async_computation.13 | async-start | bytes 532480 | tf_op jit(solution)/shard_map/transpose | solution.py:122
  373.8 3.0 copy-start.1
Sparse Core Ops, SparseCore 0:
  43.2 55.5 reduce-scatter.10
Sparse Core Ops, SparseCore 1:
  48.0 96.3 all-gather.4
  148.5 92.4 all-gather.6
  243.7 62.7 all-gather.8
  308.7 65.0 all-gather.10
  377.4 570.8 reduce-scatter.16
  951.6 558.4 reduce-scatter.12
  1513.5 558.5 reduce-scatter.14
where the time goes:
time: 2080 us
  waiting for transfers between devices  1830 us (88%)
  blocking collectives  182 us (9%)
    transpose x3, waiting for transfers between devices, on_device(): return (grad_layer_five, wide_six.T, wide_seven.T, wide_proj.T, grad_gain...  1590 us
    psum x1, blocking collectives, on_device(): lax.psum((gain_terms, bias_terms), ('tm', 'section'))  107 us
    all_gather x1, waiting for transfers between devices, on_device(): lax.all_gather(conv_seven, 'tm', axis=0, tiled=True)  93.9 us
    reduce_scatter x1, waiting for transfers between devices, on_device(): lax.psum_scatter(rounded(product).astype(jnp.bfloat16), 'section', scatte...  53.4 us
    all_gather x1, blocking collectives, on_device(): lax.all_gather(normed, 'section', axis=0, tiled=True)  48.7 us
    all_gather x1, waiting for transfers between devices, on_device(): lax.all_gather(conv_six, 'tm', axis=0, tiled=True)  44.4 us
    all_gather x2, waiting for transfers between devices, weight_terms(): portion = lax.all_gather(own_inputs, 'section', axis=0, tiled=True)  43.2 us
  transfers between devices with their start and end apart: 10, of which 9 were waited for; matrix products, arithmetic and copies ran while one was open for 1% of the time, Pallas kernels for 0%

commit v1 on v0

v1 whole, which is shorter than its diff:
```python
import jax
import jax.numpy as jnp
from jax import lax
from jax.sharding import Mesh, PartitionSpec as P

norm_epsilon = 1e-05
half_root = 0.7071067811865476
inv_root_tau = 0.3989422804014327
narrow = jnp.bfloat16
wide = jnp.float32


def gelu_parts(preact):
    normal_cdf = 0.5 * (1.0 + lax.erf(preact * half_root))
    density = jnp.exp(-0.5 * preact * preact) * inv_root_tau
    return (preact * normal_cdf, normal_cdf + preact * density)


def norm_forward(hidden, gain_row, bias_row):
    average = jnp.mean(hidden, axis=-1, keepdims=True)
    centred = hidden - average
    inv_scale = lax.rsqrt(jnp.mean(centred * centred, axis=-1, keepdims=True) + norm_epsilon)
    normal_part = centred * inv_scale
    return (normal_part * gain_row + bias_row, normal_part, inv_scale)


def norm_backward(incoming, normal_part, inv_scale, gain_row):
    scaled = incoming * gain_row
    first_mean = jnp.mean(scaled, axis=-1, keepdims=True)
    second_mean = jnp.mean(scaled * normal_part, axis=-1, keepdims=True)
    return inv_scale * (scaled - first_mean - normal_part * second_mean)


def spread(block, axes):
    count = lax.axis_size(axes)
    copies = jnp.broadcast_to(block[None], (count,) + block.shape)
    return lax.all_to_all(copies, axes, 0, 0, tiled=True)


def swap(value, axis):
    return lax.ppermute(value, axis, [(0, 1), (1, 0)])


def on_device(layer_five, conv_six, conv_seven, gains, biases, proj_weight, feature_grad):
    utt_local, positions, channels = layer_five.shape
    features = proj_weight.shape[0]
    width = feature_grad.shape[2]
    part_width = proj_weight.shape[1]
    sections = lax.axis_size("s")
    planes = lax.axis_size(("y", "x"))
    place = lax.axis_index(("y", "x"))
    half = lax.axis_index("zh")
    core = lax.axis_index("c")
    rows_conv = conv_six.shape[0]
    runs = feature_grad.shape[1]

    own_rows = jnp.stack([conv_six, conv_seven])
    other_rows = swap(own_rows, "zh")
    pair = jnp.where(
        half == 0, jnp.stack([own_rows, other_rows]), jnp.stack([other_rows, own_rows])
    )

    slice_rows = features // (2 * planes)
    start = core * (features // 2) + place * slice_rows
    proj_slice = lax.dynamic_slice_in_dim(proj_weight, start, slice_rows, 0)
    proj_copies = jnp.broadcast_to(
        proj_slice.reshape(1, -1, width), (sections, slice_rows * part_width // width, width)
    )
    grads_out = feature_grad.reshape(sections, utt_local * runs, width)
    arrived = lax.all_to_all(
        jnp.concatenate([grads_out, proj_copies], axis=1), "s", 0, 0, tiled=True
    )
    grad_rows = (
        arrived[:, : utt_local * runs]
        .reshape(sections, utt_local, runs, width)
        .transpose(1, 0, 2, 3)
        .reshape(-1, width)
    )
    proj_rows = (
        arrived[:, utt_local * runs :]
        .reshape(sections, slice_rows, part_width)
        .transpose(1, 0, 2)
        .reshape(-1, channels)
    )

    conv_part = 2 * 2 * rows_conv
    bundle = jnp.concatenate([pair.reshape(conv_part, channels), proj_rows], axis=0)
    gathered = spread(bundle, ("y", "x"))
    sibling = swap(gathered, "c")
    both = jnp.where(
        core == 0, jnp.stack([gathered, sibling]), jnp.stack([sibling, gathered])
    )
    kernels = both[:, :, :conv_part].reshape(2, planes, 2, 2, rows_conv, channels)
    kernels = kernels.transpose(3, 1, 2, 0, 4, 5).reshape(2, -1, channels)
    kernel_six, kernel_seven = kernels[0], kernels[1]
    proj_full = both[:, :, conv_part:].reshape(features, width)

    unf_six = layer_five.reshape(-1, 2 * channels)
    hid_six = jnp.dot(unf_six, kernel_six, preferred_element_type=wide)
    pre_six, part_six, scale_six = norm_forward(hid_six, gains[0], biases[0])
    act_six_f, deriv_six = gelu_parts(pre_six)
    unf_seven = act_six_f.astype(narrow).reshape(-1, 2 * channels)
    hid_seven = jnp.dot(unf_seven, kernel_seven, preferred_element_type=wide)
    pre_seven, part_seven, scale_seven = norm_forward(hid_seven, gains[1], biases[1])
    act_seven_f, deriv_seven = gelu_parts(pre_seven)
    act_seven = act_seven_f.astype(narrow)
    pre_feat, part_feat, scale_feat = norm_forward(act_seven.astype(wide), gains[2], biases[2])
    normed = pre_feat.astype(narrow)

    grad_normed = lax.dot_general(
        grad_rows, proj_full, (((1,), (1,)), ((), ())), preferred_element_type=wide
    )
    dact_seven = norm_backward(grad_normed, part_feat, scale_feat, gains[2])
    dpre_seven = dact_seven * deriv_seven
    dhid_seven = norm_backward(dpre_seven, part_seven, scale_seven, gains[1]).astype(narrow)
    dact_six = lax.dot_general(
        dhid_seven, kernel_seven, (((1,), (1,)), ((), ())), preferred_element_type=wide
    ).reshape(-1, channels)
    dpre_six = dact_six * deriv_six
    dhid_six = norm_backward(dpre_six, part_six, scale_six, gains[0]).astype(narrow)
    grad_input = lax.dot_general(
        dhid_six, kernel_six, (((1,), (1,)), ((), ())), preferred_element_type=wide
    )
    grad_layer_five = grad_input.reshape(utt_local, positions, channels).astype(narrow)

    over_rows = (((0,), (0,)), ((), ()))
    term_six = lax.dot_general(unf_six, dhid_six, over_rows, preferred_element_type=wide)
    term_seven = lax.dot_general(unf_seven, dhid_seven, over_rows, preferred_element_type=wide)
    term_proj = lax.dot_general(normed, grad_rows, over_rows, preferred_element_type=wide)
    sums = jnp.stack(
        [
            jnp.sum(dpre_six * part_six, axis=0),
            jnp.sum(dpre_seven * part_seven, axis=0),
            jnp.sum(grad_normed * part_feat, axis=0),
            jnp.sum(dpre_six, axis=0),
            jnp.sum(dpre_seven, axis=0),
            jnp.sum(grad_normed, axis=0),
        ]
    )

    rows_proj = features // (4 * planes)
    terms = jnp.concatenate(
        [
            term_six.reshape(planes, 2, 2, -1, channels),
            term_seven.reshape(planes, 2, 2, -1, channels),
            term_proj.reshape(planes, 2, 2, -1, channels),
        ],
        axis=3,
    ).astype(narrow)
    kept = jnp.where(core == 0, terms[:, :, 0], terms[:, :, 1])
    given = jnp.where(core == 0, terms[:, :, 1], terms[:, :, 0])
    chip = kept.astype(wide) + swap(given, "c").astype(wide)

    count = chip.shape[2]
    sums_high = lax.reduce_precision(sums, 8, 7)
    sum_pair = jnp.concatenate([sums_high, sums - sums_high], axis=0).astype(narrow)
    sum_rows = sum_pair.shape[0]
    plane_send = jnp.concatenate(
        [
            chip.astype(narrow).reshape(planes, -1, channels),
            jnp.broadcast_to(sum_pair[None], (planes, sum_rows, channels)),
        ],
        axis=1,
    )
    plane_sum = jnp.sum(
        lax.all_to_all(plane_send, ("y", "x"), 0, 0, tiled=True).astype(wide), axis=0
    )

    parts = plane_sum[: 2 * count].reshape(2, count, channels)
    conv_rows = parts[:, : 2 * rows_conv].reshape(2, 2 * rows_conv, sections, -1)
    conv_rows = conv_rows.transpose(0, 2, 1, 3).reshape(2 * sections, -1)
    proj_part = parts[:, 2 * rows_conv :].reshape(2, rows_proj, sections, part_width)
    proj_part = proj_part.transpose(0, 2, 1, 3).reshape(2 * sections, -1)
    totals = plane_sum[2 * count :].reshape(2, -1, channels).sum(axis=0)
    totals_high = lax.reduce_precision(totals, 8, 7)
    total_pair = jnp.stack([totals_high, totals - totals_high]).reshape(1, -1)
    line_send = jnp.concatenate(
        [conv_rows, proj_part, jnp.broadcast_to(total_pair, (2 * sections, total_pair.shape[1]))],
        axis=1,
    ).astype(narrow)
    line_sum = jnp.sum(
        lax.all_to_all(line_send, ("zh", "s"), 0, 0, tiled=True).astype(wide), axis=0
    )
    conv_size, proj_size = conv_rows.shape[1], proj_part.shape[1]
    out_conv = line_sum[:conv_size].reshape(2, rows_conv, -1)
    out_proj = line_sum[conv_size : conv_size + proj_size].reshape(rows_proj, part_width)
    out_sums = line_sum[conv_size + proj_size :].reshape(2, 6, channels).sum(axis=0)
    out_sums = out_sums + swap(out_sums, "c")
    return (
        grad_layer_five,
        out_conv[0],
        out_conv[1],
        out_proj,
        out_sums[:3],
        out_sums[3:],
    )


def solution(mesh):
    fine = Mesh(mesh.devices.reshape(4, 4, 2, 2, 8), ("y", "x", "zh", "c", "s"))
    tm = ("y", "x", "zh", "c")
    return jax.shard_map(
        on_device,
        mesh=fine,
        in_specs=(
            P("s", tm, None),
            P(tm, None),
            P(tm, None),
            P(),
            P(),
            P(None, "s"),
            P(None, tm + ("s",), None),
        ),
        out_specs=(
            P("s", tm, None),
            P(tm, "s"),
            P(tm, "s"),
            P(tm, "s"),
            P(),
            P(),
        ),
        check_vma=False,
    )
```

time: 2080 us -> 210 us (0.10)
  the two profiles are of different devices: /device:TPU:64 before, /device:TPU:1 now
where the time goes in v1:
time: 210 us; the launch traced here: 209 us
  starting transfers between devices  60.6 us (29%)
  blocking collectives  57.7 us (27%)
  local copies, waits for them, and re-layouts  34.5 us (16%)
  waiting for transfers between devices  33.7 us (16%)
  other arithmetic  11.9 us (6%)
  matrix products  8.88 us (4%)
    ppermute x4, starting transfers between devices, swap(): return lax.ppermute(value, axis, [(0, 1), (1, 0)])  32.6 us
    all_to_all x1, blocking collectives, on_device(): lax.all_to_all(plane_send, ('y', 'x'), 0, 0, tiled=True).astype(wide)  32.1 us
    all_to_all x1, blocking collectives, spread(): return lax.all_to_all(copies, axes, 0, 0, tiled=True)  25.7 us
    ppermute x4, waiting for transfers between devices, swap(): return lax.ppermute(value, axis, [(0, 1), (1, 0)])  15 us
    all_to_all x1, starting transfers between devices, on_device(): lax.all_to_all(line_send, ('zh', 's'), 0, 0, tiled=True).astype(wide)  15 us
    all_to_all x1, starting transfers between devices, on_device(): lax.all_to_all(jnp.concatenate([grads_out, proj_copies], axis=1), 's', 0,...  13.1 us
    all_to_all x1, waiting for transfers between devices, on_device(): lax.all_to_all(line_send, ('zh', 's'), 0, 0, tiled=True).astype(wide)  13 us
    unnamed x30, local copies, waits for them, and re-layouts  6.11 us
  transfers between devices with their start and end apart: 6, of which 5 were waited for; matrix products, arithmetic and copies ran while one was open for 2% of the time, Pallas kernels for 0%

profile of v1, /device:TPU:1, one launch (start us, length us, event | category | flops | bytes accessed | tf_op | source)
XLA Modules:
  0.0 208.8 jit_solution(12713298046573974389)
XLA Ops:
  0.7 0.9 copy-done
  1.9 1.0 reshape.319
  2.9 0.8 pad_maximum_fusion.2
  3.7 13.1 %all-to-all-start = ((bf16[8,10,1920]{2,1,0:T(8,128)(2,1)}), bf16[8,10,1920]{2,1,0:T(8,128)(2,1)S(1)}, u32[]{:S(2)}, u32[]{:S(2)}) async-start(bf16[8,10,1920]{2,1,0:T(8,128)(2,1)} %pad_maximum_fusion.2), calls=%async_computation | async-start | bytes 983040 | tf_op jit(solution)/shard_map/all_to_all | solution.py:70
  16.9 7.9 %collective-permute-start = (bf16[2,16,512]{2,1,0:T(8,128)(2,1)S(1)}, bf16[2,16,512]{2,1,0:T(8,128)(2,1)S(1)}, u32[]{:S(2)}, u32[]{:S(2)}) collective-permute-start(bf16[2,16,512]{2,1,0:T(8,128)(2,1)S(1)} %get-tuple-element.27), channel_id=1, source_target_pairs={{0,16},{16,0},{1,17},{17,1},{2,18},{18,2},{3,19},{19,3},{4,20},{20... | collective-permute-start | bytes 98312 | tf_op jit(solution)/shard_map/ppermute | solution.py:41
  24.8 8.1 %collective-permute-done = bf16[2,16,512]{2,1,0:T(8,128)(2,1)S(1)} collective-permute-done((bf16[2,16,512]{2,1,0:T(8,128)(2,1)S(1)}, bf16[2,16,512]{2,1,0:T(8,128)(2,1)S(1)}, u32[]{:S(2)}, u32[]{:S(2)}) %collective-permute-start) | collective-permute-done | bytes 32800 | tf_op jit(solution)/shard_map/ppermute | solution.py:41
  32.9 5.7 %all-to-all-done = bf16[8,10,1920]{2,1,0:T(8,128)(2,1)S(1)} async-done(((bf16[8,10,1920]{2,1,0:T(8,128)(2,1)}), bf16[8,10,1920]{2,1,0:T(8,128)(2,1)S(1)}, u32[]{:S(2)}, u32[]{:S(2)}) %all-to-all-start) | async-done | bytes 307232 | tf_op jit(solution)/shard_map/all_to_all | solution.py:70
  38.8 0.2 reshape.321
  39.0 0.2 broadcast_in_dim.14
  39.2 25.7 %all_to_all.21 = bf16[16,124,512]{2,1,0:T(8,128)(2,1)S(1)} all-to-all(bf16[16,124,512]{2,1,0:T(8,128)(2,1)S(1)} %broadcast_in_dim.14), channel_id=1, replica_groups=mesh['y'=4,'x'=4,'zh'=2,'c'=2,'s'=8] {'y','x'}, dimensions={0} | all-to-all | bytes 4063232 | tf_op jit(solution)/shard_map/all_to_all | solution.py:37
  64.9 2.4 %copy.149 = bf16[16,124,512]{2,0,1:T(8,128)(2,1)} copy(bf16[16,124,512]{2,1,0:T(8,128)(2,1)S(1)} %all_to_all.21) | data formatting | bytes 4063232 | tf_op jit(solution)/shard_map/all_to_all | solution.py:37
  67.3 12.6 %collective-permute-start.1 = (bf16[16,124,512]{2,0,1:T(8,128)(2,1)}, bf16[16,124,512]{2,0,1:T(8,128)(2,1)}, u32[]{:S(2)}, u32[]{:S(2)}) collective-permute-start(bf16[16,124,512]{2,0,1:T(8,128)(2,1)} %copy.149), channel_id=1, source_target_pairs={{0,8},{8,0},{1,9},{9,1},{2,10},{10,2},{3,11},{11,3},{4,12},{12,4},... | collective-permute-start | bytes 6094856 | tf_op jit(solution)/shard_map/ppermute | solution.py:41
  80.3 3.4 %collective-permute-done.1 = bf16[16,124,512]{2,0,1:T(8,128)(2,1)} collective-permute-done((bf16[16,124,512]{2,0,1:T(8,128)(2,1)}, bf16[16,124,512]{2,0,1:T(8,128)(2,1)}, u32[]{:S(2)}, u32[]{:S(2)}) %collective-permute-start.1) | collective-permute-done | bytes 2031648 | tf_op jit(solution)/shard_map/ppermute | solution.py:41
  83.7 2.7 %copy.176 = bf16[16,124,512]{2,1,0:T(8,128)(2,1)S(1)} copy(bf16[16,124,512]{2,0,1:T(8,128)(2,1)} %collective-permute-done.1) | data formatting | bytes 4063232 | tf_op jit(solution)/shard_map/ppermute | solution.py:41
  86.4 0.7 maximum_select_fusion
  87.1 1.6 slice.139
  88.7 0.9 copy-done.2
  89.7 4.8 %reshape.327 = bf16[512,1920]{1,0:T(8,128)(2,1)} reshape(bf16[2,16,60,512]{3,2,1,0:T(8,128)(2,1)} %slice.139) | data formatting | bytes 3932160 | tf_op jit(solution)/shard_map/reshape | solution.py:96
  94.5 0.2 fusion.43
  94.9 0.5 fusion.48
  95.5 0.2 multiply_convert_fusion
  95.9 0.4 fusion.49
  96.3 0.2 multiply_reduce_fusion.4
  96.5 0.2 convert_reduce_fusion.2
  96.8 0.2 fusion.27
  97.0 2.4 %fusion.26 = (f32[512]{0:T(512)S(1)}, f32[64]{0:T(128)S(1)}, f32[64]{0:T(128)S(1)}, f32[512]{0:T(512)S(1)}, f32[64,512]{1,0:T(8,128)S(1)}) fusion(bf16[64,512]{1,0:T(8,128)(2,1)S(1)} %get-tuple-element.21, f32[64]{0:T(128)S(1)} %add_rsqrt_fusion, f32[64]{0:T(128)S(1)} %broadcast_multiply_fusion.4, f32[512]{0:T(512)S(1)} %bitcast.124, ...), kind=kOutput, calls=%fused_computation.54 | convolution fusion | flops 126155648 | bytes 2415616 | tf_op jit(solution)/shard_map/dot_general | solution.py:110
  99.4 0.3 multiply_reduce_fusion.2
  99.7 1.2 fusion.40
  100.9 1.0 reshape.328
  102.0 0.4 fusion.12
  102.4 0.2 copy.158
  102.6 1.5 convolution_convert_fusion.2
  104.3 0.6 copy-done.7
  104.9 0.4 fusion.1
  105.3 0.5 copy.157
  105.9 1.6 copy.160
  107.5 2.1 convolution_convert_fusion
  109.5 3.7 %reshape.330 = bf16[16,2,2,30,512]{4,3,2,1,0:T(8,128)(2,1)S(1)} reshape(bf16[512,1920]{1,0:T(8,128)(2,1)} %convolution_convert_fusion) | data formatting | bytes 3932160 | tf_op jit(solution)/shard_map/reshape | solution.py:146
  113.3 1.1 copy.161
  114.5 0.3 copy-done.4
  114.8 0.4 pad_maximum_fusion
  115.2 0.2 select_bitcast_fusion
  115.5 1.7 copy-done.1
  117.1 2.5 %collective-permute-start.2 = (bf16[16,2,62,512]{3,0,2,1:T(8,128)(2,1)S(1)}, bf16[16,2,62,512]{3,0,2,1:T(8,128)(2,1)}, u32[]{:S(2)}, u32[]{:S(2)}) collective-permute-start(bf16[16,2,62,512]{3,0,2,1:T(8,128)(2,1)S(1)} %select_bitcast_fusion), channel_id=1, source_target_pairs={{0,8},{8,0},{1,9},{9,1},{2,10},{10,2},{3,11},{11,3},{4,12},{12,4},... | collective-permute-start | bytes 6094856 | tf_op jit(solution)/shard_map/ppermute | solution.py:41
  119.7 3.5 %collective-permute-done.2 = bf16[16,2,62,512]{3,0,2,1:T(8,128)(2,1)} collective-permute-done((bf16[16,2,62,512]{3,0,2,1:T(8,128)(2,1)S(1)}, bf16[16,2,62,512]{3,0,2,1:T(8,128)(2,1)}, u32[]{:S(2)}, u32[]{:S(2)}) %collective-permute-start.2) | collective-permute-done | bytes 2031648 | tf_op jit(solution)/shard_map/ppermute | solution.py:41
  123.2 4.2 %fusion = bf16[16,2,62,512]{3,0,2,1:T(8,128)(2,1)S(1)} fusion(bf16[16,2,62,512]{3,0,2,1:T(8,128)(2,1)} %collective-permute-done.2, pred[]{:T(512)S(6)} %eq.8, bf16[16,2,2,62,512]{4,0,3,1,2:T(8,128)(2,1)} %copy-done.1), kind=kLoop, calls=%fused_computation.4 | loop fusion | flops 5079040 | bytes 8126465 | tf_op jit(solution)/shard_map/convert_element_type | solution.py:160
  127.4 0.2 pad_maximum_fusion.1
  127.6 1.2 copy.162
  128.9 32.1 %all_to_all.22 = bf16[16,136,512]{2,1,0:T(8,128)(2,1)S(1)} all-to-all(bf16[16,136,512]{2,1,0:T(8,128)(2,1)S(1)} %copy.162), channel_id=1, replica_groups=mesh['y'=4,'x'=4,'zh'=2,'c'=2,'s'=8] {'y','x'}, dimensions={0} | all-to-all | bytes 4456448 | tf_op jit(solution)/shard_map/all_to_all | solution.py:166
  160.9 0.3 convert_reduce_fusion
  162.1 0.5 maximum_maximum_fusion
  162.6 0.5 broadcast.140
  163.1 2.5 %reduce.3 = bf16[16,10112]{1,0:T(8,128)(2,1)S(1)} reduce(bf16[16,1,10112]{2,1,0:T(2,128)(2,1)S(1)} %maximum_maximum_fusion, bf16[]{:T(256)} %broadcast.140), dimensions={1}, to_apply=%maximum_maximum_fusion.reduce_sub_computation | reduce | bytes 647170 | tf_op jit(solution)/shard_map/concatenate | solution.py:177
  165.7 1.0 reshape.343
  166.7 15.0 %all-to-all-start.3 = ((bf16[16,2,5056]{2,1,0:T(2,128)(2,1)}), bf16[16,2,5056]{2,1,0:T(2,128)(2,1)S(1)}, u32[]{:S(2)}, u32[]{:S(2)}) async-start(bf16[16,2,5056]{2,1,0:T(2,128)(2,1)} %reshape.343), calls=%async_computation.3 | async-start | bytes 655360 | tf_op jit(solution)/shard_map/all_to_all | solution.py:182
  181.7 0.5 convolution_convert_fusion.3
  182.2 0.8 convert_element_type.63
  183.0 13.0 %all-to-all-done.3 = bf16[16,2,5056]{2,1,0:T(2,128)(2,1)S(1)} async-done(((bf16[16,2,5056]{2,1,0:T(2,128)(2,1)}), bf16[16,2,5056]{2,1,0:T(2,128)(2,1)S(1)}, u32[]{:S(2)}, u32[]{:S(2)}) %all-to-all-start.3) | async-done | bytes 323616 | tf_op jit(solution)/shard_map/all_to_all | solution.py:182
  195.9 0.4 reshape.344
  196.5 9.6 %collective-permute-start.3 = (f32[6,512]{1,0:T(8,128)S(1)}, f32[6,512]{1,0:T(8,128)S(1)}, u32[]{:S(2)}, u32[]{:S(2)}) collective-permute-start(f32[6,512]{1,0:T(8,128)S(1)} %reduce_sum.222), channel_id=1, source_target_pairs={{0,8},{8,0},{1,9},{9,1},{2,10},{10,2},{3,11},{11,3},{4,12},{12,4},... | collective-permute-start | bytes 36872 | tf_op jit(solution)/shard_map/ppermute | solution.py:41
  206.2 0.7 reshape.336
  206.9 0.7 slice.129
  207.5 0.7 slice.127
  208.2 0.6 fusion.45
  (89 shorter events, 2.7 us)
Async XLA Ops:
  0.6 1.0 copy-start
  0.6 16.2 %copy-start.10 = (bf16[16,512]{1,0:T(8,128)(2,1)S(1)}, bf16[16,512]{1,0:T(8,128)(2,1)}, u32[]{:S(2)}) copy-start(bf16[16,512]{1,0:T(8,128)(2,1)} %param.9) | copy-start | bytes 49156
  0.7 16.2 %copy-start.11 = (bf16[16,512]{1,0:T(8,128)(2,1)S(1)}, bf16[16,512]{1,0:T(8,128)(2,1)}, u32[]{:S(2)}) copy-start(bf16[16,512]{1,0:T(8,128)(2,1)} %param.8) | copy-start | bytes 49156
  3.7 34.9 %all-to-all-start = ((bf16[8,10,1920]{2,1,0:T(8,128)(2,1)}), bf16[8,10,1920]{2,1,0:T(8,128)(2,1)S(1)}, u32[]{:S(2)}, u32[]{:S(2)}) async-start(bf16[8,10,1920]{2,1,0:T(8,128)(2,1)} %pad_maximum_fusion.2), calls=%async_computation | async-start | bytes 983040 | tf_op jit(solution)/shard_map/all_to_all | solution.py:70
  16.9 16.0 %collective-permute-start = (bf16[2,16,512]{2,1,0:T(8,128)(2,1)S(1)}, bf16[2,16,512]{2,1,0:T(8,128)(2,1)S(1)}, u32[]{:S(2)}, u32[]{:S(2)}) collective-permute-start(bf16[2,16,512]{2,1,0:T(8,128)(2,1)S(1)} %get-tuple-element.27), channel_id=1, source_target_pairs={{0,16},{16,0},{1,17},{17,1},{2,18},{18,2},{3,19},{19,3},{4,20},{20... | collective-permute-start | bytes 98312 | tf_op jit(solution)/shard_map/ppermute | solution.py:41
  64.9 15.0 %copy-start.9 = (bf16[2,128,512]{2,1,0:T(8,128)(2,1)S(1)}, bf16[2,128,512]{2,1,0:T(8,128)(2,1)}, u32[]{:S(2)}) copy-start(bf16[2,128,512]{2,1,0:T(8,128)(2,1)} %param.7) | copy-start | bytes 786436
  64.9 15.1 %copy-start.12 = (f32[3,512]{1,0:T(4,128)S(1)}, f32[3,512]{1,0:T(4,128)}, u32[]{:S(2)}) copy-start(f32[3,512]{1,0:T(4,128)} %param.10) | copy-start | bytes 18436
  64.9 15.1 %copy-start.13 = (f32[3,512]{1,0:T(4,128)S(1)}, f32[3,512]{1,0:T(4,128)}, u32[]{:S(2)}) copy-start(f32[3,512]{1,0:T(4,128)} %param.11) | copy-start | bytes 18436
  67.3 16.4 %collective-permute-start.1 = (bf16[16,124,512]{2,0,1:T(8,128)(2,1)}, bf16[16,124,512]{2,0,1:T(8,128)(2,1)}, u32[]{:S(2)}, u32[]{:S(2)}) collective-permute-start(bf16[16,124,512]{2,0,1:T(8,128)(2,1)} %copy.149), channel_id=1, source_target_pairs={{0,8},{8,0},{1,9},{9,1},{2,10},{10,2},{3,11},{11,3},{4,12},{12,4},... | collective-permute-start | bytes 6094856 | tf_op jit(solution)/shard_map/ppermute | solution.py:41
  80.3 16.7 %copy-start.5 = (bf16[64,1920]{1,0:T(8,128)(2,1)}, bf16[64,1920]{1,0:T(8,128)(2,1)S(1)}, u32[]{:S(2)}) copy-start(bf16[64,1920]{1,0:T(8,128)(2,1)S(1)} %reshape.326) | copy-start | bytes 737284
  87.1 2.6 %copy-start.2 = (bf16[2,16,124,512]{3,2,1,0:T(8,128)(2,1)}, bf16[2,16,124,512]{3,2,1,0:T(8,128)(2,1)S(1)}, u32[]{:S(2)}) copy-start(bf16[2,16,124,512]{3,2,1,0:T(8,128)(2,1)S(1)} %maximum_select_fusion) | copy-start | bytes 12189700
  89.7 4.8 %slice-start = ((bf16[2,16,124,512]{3,2,1,0:T(8,128)(2,1)}), bf16[2,16,64,512]{3,2,1,0:T(8,128)(2,1)S(1)}, s32[]{:S(2)}) async-start(bf16[2,16,124,512]{3,2,1,0:T(8,128)(2,1)} %copy-done.2), calls=%async_computation.4 | async-start | bytes 4194304 | tf_op jit(solution)/shard_map/slice | solution.py:93
  104.3 0.7 copy-start.7
  105.9 1.6 copy-start.6
  113.3 1.2 copy-start.3
  113.3 1.5 copy-start.4
  115.2 1.9 copy-start.1
  117.1 6.1 %collective-permute-start.2 = (bf16[16,2,62,512]{3,0,2,1:T(8,128)(2,1)S(1)}, bf16[16,2,62,512]{3,0,2,1:T(8,128)(2,1)}, u32[]{:S(2)}, u32[]{:S(2)}) collective-permute-start(bf16[16,2,62,512]{3,0,2,1:T(8,128)(2,1)S(1)} %select_bitcast_fusion), channel_id=1, source_target_pairs={{0,8},{8,0},{1,9},{9,1},{2,10},{10,2},{3,11},{11,3},{4,12},{12,4},... | collective-permute-start | bytes 6094856 | tf_op jit(solution)/shard_map/ppermute | solution.py:41
  161.7 20.0 %copy-start.8 = (bf16[128,512]{0,1:T(8,128)(2,1)S(1)}, bf16[128,512]{0,1:T(8,128)(2,1)}, u32[]{:S(2)}) copy-start(bf16[128,512]{0,1:T(8,128)(2,1)} %copy-done.7) | copy-start | bytes 393220
  166.7 29.2 %all-to-all-start.3 = ((bf16[16,2,5056]{2,1,0:T(2,128)(2,1)}), bf16[16,2,5056]{2,1,0:T(2,128)(2,1)S(1)}, u32[]{:S(2)}, u32[]{:S(2)}) async-start(bf16[16,2,5056]{2,1,0:T(2,128)(2,1)} %reshape.343), calls=%async_computation.3 | async-start | bytes 655360 | tf_op jit(solution)/shard_map/all_to_all | solution.py:182
  196.5 11.7 %collective-permute-start.3 = (f32[6,512]{1,0:T(8,128)S(1)}, f32[6,512]{1,0:T(8,128)S(1)}, u32[]{:S(2)}, u32[]{:S(2)}) collective-permute-start(f32[6,512]{1,0:T(8,128)S(1)} %reduce_sum.222), channel_id=1, source_target_pairs={{0,8},{8,0},{1,9},{9,1},{2,10},{10,2},{3,11},{11,3},{4,12},{12,4},... | collective-permute-start | bytes 36872 | tf_op jit(solution)/shard_map/ppermute | solution.py:41

commit v2 on v0

v2 whole, which is shorter than its diff:
```python
import jax
import jax.numpy as jnp
from jax import lax
from jax.experimental import pallas as pl
from jax.experimental.pallas import tpu as pltpu
from jax.sharding import Mesh, PartitionSpec as P

norm_epsilon = 1e-05
half_root = 0.7071067811865476
inv_root_tau = 0.3989422804014327
narrow = jnp.bfloat16
wide = jnp.float32
LANES = 128
TILE = 16
VMEM_BYTES = 56 * 1024 * 1024


def gelu_parts(preact):
    normal_cdf = 0.5 * (1.0 + lax.erf(preact * half_root))
    density = jnp.exp(-0.5 * preact * preact) * inv_root_tau
    return (preact * normal_cdf, normal_cdf + preact * density)


def norm_forward(hidden, gain_row, bias_row):
    average = jnp.mean(hidden, axis=-1, keepdims=True)
    centred = hidden - average
    inv_scale = lax.rsqrt(jnp.mean(centred * centred, axis=-1, keepdims=True) + norm_epsilon)
    normal_part = centred * inv_scale
    return (normal_part * gain_row + bias_row, normal_part, inv_scale)


def norm_backward(incoming, normal_part, inv_scale, gain_row):
    scaled = incoming * gain_row
    first_mean = jnp.mean(scaled, axis=-1, keepdims=True)
    second_mean = jnp.mean(scaled * normal_part, axis=-1, keepdims=True)
    return inv_scale * (scaled - first_mean - normal_part * second_mean)


def matmul(left, right, over=(1, 0)):
    return lax.dot_general(
        left, right, (((over[0],), (over[1],)), ((), ())), preferred_element_type=wide
    )


def one_hot(shape, column_of_row):
    rows = lax.broadcasted_iota(jnp.int32, shape, 0)
    columns = lax.broadcasted_iota(jnp.int32, shape, 1)
    return jnp.where(columns == column_of_row(rows), 1.0, 0.0).astype(narrow)


def exchange(value, axes):
    return lax.all_to_all(value, axes, 0, 0, tiled=True)


def swap(value, axis):
    return lax.ppermute(value, axis, [(0, 1), (1, 0)])


def on_core(kernel, out_shape, scalars, arrays, scratch=(), flops=0, moved=0):
    multiple = isinstance(out_shape, (list, tuple))
    vmem = pl.BlockSpec(memory_space=pltpu.VMEM)
    return pl.pallas_call(
        kernel,
        out_shape=out_shape,
        in_specs=[pl.BlockSpec(memory_space=pltpu.SMEM)] * len(scalars) + [vmem] * len(arrays),
        out_specs=[vmem] * len(out_shape) if multiple else vmem,
        scratch_shapes=list(scratch),
        compiler_params=pltpu.CompilerParams(vmem_limit_bytes=VMEM_BYTES),
        cost_estimate=pl.CostEstimate(flops=flops, bytes_accessed=moved, transcendentals=0),
    )(*scalars, *arrays)


def pick_kernel(place_ref, six_ref, seven_ref, proj_ref, out_ref):
    plane, half, core, section = (place_ref[k] for k in range(4))
    lanes_conv = pl.ds(pl.multiple_of(lax.rem(section, 4) * LANES, LANES), LANES)
    first = section < 4
    conv = jnp.where(first, six_ref[:, lanes_conv].astype(wide), seven_ref[:, lanes_conv].astype(wide))
    row_tiles = proj_ref.shape[0] // TILE
    row = pl.multiple_of(jnp.minimum(plane, row_tiles - 1) * TILE, TILE)
    lane = pl.multiple_of((half * 2 + core) * LANES, LANES)
    block = jnp.concatenate(
        [conv.astype(narrow), proj_ref[pl.ds(row, TILE), pl.ds(lane, LANES)]], axis=0
    )
    out_ref[...] = jnp.broadcast_to(block[None], out_ref.shape)


def layer_kernel(
    place_ref,
    input_ref,
    own_ref,
    other_ref,
    grad_ref,
    gains_ref,
    biases_ref,
    back_ref,
    kept_ref,
    given_ref,
    six_ref,
    seven_ref,
    proj_ref,
    term_six_ref,
    term_seven_ref,
    term_proj_ref,
):
    core = place_ref[2]
    channels = input_ref.shape[1]
    frames = grad_ref.shape[0]
    lane_tiles = channels // LANES
    planes = own_ref.shape[0]
    sections = own_ref.shape[1] // 2
    width = grad_ref.shape[1]
    section_rows = width // sections
    row_tiles = section_rows // TILE

    def place_tiles(plane, carry):
        for half in range(2):
            for source, index in ((own_ref, core), (other_ref, 1 - core)):
                rows = pl.ds(
                    pl.multiple_of(((plane * 2 + half) * 2 + index) * TILE, TILE), TILE
                )
                for lane in range(lane_tiles):
                    lanes = slice(lane * LANES, (lane + 1) * LANES)
                    six_ref[rows, lanes] = source[plane, half * sections + lane, :TILE]
                    seven_ref[rows, lanes] = source[
                        plane, half * sections + lane_tiles + lane, :TILE
                    ]
        return carry

    lax.fori_loop(0, planes, place_tiles, 0)

    def place_proj(plane, carry):
        for half in range(2):
            for source, index in ((own_ref, core), (other_ref, 1 - core)):
                lanes = pl.ds(pl.multiple_of((half * 2 + index) * LANES, LANES), LANES)
                for section in range(sections):
                    rows = pl.ds(
                        pl.multiple_of(section * section_rows + plane * TILE, TILE), TILE
                    )
                    proj_ref[rows, lanes] = source[plane, half * sections + section, TILE:]
        return carry

    lax.fori_loop(0, row_tiles, place_proj, 0)

    count = 4 * frames

    def source_row(rows):
        run = rows // frames
        return 4 * (rows % frames) + (run % 2) * 2 + run // 2

    order = one_hot((count, count), source_row)
    positions = matmul(order, input_ref[...]).astype(narrow)
    tap_zero, tap_one = positions[: 2 * frames], positions[2 * frames :]
    hid_six = matmul(tap_zero, six_ref[:channels]) + matmul(tap_one, six_ref[channels:])
    pre_six, part_six, scale_six = norm_forward(hid_six, gains_ref[0:1], biases_ref[0:1])
    act_six_f, deriv_six = gelu_parts(pre_six)
    act_six = act_six_f.astype(narrow)
    act_zero, act_one = act_six[:frames], act_six[frames:]
    hid_seven = matmul(act_zero, seven_ref[:channels]) + matmul(act_one, seven_ref[channels:])
    pre_seven, part_seven, scale_seven = norm_forward(
        hid_seven, gains_ref[1:2], biases_ref[1:2]
    )
    act_seven_f, deriv_seven = gelu_parts(pre_seven)
    pre_feat, part_feat, scale_feat = norm_forward(
        act_seven_f.astype(narrow).astype(wide), gains_ref[2:3], biases_ref[2:3]
    )
    normed = pre_feat.astype(narrow)

    run = frames // (2 * sections)

    def arrived_row(rows):
        utterance = rows // (sections * run)
        rest = rows % (sections * run)
        return (rest // run) * (2 * run) + utterance * run + rest % run

    grad_rows = matmul(one_hot((frames, frames), arrived_row), grad_ref[...]).astype(narrow)
    term_proj_ref[...] = matmul(normed, grad_rows, (0, 0))

    grad_normed = matmul(grad_rows, proj_ref[...])
    dact_seven = norm_backward(grad_normed, part_feat, scale_feat, gains_ref[2:3])
    dpre_seven = dact_seven * deriv_seven
    dhid_seven = norm_backward(dpre_seven, part_seven, scale_seven, gains_ref[1:2]).astype(narrow)
    term_seven_ref[:channels] = matmul(act_zero, dhid_seven, (0, 0))
    term_seven_ref[channels:] = matmul(act_one, dhid_seven, (0, 0))
    dact_six = jnp.concatenate(
        [
            matmul(dhid_seven, seven_ref[:channels], (1, 1)),
            matmul(dhid_seven, seven_ref[channels:], (1, 1)),
        ],
        axis=0,
    )
    dpre_six = dact_six * deriv_six
    dhid_six = norm_backward(dpre_six, part_six, scale_six, gains_ref[0:1]).astype(narrow)
    term_six_ref[:channels] = matmul(tap_zero, dhid_six, (0, 0))
    term_six_ref[channels:] = matmul(tap_one, dhid_six, (0, 0))
    back = jnp.concatenate(
        [
            matmul(dhid_six, six_ref[:channels], (1, 1)).astype(narrow),
            matmul(dhid_six, six_ref[channels:], (1, 1)).astype(narrow),
        ],
        axis=0,
    )
    back_ref[...] = matmul(order, back, (0, 0)).astype(narrow)

    half_rows = TILE // 2

    def pack(plane, carry):
        for target, index in ((kept_ref, core), (given_ref, 1 - core)):
            proj_rows = []
            for half in range(2):
                group = (plane * 2 + half) * 2 + index
                rows = pl.ds(pl.multiple_of(group * TILE, TILE), TILE)
                for lane in range(lane_tiles):
                    lanes = slice(lane * LANES, (lane + 1) * LANES)
                    at = (half * lane_tiles + lane) * TILE
                    target[plane, at : at + TILE] = term_six_ref[rows, lanes].astype(narrow)
                    at += 2 * lane_tiles * TILE
                    target[plane, at : at + TILE] = term_seven_ref[rows, lanes].astype(narrow)
                proj_rows.append(
                    term_proj_ref[pl.ds(pl.multiple_of(group * half_rows, half_rows), half_rows)]
                )
            proj_block = jnp.concatenate(proj_rows, axis=0).astype(narrow)
            for lane in range(width // LANES):
                at = (4 * lane_tiles + lane) * TILE
                target[plane, at : at + TILE] = proj_block[:, lane * LANES : (lane + 1) * LANES]
        return carry

    lax.fori_loop(0, planes, pack, 0)

    def total(value):
        return jnp.sum(value, axis=0, keepdims=True)

    sums = jnp.concatenate(
        [
            total(dpre_six * part_six),
            total(dpre_seven * part_seven),
            total(grad_normed * part_feat),
            total(dpre_six),
            total(dpre_seven),
            total(grad_normed),
            jnp.zeros((2, channels), wide),
        ],
        axis=0,
    )
    sums = jnp.concatenate(
        [sums[:, lane * LANES : (lane + 1) * LANES] for lane in range(lane_tiles)], axis=0
    ).astype(narrow)
    at = (4 * lane_tiles + width // LANES) * TILE
    spread_sums = jnp.broadcast_to(sums[None], (planes,) + sums.shape)
    kept_ref[:, at:] = spread_sums
    given_ref[:, at:] = spread_sums


def add_kernel(left_ref, right_ref, out_ref):
    for plane in range(out_ref.shape[0]):
        out_ref[plane] = (left_ref[plane].astype(wide) + right_ref[plane].astype(wide)).astype(
            narrow
        )


def plane_kernel(arrived_ref, out_ref, total_ref):
    planes, rows = arrived_ref.shape[0], arrived_ref.shape[1]
    running = arrived_ref[0].astype(wide)
    for plane in range(1, planes):
        running += arrived_ref[plane].astype(wide)
    total_ref[...] = running
    sections = out_ref.shape[0] // 2
    lane_tiles = sections // 2
    proj_tiles = rows // TILE - 4 * lane_tiles - 2
    left = lax.broadcasted_iota(jnp.int32, (TILE, LANES), 1) < LANES // 2
    for half in range(2):
        for lane in range(lane_tiles):
            at = (half * lane_tiles + lane) * TILE
            six = total_ref[at : at + TILE]
            at += 2 * lane_tiles * TILE
            seven = total_ref[at : at + TILE]
            place = half * sections + 2 * lane
            out_ref[place, :TILE] = jnp.where(
                left, six, pltpu.roll(seven, LANES // 2, 1)
            ).astype(narrow)
            out_ref[place + 1, :TILE] = jnp.where(
                left, pltpu.roll(six, LANES // 2, 1), seven
            ).astype(narrow)
    base = 4 * lane_tiles * TILE
    proj = jnp.concatenate(
        [total_ref[base + lane * TILE : base + (lane + 1) * TILE] for lane in range(proj_tiles)],
        axis=1,
    )
    width = proj.shape[1]
    part = width // sections
    for section in range(sections):
        shift = (width - section * part) % width
        moved = pltpu.roll(proj, shift, 1) if shift else proj
        for half in range(2):
            rows_of = slice(half * (TILE // 2), (half + 1) * (TILE // 2))
            out_ref[half * sections + section, TILE : 2 * TILE] = jnp.concatenate(
                [moved[rows_of, :LANES], moved[rows_of, LANES : 2 * LANES]], axis=0
            ).astype(narrow)
    sums = total_ref[rows - 2 * TILE :].astype(narrow)
    out_ref[:, 2 * TILE :] = jnp.broadcast_to(sums[None], (2 * sections,) + sums.shape)


def line_kernel(arrived_ref, six_ref, seven_ref, proj_ref, gains_ref, biases_ref):
    running = arrived_ref[0].astype(wide)
    for source in range(1, arrived_ref.shape[0]):
        running += arrived_ref[source].astype(wide)
    half = LANES // 2
    six_ref[...] = running[:TILE, :half]
    seven_ref[...] = running[:TILE, half:]
    rows = TILE // 2
    proj = jnp.concatenate(
        [running[TILE : TILE + rows], running[TILE + rows : 2 * TILE]], axis=1
    )
    proj_ref[...] = proj[:, : proj_ref.shape[1]]
    sums = jnp.concatenate(
        [running[2 * TILE + k * rows : 2 * TILE + (k + 1) * rows] for k in range(4)], axis=1
    )
    gains_ref[...] = sums[:3]
    biases_ref[...] = sums[3:6]


def on_device(layer_five, conv_six, conv_seven, gains, biases, proj_weight, feature_grad):
    utt_local, positions, channels = layer_five.shape
    width = feature_grad.shape[2]
    part_width = proj_weight.shape[1]
    sections = lax.axis_size("s")
    planes = lax.axis_size(("y", "x"))
    frames = utt_local * positions // 4
    shape = jax.ShapeDtypeStruct
    place = jnp.stack(
        [lax.axis_index(("y", "x")), lax.axis_index("zh"), lax.axis_index("c"), lax.axis_index("s")]
    ).astype(jnp.int32)

    picked = on_core(
        pick_kernel,
        shape((2 * sections, 2 * TILE, LANES), narrow),
        [place],
        [conv_six, conv_seven, proj_weight.T],
    )
    line = exchange(picked, ("zh", "s"))
    bundle = line.reshape(1, 2 * sections * 2 * TILE, LANES)
    gathered = exchange(jnp.broadcast_to(bundle, (planes,) + bundle.shape[1:]), ("y", "x"))
    gathered_flat = gathered.reshape(-1, LANES)
    sibling = swap(gathered_flat, "c")

    grads = exchange(feature_grad.reshape(sections, -1, width), "s").reshape(frames, width)

    tiles_shape = (planes, 2 * sections, 2 * TILE, LANES)
    send_rows = (4 * (channels // LANES) + width // LANES + 2) * TILE
    back, kept, given = on_core(
        layer_kernel,
        [
            shape((4 * frames, channels), narrow),
            shape((planes, send_rows, LANES), narrow),
            shape((planes, send_rows, LANES), narrow),
        ],
        [place],
        [
            layer_five.reshape(4 * frames, channels),
            gathered.reshape(tiles_shape),
            sibling.reshape(tiles_shape),
            grads,
            gains,
            biases,
        ],
        scratch=[
            pltpu.VMEM((2 * channels, channels), narrow),
            pltpu.VMEM((2 * channels, channels), narrow),
            pltpu.VMEM((width, channels), narrow),
            pltpu.VMEM((2 * channels, channels), wide),
            pltpu.VMEM((2 * channels, channels), wide),
            pltpu.VMEM((channels, width), wide),
        ],
    )
    received = swap(given.reshape(-1, LANES), "c").reshape(given.shape)
    chip = on_core(add_kernel, shape(kept.shape, narrow), [], [kept, received])
    plane_in = exchange(chip, ("y", "x"))
    line_out = on_core(
        plane_kernel,
        shape((2 * sections, 4 * TILE, LANES), narrow),
        [],
        [plane_in],
        scratch=[pltpu.VMEM((send_rows, LANES), wide)],
    )
    line_in = exchange(line_out, ("zh", "s"))
    out_six, out_seven, out_proj, out_gains, out_biases = on_core(
        line_kernel,
        [
            shape((TILE, channels // sections), wide),
            shape((TILE, channels // sections), wide),
            shape((TILE // 2, part_width), wide),
            shape((3, channels), wide),
            shape((3, channels), wide),
        ],
        [],
        [line_in],
    )
    return (
        back.reshape(utt_local, positions, channels),
        out_six,
        out_seven,
        out_proj,
        out_gains,
        out_biases,
    )


def solution(mesh):
    fine = Mesh(mesh.devices.reshape(4, 4, 2, 2, 8), ("y", "x", "zh", "c", "s"))
    tm = ("y", "x", "zh", "c")
    return jax.shard_map(
        on_device,
        mesh=fine,
        in_specs=(
            P("s", tm, None),
            P(tm, None),
            P(tm, None),
            P(),
            P(),
            P(None, "s"),
            P(None, tm + ("s",), None),
        ),
        out_specs=(
            P("s", tm, None),
            P(tm, "s"),
            P(tm, "s"),
            P(tm, "s"),
            P(),
            P(),
        ),
        check_vma=False,
    )
```

time: 2080 us -> 176 us (0.08)
  waiting for transfers between devices: 1830 us -> 4.43 us
  blocking collectives: 182 us -> 144 us
    transpose x3 -> x0, waiting for transfers between devices: 1590 us -> none  [on_device(): return (grad_layer_five, wide_six.T, wide_seven.T, wide_proj.T, grad_gain...]
    all_gather x4 -> x0, waiting for transfers between devices: 182 us -> none  [the longest x1 93.9 us: on_device(): lax.all_gather(conv_seven, 'tm', axis=0, tiled=True)]
    all_to_all x1 -> x5, blocking collectives: 26.4 us -> 144 us  [exchange(): return lax.all_to_all(value, axes, 0, 0, tiled=True)]
    psum x1 -> x0, blocking collectives: 107 us -> none  [on_device(): lax.psum((gain_terms, bias_terms), ('tm', 'section'))]
    reduce_scatter x1 -> x0, waiting for transfers between devices: 53.4 us -> none  [on_device(): lax.psum_scatter(rounded(product).astype(jnp.bfloat16), 'section', scatte...]
    all_gather x1 -> x0, blocking collectives: 48.7 us -> none  [on_device(): lax.all_gather(normed, 'section', axis=0, tiled=True)]
  transfers between devices with their start and end apart: 10 -> 2, of which waited for: 9 -> 1; matrix products, arithmetic and copies ran while one was open for 1% -> 0% of each run, Pallas kernels for 0% -> 0%
where the time goes in v2:
time: 176 us
  blocking collectives  144 us (82%)
  Pallas kernels  20.4 us (12%)
  waiting for transfers between devices  4.43 us (3%)
  starting transfers between devices  3.82 us (2%)
  local copies, waits for them, and re-layouts  1.85 us (1%)
    all_to_all x5, blocking collectives, exchange(): return lax.all_to_all(value, axes, 0, 0, tiled=True)  144 us
    pallas_call x5, Pallas kernels, on_core(): pl.pallas_call(kernel, out_shape=out_shape, in_specs=[pl.BlockSpec(memory...  20.4 us
    ppermute x2, waiting for transfers between devices, swap(): return lax.ppermute(value, axis, [(0, 1), (1, 0)])  4.43 us
    ppermute x2, starting transfers between devices, swap(): return lax.ppermute(value, axis, [(0, 1), (1, 0)])  3.82 us
  transfers between devices with their start and end apart: 2, of which 1 were waited for; matrix products, arithmetic and copies ran while one was open for 0% of the time, Pallas kernels for 0%

profile of v2, /device:TPU:64, one launch (start us, length us, event | category | flops | bytes accessed | tf_op | source)
XLA Modules:
  0.0 175.9 jit_solution(12252153232810875264)
XLA Ops:
  0.6 0.6 pad_add_fusion.place_ref
  1.2 1.7 shard_map.118
  2.9 28.2 %all_to_all.25 = bf16[16,32,128]{2,1,0:T(8,128)(2,1)S(1)} all-to-all(bf16[16,32,128]{2,1,0:T(8,128)(2,1)} %shard_map.118), channel_id=1, replica_groups=mesh['y'=4,'x'=4,'zh'=2,'c'=2,'s'=8] {'zh','s'}, dimensions={0} | all-to-all | bytes 262144 | tf_op jit(solution)/shard_map/all_to_all | solution.py:52
  31.1 0.4 broadcast_in_dim.8
  31.5 0.0 copy-start.2
  31.5 33.0 %all_to_all.26 = bf16[16,512,128]{2,1,0:T(8,128)(2,1)S(1)} all-to-all(bf16[16,512,128]{2,1,0:T(8,128)(2,1)S(1)} %broadcast_in_dim.8), channel_id=1, replica_groups=mesh['y'=4,'x'=4,'zh'=2,'c'=2,'s'=8] {'y','x'}, dimensions={0} | all-to-all | bytes 4194304 | tf_op jit(solution)/shard_map/all_to_all | solution.py:52
  64.5 0.0 copy-start
  64.5 1.9 %collective-permute-start = (bf16[8192,128]{1,0:T(8,128)(2,1)S(1)}, bf16[8192,128]{1,0:T(8,128)(2,1)}, u32[]{:S(2)}, u32[]{:S(2)}) collective-permute-start(bf16[8192,128]{1,0:T(8,128)(2,1)S(1)} %bitcast.14), channel_id=1, source_target_pairs={{0,8},{8,0},{1,9},{9,1},{2,10},{10,2},{3,11},{11,3},{4,12},{12,4},... | collective-permute-start | bytes 6291464 | tf_op jit(solution)/shard_map/ppermute | solution.py:56
  66.4 0.0 copy-done.2
  66.4 0.1 reshape.45
  66.5 21.9 %all_to_all.27 = bf16[8,8,1920]{2,1,0:T(8,128)(2,1)} all-to-all(bf16[8,8,1920]{2,1,0:T(8,128)(2,1)S(1)} %reshape.45), channel_id=1, replica_groups=mesh['y'=4,'x'=4,'zh'=2,'c'=2,'s'=8] {'s'}, dimensions={0} | all-to-all | bytes 491520 | tf_op jit(solution)/shard_map/all_to_all | solution.py:52
  88.4 0.0 collective-permute-done
  88.4 0.0 copy-done
  88.4 10.3 %shard_map.119 = (bf16[256,512]{1,0:T(8,128)(2,1)}, bf16[16,528,128]{2,1,0:T(8,128)(2,1)}, bf16[16,528,128]{2,1,0:T(8,128)(2,1)}) custom-call(s32[4]{0:T(128)} %pad_add_fusion.place_ref, bf16[256,512]{1,0:T(8,128)(2,1)} %bitcast.19, bf16[16,16,32,128]{3,2,1,0:T(8,128)(2,1)} %bitcast.15, bf16[16,16,32,128]{3,2,1,0:T(8,128)(2,1)} %bitcast.9.other_ref, ...), custom_call_target="tpu_custom_call" | custom-call | tf_op jit(solution)/shard_map/pallas_call | solution.py:62
  98.7 1.9 %collective-permute-start.1 = (bf16[8448,128]{1,0:T(8,128)(2,1)}, bf16[8448,128]{1,0:T(8,128)(2,1)S(1)}, u32[]{:S(2)}, u32[]{:S(2)}) collective-permute-start(bf16[8448,128]{1,0:T(8,128)(2,1)} %bitcast.21), channel_id=1, source_target_pairs={{0,8},{8,0},{1,9},{9,1},{2,10},{10,2},{3,11},{11,3},{4,12},{12,4},... | collective-permute-start | bytes 6488072 | tf_op jit(solution)/shard_map/ppermute | solution.py:56
  100.6 4.4 %collective-permute-done.1 = bf16[8448,128]{1,0:T(8,128)(2,1)S(1)} collective-permute-done((bf16[8448,128]{1,0:T(8,128)(2,1)}, bf16[8448,128]{1,0:T(8,128)(2,1)S(1)}, u32[]{:S(2)}, u32[]{:S(2)}) %collective-permute-start.1) | collective-permute-done | bytes 2162720 | tf_op jit(solution)/shard_map/ppermute | solution.py:56
  105.0 0.0 copy-start.1
  105.0 1.4 copy-done.1
  106.4 4.1 %shard_map.120 = bf16[16,528,128]{2,1,0:T(8,128)(2,1)} custom-call(bf16[16,528,128]{2,1,0:T(8,128)(2,1)} %get-tuple-element.15.left_ref, bf16[16,528,128]{2,1,0:T(8,128)(2,1)} %bitcast.16), custom_call_target="tpu_custom_call" | custom-call | tf_op jit(solution)/shard_map/pallas_call | solution.py:62
  110.5 34.2 %all_to_all.28.arrived_ref = bf16[16,528,128]{2,1,0:T(8,128)(2,1)} all-to-all(bf16[16,528,128]{2,1,0:T(8,128)(2,1)} %shard_map.120), channel_id=1, replica_groups=mesh['y'=4,'x'=4,'zh'=2,'c'=2,'s'=8] {'y','x'}, dimensions={0} | all-to-all | bytes 4325376 | tf_op jit(solution)/shard_map/all_to_all | solution.py:52
  144.7 2.6 %shard_map.121 = bf16[16,64,128]{2,1,0:T(8,128)(2,1)} custom-call(bf16[16,528,128]{2,1,0:T(8,128)(2,1)} %all_to_all.28.arrived_ref), custom_call_target="tpu_custom_call" | custom-call | tf_op jit(solution)/shard_map/pallas_call | solution.py:62
  147.4 26.9 %all_to_all.29.arrived_ref = bf16[16,64,128]{2,1,0:T(8,128)(2,1)} all-to-all(bf16[16,64,128]{2,1,0:T(8,128)(2,1)} %shard_map.121), channel_id=1, replica_groups=mesh['y'=4,'x'=4,'zh'=2,'c'=2,'s'=8] {'zh','s'}, dimensions={0} | all-to-all | bytes 524288 | tf_op jit(solution)/shard_map/all_to_all | solution.py:52
  174.3 1.6 shard_map.122
Async XLA Ops:
  31.5 34.9 %copy-start.2 = (bf16[16,4,1920]{2,1,0:T(4,128)(2,1)S(1)}, bf16[16,4,1920]{2,1,0:T(4,128)(2,1)}, u32[]{:S(2)}) copy-start(bf16[16,4,1920]{2,1,0:T(4,128)(2,1)} %param.13) | copy-start | bytes 737284
  64.5 23.9 %copy-start = (bf16[16,512,128]{2,1,0:T(8,128)(2,1)}, bf16[16,512,128]{2,1,0:T(8,128)(2,1)S(1)}, u32[]{:S(2)}) copy-start(bf16[16,512,128]{2,1,0:T(8,128)(2,1)S(1)} %all_to_all.26) | copy-start | bytes 6291460
  64.5 23.9 %collective-permute-start = (bf16[8192,128]{1,0:T(8,128)(2,1)S(1)}, bf16[8192,128]{1,0:T(8,128)(2,1)}, u32[]{:S(2)}, u32[]{:S(2)}) collective-permute-start(bf16[8192,128]{1,0:T(8,128)(2,1)S(1)} %bitcast.14), channel_id=1, source_target_pairs={{0,8},{8,0},{1,9},{9,1},{2,10},{10,2},{3,11},{11,3},{4,12},{12,4},... | collective-permute-start | bytes 6291464 | tf_op jit(solution)/shard_map/ppermute | solution.py:56
  98.7 6.3 %collective-permute-start.1 = (bf16[8448,128]{1,0:T(8,128)(2,1)}, bf16[8448,128]{1,0:T(8,128)(2,1)S(1)}, u32[]{:S(2)}, u32[]{:S(2)}) collective-permute-start(bf16[8448,128]{1,0:T(8,128)(2,1)} %bitcast.21), channel_id=1, source_target_pairs={{0,8},{8,0},{1,9},{9,1},{2,10},{10,2},{3,11},{11,3},{4,12},{12,4},... | collective-permute-start | bytes 6488072 | tf_op jit(solution)/shard_map/ppermute | solution.py:56
  105.0 1.4 copy-start.1

commit v3 on v2

--- a/solution.py
+++ b/solution.py
@@ -12,7 +12,6 @@
 wide = jnp.float32
 LANES = 128
 TILE = 16
-VMEM_BYTES = 56 * 1024 * 1024
 
 
 def gelu_parts(preact):
@@ -56,7 +55,7 @@
     return lax.ppermute(value, axis, [(0, 1), (1, 0)])
 
 
-def on_core(kernel, out_shape, scalars, arrays, scratch=(), flops=0, moved=0):
+def on_core(kernel, out_shape, scalars, arrays, scratch=(), megabytes=8):
     multiple = isinstance(out_shape, (list, tuple))
     vmem = pl.BlockSpec(memory_space=pltpu.VMEM)
     return pl.pallas_call(
@@ -65,23 +64,54 @@
         in_specs=[pl.BlockSpec(memory_space=pltpu.SMEM)] * len(scalars) + [vmem] * len(arrays),
         out_specs=[vmem] * len(out_shape) if multiple else vmem,
         scratch_shapes=list(scratch),
-        compiler_params=pltpu.CompilerParams(vmem_limit_bytes=VMEM_BYTES),
-        cost_estimate=pl.CostEstimate(flops=flops, bytes_accessed=moved, transcendentals=0),
+        compiler_params=pltpu.CompilerParams(vmem_limit_bytes=megabytes * 1024 * 1024),
     )(*scalars, *arrays)
 
 
-def pick_kernel(place_ref, six_ref, seven_ref, proj_ref, out_ref):
-    plane, half, core, section = (place_ref[k] for k in range(4))
-    lanes_conv = pl.ds(pl.multiple_of(lax.rem(section, 4) * LANES, LANES), LANES)
-    first = section < 4
-    conv = jnp.where(first, six_ref[:, lanes_conv].astype(wide), seven_ref[:, lanes_conv].astype(wide))
+def pick_kernel(place_ref, six_ref, seven_ref, proj_ref, grad_ref, conv_ref, out_ref):
+    plane, core = place_ref[0], place_ref[2]
+    lane_tiles = six_ref.shape[1] // LANES
+    for index, source in enumerate((six_ref, seven_ref)):
+        for lane in range(lane_tiles):
+            at = (index * lane_tiles + lane) * TILE
+            conv_ref[at : at + TILE] = source[:, lane * LANES : (lane + 1) * LANES]
+
+    sections = out_ref.shape[0]
+    rows = grad_ref.shape[0] // sections
+    width = grad_ref.shape[1]
+    wide_tiles = width // LANES
+    proj_at = (wide_tiles + 1) // 2 * TILE
     row_tiles = proj_ref.shape[0] // TILE
     row = pl.multiple_of(jnp.minimum(plane, row_tiles - 1) * TILE, TILE)
-    lane = pl.multiple_of((half * 2 + core) * LANES, LANES)
-    block = jnp.concatenate(
-        [conv.astype(narrow), proj_ref[pl.ds(row, TILE), pl.ds(lane, LANES)]], axis=0
-    )
-    out_ref[...] = jnp.broadcast_to(block[None], out_ref.shape)
+    proj = [
+        proj_ref[pl.ds(row, TILE), pl.ds(pl.multiple_of((core * 2 + k) * LANES, LANES), LANES)]
+        for k in range(2)
+    ]
+    for pair in range(sections // 2):
+        block = grad_ref[pair * 2 * rows : (pair + 1) * 2 * rows].astype(wide)
+        block = jnp.concatenate([block, jnp.zeros((2 * rows, LANES), wide)], axis=1)
+        for inner in range(2):
+            section = pair * 2 + inner
+            part = block[inner * rows : (inner + 1) * rows]
+            for tile in range(proj_at // TILE):
+                lane = 2 * tile * LANES
+                stacked = jnp.concatenate(
+                    [part[:, lane : lane + LANES], part[:, lane + LANES : lane + 2 * LANES]], axis=0
+                )
+                out_ref[section, tile * TILE : (tile + 1) * TILE] = stacked.astype(narrow)
+            for k in range(2):
+                out_ref[section, proj_at + k * TILE : proj_at + (k + 1) * TILE] = proj[k]
+
+
+def bundle_kernel(place_ref, own_ref, other_ref, arrived_ref, out_ref):
+    half = place_ref[1]
+    rows = own_ref.shape[0]
+    out_ref[pl.ds(pl.multiple_of(half * rows, TILE), rows)] = own_ref[...]
+    out_ref[pl.ds(pl.multiple_of((1 - half) * rows, TILE), rows)] = other_ref[...]
+    start = arrived_ref.shape[1] - 2 * TILE
+    for section in range(arrived_ref.shape[0]):
+        at = 2 * rows + section * 2 * TILE
+        out_ref[at : at + 2 * TILE] = arrived_ref[section, start:]
 
 
 def layer_kernel(
@@ -98,17 +128,17 @@
     six_ref,
     seven_ref,
     proj_ref,
+    rows_ref,
     term_six_ref,
     term_seven_ref,
     term_proj_ref,
 ):
     core = place_ref[2]
     channels = input_ref.shape[1]
-    frames = grad_ref.shape[0]
+    frames, width = rows_ref.shape
     lane_tiles = channels // LANES
     planes = own_ref.shape[0]
-    sections = own_ref.shape[1] // 2
-    width = grad_ref.shape[1]
+    sections = grad_ref.shape[0]
     section_rows = width // sections
     row_tiles = section_rows // TILE
 
@@ -120,23 +150,23 @@
                 )
                 for lane in range(lane_tiles):
                     lanes = slice(lane * LANES, (lane + 1) * LANES)
-                    six_ref[rows, lanes] = source[plane, half * sections + lane, :TILE]
-                    seven_ref[rows, lanes] = source[
-                        plane, half * sections + lane_tiles + lane, :TILE
-                    ]
+                    tile = half * 2 * lane_tiles + lane
+                    six_ref[rows, lanes] = source[plane, tile]
+                    seven_ref[rows, lanes] = source[plane, tile + lane_tiles]
         return carry
 
     lax.fori_loop(0, planes, place_tiles, 0)
 
     def place_proj(plane, carry):
-        for half in range(2):
+        for k in range(2):
             for source, index in ((own_ref, core), (other_ref, 1 - core)):
-                lanes = pl.ds(pl.multiple_of((half * 2 + index) * LANES, LANES), LANES)
+                lanes = pl.ds(pl.multiple_of((index * 2 + k) * LANES, LANES), LANES)
                 for section in range(sections):
                     rows = pl.ds(
                         pl.multiple_of(section * section_rows + plane * TILE, TILE), TILE
                     )
-                    proj_ref[rows, lanes] = source[plane, half * sections + section, TILE:]
+                    tile = 4 * lane_tiles + section * 2 + k
+                    proj_ref[rows, lanes] = source[plane, tile]
         return carry
 
     lax.fori_loop(0, row_tiles, place_proj, 0)
@@ -172,7 +202,17 @@
         rest = rows % (sections * run)
         return (rest // run) * (2 * run) + utterance * run + rest % run
 
-    grad_rows = matmul(one_hot((frames, frames), arrived_row), grad_ref[...]).astype(narrow)
+    eight = frames // sections
+    for section in range(sections):
+        for lane in range(width // LANES):
+            if lane % 2 == 0:
+                stacked = grad_ref[section, lane // 2 * TILE : (lane // 2 + 1) * TILE].astype(wide)
+            rows_ref[
+                section * eight : (section + 1) * eight, lane * LANES : (lane + 1) * LANES
+            ] = stacked[(lane % 2) * eight : (lane % 2 + 1) * eight]
+    grad_rows = matmul(
+        one_hot((frames, frames), arrived_row), rows_ref[...].astype(narrow)
+    ).astype(narrow)
     term_proj_ref[...] = matmul(normed, grad_rows, (0, 0))
 
     grad_normed = matmul(grad_rows, proj_ref[...])
@@ -248,13 +288,6 @@
     spread_sums = jnp.broadcast_to(sums[None], (planes,) + sums.shape)
     kept_ref[:, at:] = spread_sums
     given_ref[:, at:] = spread_sums
-
-
-def add_kernel(left_ref, right_ref, out_ref):
-    for plane in range(out_ref.shape[0]):
-        out_ref[plane] = (left_ref[plane].astype(wide) + right_ref[plane].astype(wide)).astype(
-            narrow
-        )
 
 
 def plane_kernel(arrived_ref, out_ref, total_ref):
@@ -330,21 +363,34 @@
         [lax.axis_index(("y", "x")), lax.axis_index("zh"), lax.axis_index("c"), lax.axis_index("s")]
     ).astype(jnp.int32)
 
-    picked = on_core(
+    tile_rows = 2 * (channels // LANES) * TILE
+    grad_tiles = (width // LANES + 1) // 2
+    convs, outgoing = on_core(
         pick_kernel,
-        shape((2 * sections, 2 * TILE, LANES), narrow),
+        [
+            shape((tile_rows, LANES), narrow),
+            shape((sections, (grad_tiles + 2) * TILE, LANES), narrow),
+        ],
         [place],
-        [conv_six, conv_seven, proj_weight.T],
-    )
-    line = exchange(picked, ("zh", "s"))
-    bundle = line.reshape(1, 2 * sections * 2 * TILE, LANES)
-    gathered = exchange(jnp.broadcast_to(bundle, (planes,) + bundle.shape[1:]), ("y", "x"))
-    gathered_flat = gathered.reshape(-1, LANES)
-    sibling = swap(gathered_flat, "c")
-
-    grads = exchange(feature_grad.reshape(sections, -1, width), "s").reshape(frames, width)
-
-    tiles_shape = (planes, 2 * sections, 2 * TILE, LANES)
+        [conv_six, conv_seven, proj_weight.T, feature_grad.reshape(frames, width)],
+    )
+    line = 2 * sections
+    opposite = [
+        (z, (1 - z // sections) * sections + (z % sections + sections // 2) % sections)
+        for z in range(line)
+    ]
+    other_convs = lax.ppermute(convs, ("zh", "s"), opposite)
+    arrived = exchange(outgoing, "s")
+    bundle = on_core(
+        bundle_kernel,
+        shape((2 * tile_rows + sections * 2 * TILE, LANES), narrow),
+        [place],
+        [convs, other_convs, arrived],
+    )
+    gathered = exchange(jnp.broadcast_to(bundle[None], (planes,) + bundle.shape), ("y", "x"))
+    sibling = swap(gathered.reshape(-1, LANES), "c")
+
+    tiles_shape = (planes, bundle.shape[0] // TILE, TILE, LANES)
     send_rows = (4 * (channels // LANES) + width // LANES + 2) * TILE
     back, kept, given = on_core(
         layer_kernel,
@@ -358,7 +404,7 @@
             layer_five.reshape(4 * frames, channels),
             gathered.reshape(tiles_shape),
             sibling.reshape(tiles_shape),
-            grads,
+            arrived,
             gains,
             biases,
         ],
@@ -366,13 +412,15 @@
             pltpu.VMEM((2 * channels, channels), narrow),
             pltpu.VMEM((2 * channels, channels), narrow),
             pltpu.VMEM((width, channels), narrow),
+            pltpu.VMEM((frames, width), wide),
             pltpu.VMEM((2 * channels, channels), wide),
             pltpu.VMEM((2 * channels, channels), wide),
             pltpu.VMEM((channels, width), wide),
         ],
+        megabytes=36,
     )
     received = swap(given.reshape(-1, LANES), "c").reshape(given.shape)
-    chip = on_core(add_kernel, shape(kept.shape, narrow), [], [kept, received])
+    chip = (kept.astype(wide) + received.astype(wide)).astype(narrow)
     plane_in = exchange(chip, ("y", "x"))
     line_out = on_core(
         plane_kernel,

time: 176 us -> 151 us (0.86)
  the two profiles are of different devices: /device:TPU:64 before, /device:TPU:32 now
where the time goes in v3:
time: 151 us; the launch traced here: 150 us
  blocking collectives  90.7 us (60%)
  starting transfers between devices  24.7 us (16%)
  waiting for transfers between devices  19.6 us (13%)
  Pallas kernels  9.98 us (7%)
  local copies, waits for them, and re-layouts  3.8 us (3%)
    all_to_all x3, blocking collectives, exchange(): return lax.all_to_all(value, axes, 0, 0, tiled=True)  90.7 us
    all_to_all x1, starting transfers between devices, exchange(): return lax.all_to_all(value, axes, 0, 0, tiled=True)  12.6 us
    pallas_call x5, Pallas kernels, on_core(): pl.pallas_call(kernel, out_shape=out_shape, in_specs=[pl.BlockSpec(memory...  9.98 us
    ppermute x2, waiting for transfers between devices, swap(): return lax.ppermute(value, axis, [(0, 1), (1, 0)])  8.25 us
    ppermute x1, starting transfers between devices, on_device(): other_convs = lax.ppermute(convs, ('zh', 's'), opposite)  8.21 us
    ppermute x1, waiting for transfers between devices, on_device(): other_convs = lax.ppermute(convs, ('zh', 's'), opposite)  5.73 us
    all_to_all x1, waiting for transfers between devices, exchange(): return lax.all_to_all(value, axes, 0, 0, tiled=True)  5.66 us
    ppermute x2, starting transfers between devices, swap(): return lax.ppermute(value, axis, [(0, 1), (1, 0)])  3.91 us
  transfers between devices with their start and end apart: 4, of which 4 were waited for; matrix products, arithmetic and copies ran while one was open for 0% of the time, Pallas kernels for 0%

profile of v3, /device:TPU:32, one launch (start us, length us, event | category | flops | bytes accessed | tf_op | source)
XLA Modules:
  0.0 150.3 jit_solution(44567737947750763)
XLA Ops:
  0.6 1.0 reshape.38.grad_ref
  1.7 0.1 pad_add_fusion.place_ref
  1.7 0.0 copy-start.1
  1.7 0.9 copy-done.1
  2.7 0.0 copy-start.2
  2.7 0.7 copy-done.2
  3.4 0.0 copy-start.3
  3.4 0.7 copy-done.3
  4.1 1.3 shard_map.118
  5.4 12.6 %all-to-all-start = ((bf16[8,160,128]{2,1,0:T(8,128)(2,1)}), bf16[8,160,128]{2,1,0:T(8,128)(2,1)S(1)}, u32[]{:S(2)}, u32[]{:S(2)}) async-start(bf16[8,160,128]{2,1,0:T(8,128)(2,1)} %get-tuple-element.17), calls=%async_computation | async-start | bytes 655360 | tf_op jit(solution)/shard_map/all_to_all | solution.py:51
  18.1 8.2 %collective-permute-start = (bf16[128,128]{1,0:T(8,128)(2,1)S(1)}, bf16[128,128]{1,0:T(8,128)(2,1)S(1)}, u32[]{:S(2)}, u32[]{:S(2)}) collective-permute-start(bf16[128,128]{1,0:T(8,128)(2,1)S(1)} %get-tuple-element.16.own_ref), channel_id=1, source_target_pairs={{0,20},{1,21},{2,22},{3,23},{4,16},{5,17},{6,18},{7,19},{16,4},{17... | collective-permute-start | bytes 98312 | tf_op jit(solution)/shard_map/ppermute | solution.py:382
  26.3 5.7 %collective-permute-done.other_ref = bf16[128,128]{1,0:T(8,128)(2,1)S(1)} collective-permute-done((bf16[128,128]{1,0:T(8,128)(2,1)S(1)}, bf16[128,128]{1,0:T(8,128)(2,1)S(1)}, u32[]{:S(2)}, u32[]{:S(2)}) %collective-permute-start) | collective-permute-done | bytes 32800 | tf_op jit(solution)/shard_map/ppermute | solution.py:382
  32.0 5.7 %all-to-all-done.arrived_ref.grad_ref = bf16[8,160,128]{2,1,0:T(8,128)(2,1)S(1)} async-done(((bf16[8,160,128]{2,1,0:T(8,128)(2,1)}), bf16[8,160,128]{2,1,0:T(8,128)(2,1)S(1)}, u32[]{:S(2)}, u32[]{:S(2)}) %all-to-all-start) | async-done | bytes 327712 | tf_op jit(solution)/shard_map/all_to_all | solution.py:51
  37.7 0.6 shard_map.119
  38.2 0.4 broadcast_in_dim.2
  38.6 0.0 copy-start
  38.6 0.0 copy-start.4
  38.7 0.0 copy-start.5
  38.7 30.1 %all_to_all.20 = bf16[16,512,128]{2,1,0:T(8,128)(2,1)S(1)} all-to-all(bf16[16,512,128]{2,1,0:T(8,128)(2,1)S(1)} %broadcast_in_dim.2), channel_id=1, replica_groups=mesh['y'=4,'x'=4,'zh'=2,'c'=2,'s'=8] {'y','x'}, dimensions={0} | all-to-all | bytes 4194304 | tf_op jit(solution)/shard_map/all_to_all | solution.py:51
  68.8 1.9 %collective-permute-start.1 = (bf16[8192,128]{1,0:T(8,128)(2,1)S(1)}, bf16[8192,128]{1,0:T(8,128)(2,1)S(1)}, u32[]{:S(2)}, u32[]{:S(2)}) collective-permute-start(bf16[8192,128]{1,0:T(8,128)(2,1)S(1)} %bitcast.13), channel_id=1, source_target_pairs={{0,8},{8,0},{1,9},{9,1},{2,10},{10,2},{3,11},{11,3},{4,12},{12,4},... | collective-permute-start | bytes 6291464 | tf_op jit(solution)/shard_map/ppermute | solution.py:55
  70.7 4.1 %collective-permute-done.1 = bf16[8192,128]{1,0:T(8,128)(2,1)S(1)} collective-permute-done((bf16[8192,128]{1,0:T(8,128)(2,1)S(1)}, bf16[8192,128]{1,0:T(8,128)(2,1)S(1)}, u32[]{:S(2)}, u32[]{:S(2)}) %collective-permute-start.1) | collective-permute-done | bytes 2097184 | tf_op jit(solution)/shard_map/ppermute | solution.py:55
  74.8 0.0 copy-done
  74.8 0.0 copy-done.4
  74.8 0.0 copy-done.5
  74.8 7.1 %shard_map.120 = (bf16[256,512]{1,0:T(8,128)(2,1)}, bf16[16,528,128]{2,1,0:T(8,128)(2,1)S(1)}, bf16[16,528,128]{2,1,0:T(8,128)(2,1)S(1)}) custom-call(s32[4]{0:T(128)S(1)} %pad_add_fusion.place_ref, bf16[256,512]{1,0:T(8,128)(2,1)S(1)} %bitcast.16, bf16[16,32,16,128]{3,2,1,0:T(8,128)(2,1)S(1)} %bitcast.14, bf16[16,32,16,128]{3,2,1,0:T(8,128)(2,1)S(1)} %bitcast.15, ...), custom_call_target="tpu_custom_call" | custom-call | tf_op jit(solution)/shard_map/pallas_call | solution.py:61
  81.9 2.0 %collective-permute-start.2 = (bf16[8448,128]{1,0:T(8,128)(2,1)S(1)}, bf16[8448,128]{1,0:T(8,128)(2,1)S(1)}, u32[]{:S(2)}, u32[]{:S(2)}) collective-permute-start(bf16[8448,128]{1,0:T(8,128)(2,1)S(1)} %bitcast.18), channel_id=1, source_target_pairs={{0,8},{8,0},{1,9},{9,1},{2,10},{10,2},{3,11},{11,3},{4,12},{12,4},... | collective-permute-start | bytes 6488072 | tf_op jit(solution)/shard_map/ppermute | solution.py:55
  83.9 4.1 %collective-permute-done.2 = bf16[8448,128]{1,0:T(8,128)(2,1)S(1)} collective-permute-done((bf16[8448,128]{1,0:T(8,128)(2,1)S(1)}, bf16[8448,128]{1,0:T(8,128)(2,1)S(1)}, u32[]{:S(2)}, u32[]{:S(2)}) %collective-permute-start.2) | collective-permute-done | bytes 2162720 | tf_op jit(solution)/shard_map/ppermute | solution.py:55
  88.1 0.6 fusion
  88.6 32.3 %all_to_all.21.arrived_ref = bf16[16,528,128]{2,1,0:T(8,128)(2,1)S(1)} all-to-all(bf16[16,528,128]{2,1,0:T(8,128)(2,1)S(1)} %fusion), channel_id=1, replica_groups=mesh['y'=4,'x'=4,'zh'=2,'c'=2,'s'=8] {'y','x'}, dimensions={0} | all-to-all | bytes 4325376 | tf_op jit(solution)/shard_map/all_to_all | solution.py:51
  120.9 0.3 shard_map.121
  121.2 28.3 %all_to_all.22.arrived_ref = bf16[16,64,128]{2,1,0:T(8,128)(2,1)S(1)} all-to-all(bf16[16,64,128]{2,1,0:T(8,128)(2,1)S(1)} %shard_map.121), channel_id=1, replica_groups=mesh['y'=4,'x'=4,'zh'=2,'c'=2,'s'=8] {'zh','s'}, dimensions={0} | all-to-all | bytes 524288 | tf_op jit(solution)/shard_map/all_to_all | solution.py:51
  149.6 0.7 shard_map.122
Async XLA Ops:
  1.7 0.9 copy-start.1
  2.7 0.7 copy-start.2
  3.4 0.7 copy-start.3
  5.4 32.2 %all-to-all-start = ((bf16[8,160,128]{2,1,0:T(8,128)(2,1)}), bf16[8,160,128]{2,1,0:T(8,128)(2,1)S(1)}, u32[]{:S(2)}, u32[]{:S(2)}) async-start(bf16[8,160,128]{2,1,0:T(8,128)(2,1)} %get-tuple-element.17), calls=%async_computation | async-start | bytes 655360 | tf_op jit(solution)/shard_map/all_to_all | solution.py:51
  18.1 13.9 %collective-permute-start = (bf16[128,128]{1,0:T(8,128)(2,1)S(1)}, bf16[128,128]{1,0:T(8,128)(2,1)S(1)}, u32[]{:S(2)}, u32[]{:S(2)}) collective-permute-start(bf16[128,128]{1,0:T(8,128)(2,1)S(1)} %get-tuple-element.16.own_ref), channel_id=1, source_target_pairs={{0,20},{1,21},{2,22},{3,23},{4,16},{5,17},{6,18},{7,19},{16,4},{17... | collective-permute-start | bytes 98312 | tf_op jit(solution)/shard_map/ppermute | solution.py:382
  38.6 36.2 %copy-start = (bf16[2,128,512]{2,1,0:T(8,128)(2,1)S(1)}, bf16[2,128,512]{2,1,0:T(8,128)(2,1)}, u32[]{:S(2)}) copy-start(bf16[2,128,512]{2,1,0:T(8,128)(2,1)} %param.7) | copy-start | bytes 786436
  38.6 36.2 %copy-start.4 = (f32[3,512]{1,0:T(4,128)S(1)}, f32[3,512]{1,0:T(4,128)}, u32[]{:S(2)}) copy-start(f32[3,512]{1,0:T(4,128)} %gains_ref.1) | copy-start | bytes 18436
  38.7 36.2 %copy-start.5 = (f32[3,512]{1,0:T(4,128)S(1)}, f32[3,512]{1,0:T(4,128)}, u32[]{:S(2)}) copy-start(f32[3,512]{1,0:T(4,128)} %biases_ref.1) | copy-start | bytes 18436
  68.8 6.0 %collective-permute-start.1 = (bf16[8192,128]{1,0:T(8,128)(2,1)S(1)}, bf16[8192,128]{1,0:T(8,128)(2,1)S(1)}, u32[]{:S(2)}, u32[]{:S(2)}) collective-permute-start(bf16[8192,128]{1,0:T(8,128)(2,1)S(1)} %bitcast.13), channel_id=1, source_target_pairs={{0,8},{8,0},{1,9},{9,1},{2,10},{10,2},{3,11},{11,3},{4,12},{12,4},... | collective-permute-start | bytes 6291464 | tf_op jit(solution)/shard_map/ppermute | solution.py:55
  81.9 6.1 %collective-permute-start.2 = (bf16[8448,128]{1,0:T(8,128)(2,1)S(1)}, bf16[8448,128]{1,0:T(8,128)(2,1)S(1)}, u32[]{:S(2)}, u32[]{:S(2)}) collective-permute-start(bf16[8448,128]{1,0:T(8,128)(2,1)S(1)} %bitcast.18), channel_id=1, source_target_pairs={{0,8},{8,0},{1,9},{9,1},{2,10},{10,2},{3,11},{11,3},{4,12},{12,4},... | collective-permute-start | bytes 6488072 | tf_op jit(solution)/shard_map/ppermute | solution.py:55

commit v4 on v2

--- a/solution.py
+++ b/solution.py
@@ -12,7 +12,6 @@
 wide = jnp.float32
 LANES = 128
 TILE = 16
-VMEM_BYTES = 56 * 1024 * 1024
 
 
 def gelu_parts(preact):
@@ -56,7 +55,7 @@
     return lax.ppermute(value, axis, [(0, 1), (1, 0)])
 
 
-def on_core(kernel, out_shape, scalars, arrays, scratch=(), flops=0, moved=0):
+def on_core(kernel, out_shape, scalars, arrays, scratch=(), megabytes=8):
     multiple = isinstance(out_shape, (list, tuple))
     vmem = pl.BlockSpec(memory_space=pltpu.VMEM)
     return pl.pallas_call(
@@ -65,37 +64,117 @@
         in_specs=[pl.BlockSpec(memory_space=pltpu.SMEM)] * len(scalars) + [vmem] * len(arrays),
         out_specs=[vmem] * len(out_shape) if multiple else vmem,
         scratch_shapes=list(scratch),
-        compiler_params=pltpu.CompilerParams(vmem_limit_bytes=VMEM_BYTES),
-        cost_estimate=pl.CostEstimate(flops=flops, bytes_accessed=moved, transcendentals=0),
+        compiler_params=pltpu.CompilerParams(vmem_limit_bytes=megabytes * 1024 * 1024),
     )(*scalars, *arrays)
 
 
-def pick_kernel(place_ref, six_ref, seven_ref, proj_ref, out_ref):
-    plane, half, core, section = (place_ref[k] for k in range(4))
-    lanes_conv = pl.ds(pl.multiple_of(lax.rem(section, 4) * LANES, LANES), LANES)
-    first = section < 4
-    conv = jnp.where(first, six_ref[:, lanes_conv].astype(wide), seven_ref[:, lanes_conv].astype(wide))
-    row_tiles = proj_ref.shape[0] // TILE
-    row = pl.multiple_of(jnp.minimum(plane, row_tiles - 1) * TILE, TILE)
-    lane = pl.multiple_of((half * 2 + core) * LANES, LANES)
-    block = jnp.concatenate(
-        [conv.astype(narrow), proj_ref[pl.ds(row, TILE), pl.ds(lane, LANES)]], axis=0
-    )
-    out_ref[...] = jnp.broadcast_to(block[None], out_ref.shape)
+def conv_kernel(six_ref, seven_ref, conv_ref):
+    lane_tiles = six_ref.shape[1] // LANES
+    for index, source in enumerate((six_ref, seven_ref)):
+        for lane in range(lane_tiles):
+            at = (index * lane_tiles + lane) * TILE
+            conv_ref[at : at + TILE] = source[:, lane * LANES : (lane + 1) * LANES]
+
+
+def pick_kernel(place_ref, proj_ref, grad_ref, out_ref):
+    sections = out_ref.shape[0]
+    utterances = grad_ref.shape[0] // sections
+    width = grad_ref.shape[2]
+    proj_at = (width // LANES + 1) // 2 * TILE
+    for section in range(sections):
+        part = jnp.concatenate(
+            [grad_ref[section * utterances + k].astype(wide) for k in range(utterances)], axis=0
+        )
+        part = jnp.concatenate([part, jnp.zeros((part.shape[0], LANES), wide)], axis=1)
+        for tile in range(proj_at // TILE):
+            lane = 2 * tile * LANES
+            stacked = jnp.concatenate(
+                [part[:, lane : lane + LANES], part[:, lane + LANES : lane + 2 * LANES]], axis=0
+            )
+            out_ref[section, tile * TILE : (tile + 1) * TILE] = stacked.astype(narrow)
+        for k in range(2):
+            out_ref[section, proj_at + k * TILE : proj_at + (k + 1) * TILE] = proj_ref[
+                :, k * LANES : (k + 1) * LANES
+            ]
+
+
+def bundle_kernel(place_ref, own_ref, other_ref, arrived_ref, out_ref):
+    half = place_ref[1]
+    rows = own_ref.shape[0]
+    start = arrived_ref.shape[1] - 2 * TILE
+    for plane in range(out_ref.shape[0]):
+        out_ref[plane, pl.ds(pl.multiple_of(half * rows, TILE), rows)] = own_ref[...]
+        out_ref[plane, pl.ds(pl.multiple_of((1 - half) * rows, TILE), rows)] = other_ref[...]
+        for section in range(arrived_ref.shape[0]):
+            at = 2 * rows + section * 2 * TILE
+            out_ref[plane, at : at + 2 * TILE] = arrived_ref[section, start:]
+
+
+def position_order(frames):
+    def source_row(rows):
+        run = rows // frames
+        return 4 * (rows % frames) + (run % 2) * 2 + run // 2
+
+    return one_hot((4 * frames, 4 * frames), source_row)
+
+
+def place_proj(source_ref, proj_ref, row_tiles, section_rows):
+    sections = proj_ref.shape[0] // section_rows
+    first = source_ref.shape[1] - 2 * sections
+
+    def step(plane, carry):
+        for section in range(sections):
+            rows = pl.ds(pl.multiple_of(section * section_rows + plane * TILE, TILE), TILE)
+            for k in range(2):
+                proj_ref[rows, k * LANES : (k + 1) * LANES] = source_ref[
+                    plane, first + section * 2 + k
+                ]
+        return carry
+
+    lax.fori_loop(0, row_tiles, step, 0)
+
+
+def early_kernel(input_ref, own_ref, grad_ref, taps_ref, cotangent_ref, part_ref, proj_ref, rows_ref):
+    frames, width = rows_ref.shape
+    sections = grad_ref.shape[0]
+    taps_ref[...] = matmul(position_order(frames), input_ref[...]).astype(narrow)
+
+    run = frames // (2 * sections)
+
+    def arrived_row(rows):
+        utterance = rows // (sections * run)
+        rest = rows % (sections * run)
+        return (rest // run) * (2 * run) + utterance * run + rest % run
+
+    eight = frames // sections
+    for section in range(sections):
+        for lane in range(width // LANES):
+            if lane % 2 == 0:
+                stacked = grad_ref[section, lane // 2 * TILE : (lane // 2 + 1) * TILE].astype(wide)
+            rows_ref[
+                section * eight : (section + 1) * eight, lane * LANES : (lane + 1) * LANES
+            ] = stacked[(lane % 2) * eight : (lane % 2 + 1) * eight]
+    grad_rows = matmul(
+        one_hot((frames, frames), arrived_row), rows_ref[...].astype(narrow)
+    ).astype(narrow)
+    cotangent_ref[...] = grad_rows
+    place_proj(own_ref, proj_ref, width // sections // TILE, width // sections)
+    part_ref[...] = matmul(grad_rows, proj_ref[...])
 
 
 def layer_kernel(
     place_ref,
-    input_ref,
+    taps_ref,
     own_ref,
     other_ref,
-    grad_ref,
+    cotangent_ref,
+    part_ref,
     gains_ref,
     biases_ref,
-    back_ref,
+    six_ref,
+    dhid_ref,
     kept_ref,
     given_ref,
-    six_ref,
     seven_ref,
     proj_ref,
     term_six_ref,
@@ -103,14 +182,12 @@
     term_proj_ref,
 ):
     core = place_ref[2]
-    channels = input_ref.shape[1]
-    frames = grad_ref.shape[0]
+    channels = taps_ref.shape[1]
+    frames, width = cotangent_ref.shape
     lane_tiles = channels // LANES
     planes = own_ref.shape[0]
-    sections = own_ref.shape[1] // 2
-    width = grad_ref.shape[1]
+    sections = (own_ref.shape[1] - 4 * lane_tiles) // 2
     section_rows = width // sections
-    row_tiles = section_rows // TILE
 
     def place_tiles(plane, carry):
         for half in range(2):
@@ -120,36 +197,15 @@
                 )
                 for lane in range(lane_tiles):
                     lanes = slice(lane * LANES, (lane + 1) * LANES)
-                    six_ref[rows, lanes] = source[plane, half * sections + lane, :TILE]
-                    seven_ref[rows, lanes] = source[
-                        plane, half * sections + lane_tiles + lane, :TILE
-                    ]
+                    tile = half * 2 * lane_tiles + lane
+                    six_ref[rows, lanes] = source[plane, tile]
+                    seven_ref[rows, lanes] = source[plane, tile + lane_tiles]
         return carry
 
     lax.fori_loop(0, planes, place_tiles, 0)
 
-    def place_proj(plane, carry):
-        for half in range(2):
-            for source, index in ((own_ref, core), (other_ref, 1 - core)):
-                lanes = pl.ds(pl.multiple_of((half * 2 + index) * LANES, LANES), LANES)
-                for section in range(sections):
-                    rows = pl.ds(
-                        pl.multiple_of(section * section_rows + plane * TILE, TILE), TILE
-                    )
-                    proj_ref[rows, lanes] = source[plane, half * sections + section, TILE:]
-        return carry
-
-    lax.fori_loop(0, row_tiles, place_proj, 0)
-
-    count = 4 * frames
-
-    def source_row(rows):
-        run = rows // frames
-        return 4 * (rows % frames) + (run % 2) * 2 + run // 2
-
-    order = one_hot((count, count), source_row)
-    positions = matmul(order, input_ref[...]).astype(narrow)
-    tap_zero, tap_one = positions[: 2 * frames], positions[2 * frames :]
+    place_proj(other_ref, proj_ref, section_rows // TILE, section_rows)
+    tap_zero, tap_one = taps_ref[: 2 * frames], taps_ref[2 * frames :]
     hid_six = matmul(tap_zero, six_ref[:channels]) + matmul(tap_one, six_ref[channels:])
     pre_six, part_six, scale_six = norm_forward(hid_six, gains_ref[0:1], biases_ref[0:1])
     act_six_f, deriv_six = gelu_parts(pre_six)
@@ -165,17 +221,13 @@
     )
     normed = pre_feat.astype(narrow)
 
-    run = frames // (2 * sections)
-
-    def arrived_row(rows):
-        utterance = rows // (sections * run)
-        rest = rows % (sections * run)
-        return (rest // run) * (2 * run) + utterance * run + rest % run
-
-    grad_rows = matmul(one_hot((frames, frames), arrived_row), grad_ref[...]).astype(narrow)
+    grad_rows = cotangent_ref[...]
     term_proj_ref[...] = matmul(normed, grad_rows, (0, 0))
-
-    grad_normed = matmul(grad_rows, proj_ref[...])
+    own_half, other_half = part_ref[...], matmul(grad_rows, proj_ref[...])
+    first = core == 0
+    grad_normed = jnp.concatenate(
+        [jnp.where(first, own_half, other_half), jnp.where(first, other_half, own_half)], axis=1
+    )
     dact_seven = norm_backward(grad_normed, part_feat, scale_feat, gains_ref[2:3])
     dpre_seven = dact_seven * deriv_seven
     dhid_seven = norm_backward(dpre_seven, part_seven, scale_seven, gains_ref[1:2]).astype(narrow)
@@ -190,17 +242,9 @@
     )
     dpre_six = dact_six * deriv_six
     dhid_six = norm_backward(dpre_six, part_six, scale_six, gains_ref[0:1]).astype(narrow)
+    dhid_ref[...] = dhid_six
     term_six_ref[:channels] = matmul(tap_zero, dhid_six, (0, 0))
     term_six_ref[channels:] = matmul(tap_one, dhid_six, (0, 0))
-    back = jnp.concatenate(
-        [
-            matmul(dhid_six, six_ref[:channels], (1, 1)).astype(narrow),
-            matmul(dhid_six, six_ref[channels:], (1, 1)).astype(narrow),
-        ],
-        axis=0,
-    )
-    back_ref[...] = matmul(order, back, (0, 0)).astype(narrow)
-
     half_rows = TILE // 2
 
     def pack(plane, carry):
@@ -237,12 +281,13 @@
             total(dpre_six),
             total(dpre_seven),
             total(grad_normed),
-            jnp.zeros((2, channels), wide),
         ],
         axis=0,
     )
     sums = jnp.concatenate(
-        [sums[:, lane * LANES : (lane + 1) * LANES] for lane in range(lane_tiles)], axis=0
+        [sums[:, lane * LANES : (lane + 1) * LANES] for lane in range(lane_tiles)]
+        + [jnp.zeros((TILE // 2, LANES), wide)],
+        axis=0,
     ).astype(narrow)
     at = (4 * lane_tiles + width // LANES) * TILE
     spread_sums = jnp.broadcast_to(sums[None], (planes,) + sums.shape)
@@ -250,11 +295,16 @@
     given_ref[:, at:] = spread_sums
 
 
-def add_kernel(left_ref, right_ref, out_ref):
-    for plane in range(out_ref.shape[0]):
-        out_ref[plane] = (left_ref[plane].astype(wide) + right_ref[plane].astype(wide)).astype(
-            narrow
-        )
+def input_kernel(dhid_ref, six_ref, back_ref):
+    channels = back_ref.shape[1]
+    back = jnp.concatenate(
+        [
+            matmul(dhid_ref[...], six_ref[:channels], (1, 1)).astype(narrow),
+            matmul(dhid_ref[...], six_ref[channels:], (1, 1)).astype(narrow),
+        ],
+        axis=0,
+    )
+    back_ref[...] = matmul(position_order(back_ref.shape[0] // 4), back, (0, 0)).astype(narrow)
 
 
 def plane_kernel(arrived_ref, out_ref, total_ref):
@@ -295,7 +345,7 @@
             out_ref[half * sections + section, TILE : 2 * TILE] = jnp.concatenate(
                 [moved[rows_of, :LANES], moved[rows_of, LANES : 2 * LANES]], axis=0
             ).astype(narrow)
-    sums = total_ref[rows - 2 * TILE :].astype(narrow)
+    sums = total_ref[rows - 2 * TILE : rows - TILE // 2].astype(narrow)
     out_ref[:, 2 * TILE :] = jnp.broadcast_to(sums[None], (2 * sections,) + sums.shape)
 
 
@@ -312,7 +362,7 @@
     )
     proj_ref[...] = proj[:, : proj_ref.shape[1]]
     sums = jnp.concatenate(
-        [running[2 * TILE + k * rows : 2 * TILE + (k + 1) * rows] for k in range(4)], axis=1
+        [running[2 * TILE + k * 6 : 2 * TILE + (k + 1) * 6] for k in range(4)], axis=1
     )
     gains_ref[...] = sums[:3]
     biases_ref[...] = sums[3:6]
@@ -330,53 +380,92 @@
         [lax.axis_index(("y", "x")), lax.axis_index("zh"), lax.axis_index("c"), lax.axis_index("s")]
     ).astype(jnp.int32)
 
-    picked = on_core(
+    tile_rows = 2 * (channels // LANES) * TILE
+    grad_tiles = (width // LANES + 1) // 2
+    convs = on_core(conv_kernel, shape((tile_rows, LANES), narrow), [], [conv_six, conv_seven])
+    row_tiles = part_width // TILE
+    out_block = (sections, (grad_tiles + 2) * TILE, LANES)
+    outgoing = pl.pallas_call(
         pick_kernel,
-        shape((2 * sections, 2 * TILE, LANES), narrow),
+        out_shape=shape(out_block, narrow),
+        grid_spec=pltpu.PrefetchScalarGridSpec(
+            num_scalar_prefetch=1,
+            grid=(1,),
+            in_specs=[
+                pl.BlockSpec(
+                    (TILE, 2 * LANES), lambda i, at: (jnp.minimum(at[0], row_tiles - 1), at[2])
+                ),
+                pl.BlockSpec(feature_grad.shape, lambda i, at: (0, 0, 0)),
+            ],
+            out_specs=pl.BlockSpec(out_block, lambda i, at: (0, 0, 0)),
+        ),
+        compiler_params=pltpu.CompilerParams(vmem_limit_bytes=8 * 1024 * 1024),
+    )(place, proj_weight.T, feature_grad)
+    line = 2 * sections
+    opposite = [
+        (z, (1 - z // sections) * sections + (z % sections + sections // 2) % sections)
+        for z in range(line)
+    ]
+    other_convs = lax.ppermute(convs, ("zh", "s"), opposite)
+    arrived = exchange(outgoing, "s")
+    bundle = on_core(
+        bundle_kernel,
+        shape((planes, 2 * tile_rows + sections * 2 * TILE, LANES), narrow),
         [place],
-        [conv_six, conv_seven, proj_weight.T],
-    )
-    line = exchange(picked, ("zh", "s"))
-    bundle = line.reshape(1, 2 * sections * 2 * TILE, LANES)
-    gathered = exchange(jnp.broadcast_to(bundle, (planes,) + bundle.shape[1:]), ("y", "x"))
-    gathered_flat = gathered.reshape(-1, LANES)
-    sibling = swap(gathered_flat, "c")
-
-    grads = exchange(feature_grad.reshape(sections, -1, width), "s").reshape(frames, width)
-
-    tiles_shape = (planes, 2 * sections, 2 * TILE, LANES)
+        [convs, other_convs, arrived],
+    )
+    gathered = exchange(bundle, ("y", "x"))
+    sibling = swap(gathered.reshape(-1, LANES), "c")
+
+    tiles_shape = (planes, bundle.shape[1] // TILE, TILE, LANES)
     send_rows = (4 * (channels // LANES) + width // LANES + 2) * TILE
-    back, kept, given = on_core(
+    taps, cotangents, part = on_core(
+        early_kernel,
+        [
+            shape((4 * frames, channels), narrow),
+            shape((frames, width), narrow),
+            shape((frames, 2 * LANES), wide),
+        ],
+        [],
+        [layer_five.reshape(4 * frames, channels), gathered.reshape(tiles_shape), arrived],
+        scratch=[pltpu.VMEM((width, 2 * LANES), narrow), pltpu.VMEM((frames, width), wide)],
+    )
+    six_full, dhid_six, kept, given = on_core(
         layer_kernel,
         [
-            shape((4 * frames, channels), narrow),
+            shape((2 * channels, channels), narrow),
+            shape((2 * frames, channels), narrow),
             shape((planes, send_rows, LANES), narrow),
             shape((planes, send_rows, LANES), narrow),
         ],
         [place],
         [
-            layer_five.reshape(4 * frames, channels),
+            taps,
             gathered.reshape(tiles_shape),
             sibling.reshape(tiles_shape),
-            grads,
+            cotangents,
+            part,
             gains,
             biases,
         ],
         scratch=[
             pltpu.VMEM((2 * channels, channels), narrow),
-            pltpu.VMEM((2 * channels, channels), narrow),
-            pltpu.VMEM((width, channels), narrow),
+            pltpu.VMEM((width, 2 * LANES), narrow),
             pltpu.VMEM((2 * channels, channels), wide),
             pltpu.VMEM((2 * channels, channels), wide),
             pltpu.VMEM((channels, width), wide),
         ],
+        megabytes=36,
+    )
+    back = on_core(
+        input_kernel, shape((4 * frames, channels), narrow), [], [dhid_six, six_full]
     )
     received = swap(given.reshape(-1, LANES), "c").reshape(given.shape)
-    chip = on_core(add_kernel, shape(kept.shape, narrow), [], [kept, received])
+    chip = (kept.astype(wide) + received.astype(wide)).astype(narrow)
     plane_in = exchange(chip, ("y", "x"))
     line_out = on_core(
         plane_kernel,
-        shape((2 * sections, 4 * TILE, LANES), narrow),
+        shape((2 * sections, 3 * TILE + TILE // 2, LANES), narrow),
         [],
         [plane_in],
         scratch=[pltpu.VMEM((send_rows, LANES), wide)],

time: 176 us -> 148 us (0.84)
  the two profiles are of different devices: /device:TPU:64 before, /device:TPU:32 now
where the time goes in v4:
time: 148 us; the launch traced here: 147 us
  blocking collectives  63.3 us (43%)
  starting transfers between devices  35 us (24%)
  waiting for transfers between devices  32.5 us (22%)
  Pallas kernels  11.7 us (8%)
  local copies, waits for them, and re-layouts  3.34 us (2%)
    all_to_all x2, blocking collectives, exchange(): return lax.all_to_all(value, axes, 0, 0, tiled=True)  63.3 us
    all_to_all x2, starting transfers between devices, exchange(): return lax.all_to_all(value, axes, 0, 0, tiled=True)  22.7 us
    all_to_all x2, waiting for transfers between devices, exchange(): return lax.all_to_all(value, axes, 0, 0, tiled=True)  20.8 us
    pallas_call x7, Pallas kernels, on_core(): pl.pallas_call(kernel, out_shape=out_shape, in_specs=[pl.BlockSpec(memory...  10.4 us
    ppermute x1, starting transfers between devices, on_device(): other_convs = lax.ppermute(convs, ('zh', 's'), opposite)  8.21 us
    ppermute x2, waiting for transfers between devices, swap(): return lax.ppermute(value, axis, [(0, 1), (1, 0)])  7.25 us
    ppermute x1, waiting for transfers between devices, on_device(): other_convs = lax.ppermute(convs, ('zh', 's'), opposite)  4.43 us
    ppermute x2, starting transfers between devices, swap(): return lax.ppermute(value, axis, [(0, 1), (1, 0)])  4.08 us
  transfers between devices with their start and end apart: 5, of which 5 were waited for; matrix products, arithmetic and copies ran while one was open for 0% of the time, Pallas kernels for 2%

profile of v4, /device:TPU:32, one launch (start us, length us, event | category | flops | bytes accessed | tf_op | source)
XLA Modules:
  0.0 147.1 jit_solution(1855390096913699252)
XLA Ops:
  0.6 0.1 pad_add_fusion.place_ref
  0.7 0.0 copy-start.1
  0.7 0.9 copy-done.1
  1.7 0.0 copy-start.2
  1.7 0.9 copy-done.2
  2.6 1.3 shard_map.119
  3.9 12.6 %all-to-all-start = ((bf16[8,160,128]{2,1,0:T(8,128)(2,1)}), bf16[8,160,128]{2,1,0:T(8,128)(2,1)S(1)}, u32[]{:S(2)}, u32[]{:S(2)}) async-start(bf16[8,160,128]{2,1,0:T(8,128)(2,1)} %shard_map.119), calls=%async_computation | async-start | bytes 655360 | tf_op jit(solution)/shard_map/all_to_all | solution.py:51
  16.6 0.0 copy-start.3
  16.6 0.7 copy-done.3
  17.3 0.0 copy-start.4
  17.3 0.7 copy-done.4
  18.0 8.2 %collective-permute-start = (bf16[128,128]{1,0:T(8,128)(2,1)S(1)}, bf16[128,128]{1,0:T(8,128)(2,1)S(1)}, u32[]{:S(2)}, u32[]{:S(2)}) collective-permute-start(bf16[128,128]{1,0:T(8,128)(2,1)S(1)} %shard_map.118.own_ref), channel_id=1, source_target_pairs={{0,20},{1,21},{2,22},{3,23},{4,16},{5,17},{6,18},{7,19},{16,4},{17... | collective-permute-start | bytes 98312 | tf_op jit(solution)/shard_map/ppermute | solution.py:409
  26.2 4.4 %collective-permute-done.other_ref = bf16[128,128]{1,0:T(8,128)(2,1)S(1)} collective-permute-done((bf16[128,128]{1,0:T(8,128)(2,1)S(1)}, bf16[128,128]{1,0:T(8,128)(2,1)S(1)}, u32[]{:S(2)}, u32[]{:S(2)}) %collective-permute-start) | collective-permute-done | bytes 32800 | tf_op jit(solution)/shard_map/ppermute | solution.py:409
  30.6 5.5 %all-to-all-done.arrived_ref.grad_ref = bf16[8,160,128]{2,1,0:T(8,128)(2,1)S(1)} async-done(((bf16[8,160,128]{2,1,0:T(8,128)(2,1)}), bf16[8,160,128]{2,1,0:T(8,128)(2,1)S(1)}, u32[]{:S(2)}, u32[]{:S(2)}) %all-to-all-start) | async-done | bytes 327712 | tf_op jit(solution)/shard_map/all_to_all | solution.py:51
  36.2 0.8 shard_map.120
  37.0 0.0 copy-start
  37.0 31.1 %all_to_all.20 = bf16[16,512,128]{2,1,0:T(8,128)(2,1)S(1)} all-to-all(bf16[16,512,128]{2,1,0:T(8,128)(2,1)S(1)} %shard_map.120), channel_id=1, replica_groups=mesh['y'=4,'x'=4,'zh'=2,'c'=2,'s'=8] {'y','x'}, dimensions={0} | all-to-all | bytes 4194304 | tf_op jit(solution)/shard_map/all_to_all | solution.py:51
  68.1 0.0 copy-start.5
  68.1 0.0 copy-start.6
  68.1 2.0 %collective-permute-start.1 = (bf16[8192,128]{1,0:T(8,128)(2,1)S(1)}, bf16[8192,128]{1,0:T(8,128)(2,1)S(1)}, u32[]{:S(2)}, u32[]{:S(2)}) collective-permute-start(bf16[8192,128]{1,0:T(8,128)(2,1)S(1)} %bitcast.13), channel_id=1, source_target_pairs={{0,8},{8,0},{1,9},{9,1},{2,10},{10,2},{3,11},{11,3},{4,12},{12,4},... | collective-permute-start | bytes 6291464 | tf_op jit(solution)/shard_map/ppermute | solution.py:55
  70.1 0.0 copy-done
  70.1 1.0 shard_map.121
  71.1 3.1 %collective-permute-done.1 = bf16[8192,128]{1,0:T(8,128)(2,1)S(1)} collective-permute-done((bf16[8192,128]{1,0:T(8,128)(2,1)S(1)}, bf16[8192,128]{1,0:T(8,128)(2,1)S(1)}, u32[]{:S(2)}, u32[]{:S(2)}) %collective-permute-start.1) | collective-permute-done | bytes 2097184 | tf_op jit(solution)/shard_map/ppermute | solution.py:55
  74.3 0.0 copy-done.5
  74.3 0.0 copy-done.6
  74.3 5.5 %shard_map.122 = (bf16[1024,512]{1,0:T(8,128)(2,1)S(1)}, bf16[128,512]{1,0:T(8,128)(2,1)S(1)}, bf16[16,528,128]{2,1,0:T(8,128)(2,1)S(1)}, bf16[16,528,128]{2,1,0:T(8,128)(2,1)S(1)}) custom-call(s32[4]{0:T(128)S(1)} %pad_add_fusion.place_ref, bf16[256,512]{1,0:T(8,128)(2,1)S(1)} %get-tuple-element.18.taps_ref, bf16[16,32,16,128]{3,2,1,0:T(8,128)(2,1)S(1)} %bitcast.15, ...), custom_call_target="tpu_custom_call" | custom-call | tf_op jit(solution)/shard_map/pallas_call | solution.py:61
  79.7 2.0 %collective-permute-start.2 = (bf16[8448,128]{1,0:T(8,128)(2,1)S(1)}, bf16[8448,128]{1,0:T(8,128)(2,1)S(1)}, u32[]{:S(2)}, u32[]{:S(2)}) collective-permute-start(bf16[8448,128]{1,0:T(8,128)(2,1)S(1)} %bitcast.19), channel_id=1, source_target_pairs={{0,8},{8,0},{1,9},{9,1},{2,10},{10,2},{3,11},{11,3},{4,12},{12,4},... | collective-permute-start | bytes 6488072 | tf_op jit(solution)/shard_map/ppermute | solution.py:55
  81.8 4.1 %collective-permute-done.2 = bf16[8448,128]{1,0:T(8,128)(2,1)S(1)} collective-permute-done((bf16[8448,128]{1,0:T(8,128)(2,1)S(1)}, bf16[8448,128]{1,0:T(8,128)(2,1)S(1)}, u32[]{:S(2)}, u32[]{:S(2)}) %collective-permute-start.2) | collective-permute-done | bytes 2162720 | tf_op jit(solution)/shard_map/ppermute | solution.py:55
  85.9 0.6 fusion
  86.5 32.3 %all_to_all.21.arrived_ref = bf16[16,528,128]{2,1,0:T(8,128)(2,1)S(1)} all-to-all(bf16[16,528,128]{2,1,0:T(8,128)(2,1)S(1)} %fusion), channel_id=1, replica_groups=mesh['y'=4,'x'=4,'zh'=2,'c'=2,'s'=8] {'y','x'}, dimensions={0} | all-to-all | bytes 4325376 | tf_op jit(solution)/shard_map/all_to_all | solution.py:51
  118.7 1.0 shard_map.124
  119.8 10.0 %all-to-all-start.3 = ((bf16[16,56,128]{2,1,0:T(8,128)(2,1)}), bf16[16,56,128]{2,1,0:T(8,128)(2,1)S(1)}, u32[]{:S(2)}, u32[]{:S(2)}) async-start(bf16[16,56,128]{2,1,0:T(8,128)(2,1)} %shard_map.124), calls=%async_computation.3 | async-start | bytes 458752 | tf_op jit(solution)/shard_map/all_to_all | solution.py:51
  129.8 1.4 shard_map.123
  131.2 15.3 %all-to-all-done.3.arrived_ref = bf16[16,56,128]{2,1,0:T(8,128)(2,1)S(1)} async-done(((bf16[16,56,128]{2,1,0:T(8,128)(2,1)}), bf16[16,56,128]{2,1,0:T(8,128)(2,1)S(1)}, u32[]{:S(2)}, u32[]{:S(2)}) %all-to-all-start.3) | async-done | bytes 229408 | tf_op jit(solution)/shard_map/all_to_all | solution.py:51
  146.4 0.7 shard_map.125
  (1 shorter events, 0.0 us)
Async XLA Ops:
  0.7 0.9 copy-start.1
  1.7 0.9 copy-start.2
  3.9 32.2 %all-to-all-start = ((bf16[8,160,128]{2,1,0:T(8,128)(2,1)}), bf16[8,160,128]{2,1,0:T(8,128)(2,1)S(1)}, u32[]{:S(2)}, u32[]{:S(2)}) async-start(bf16[8,160,128]{2,1,0:T(8,128)(2,1)} %shard_map.119), calls=%async_computation | async-start | bytes 655360 | tf_op jit(solution)/shard_map/all_to_all | solution.py:51
  16.6 0.7 copy-start.3
  17.3 0.7 copy-start.4
  18.0 12.6 %collective-permute-start = (bf16[128,128]{1,0:T(8,128)(2,1)S(1)}, bf16[128,128]{1,0:T(8,128)(2,1)S(1)}, u32[]{:S(2)}, u32[]{:S(2)}) collective-permute-start(bf16[128,128]{1,0:T(8,128)(2,1)S(1)} %shard_map.118.own_ref), channel_id=1, source_target_pairs={{0,20},{1,21},{2,22},{3,23},{4,16},{5,17},{6,18},{7,19},{16,4},{17... | collective-permute-start | bytes 98312 | tf_op jit(solution)/shard_map/ppermute | solution.py:409
  37.0 33.1 %copy-start = (bf16[2,128,512]{2,1,0:T(8,128)(2,1)S(1)}, bf16[2,128,512]{2,1,0:T(8,128)(2,1)}, u32[]{:S(2)}) copy-start(bf16[2,128,512]{2,1,0:T(8,128)(2,1)} %param.7) | copy-start | bytes 786436
  68.1 6.2 %copy-start.5 = (f32[3,512]{1,0:T(4,128)S(1)}, f32[3,512]{1,0:T(4,128)}, u32[]{:S(2)}) copy-start(f32[3,512]{1,0:T(4,128)} %gains_ref.1) | copy-start | bytes 18436
  68.1 6.2 %copy-start.6 = (f32[3,512]{1,0:T(4,128)S(1)}, f32[3,512]{1,0:T(4,128)}, u32[]{:S(2)}) copy-start(f32[3,512]{1,0:T(4,128)} %biases_ref.1) | copy-start | bytes 18436
  68.1 6.2 %collective-permute-start.1 = (bf16[8192,128]{1,0:T(8,128)(2,1)S(1)}, bf16[8192,128]{1,0:T(8,128)(2,1)S(1)}, u32[]{:S(2)}, u32[]{:S(2)}) collective-permute-start(bf16[8192,128]{1,0:T(8,128)(2,1)S(1)} %bitcast.13), channel_id=1, source_target_pairs={{0,8},{8,0},{1,9},{9,1},{2,10},{10,2},{3,11},{11,3},{4,12},{12,4},... | collective-permute-start | bytes 6291464 | tf_op jit(solution)/shard_map/ppermute | solution.py:55
  79.7 6.1 %collective-permute-start.2 = (bf16[8448,128]{1,0:T(8,128)(2,1)S(1)}, bf16[8448,128]{1,0:T(8,128)(2,1)S(1)}, u32[]{:S(2)}, u32[]{:S(2)}) collective-permute-start(bf16[8448,128]{1,0:T(8,128)(2,1)S(1)} %bitcast.19), channel_id=1, source_target_pairs={{0,8},{8,0},{1,9},{9,1},{2,10},{10,2},{3,11},{11,3},{4,12},{12,4},... | collective-permute-start | bytes 6488072 | tf_op jit(solution)/shard_map/ppermute | solution.py:55
  119.8 26.7 %all-to-all-start.3 = ((bf16[16,56,128]{2,1,0:T(8,128)(2,1)}), bf16[16,56,128]{2,1,0:T(8,128)(2,1)S(1)}, u32[]{:S(2)}, u32[]{:S(2)}) async-start(bf16[16,56,128]{2,1,0:T(8,128)(2,1)} %shard_map.124), calls=%async_computation.3 | async-start | bytes 458752 | tf_op jit(solution)/shard_map/all_to_all | solution.py:51

commit v5 on v4

--- a/solution.py
+++ b/solution.py
@@ -1,3 +1,5 @@
+import functools
+
 import jax
 import jax.numpy as jnp
 from jax import lax
@@ -80,34 +82,31 @@
     sections = out_ref.shape[0]
     utterances = grad_ref.shape[0] // sections
     width = grad_ref.shape[2]
-    proj_at = (width // LANES + 1) // 2 * TILE
     for section in range(sections):
+        for k in range(2):
+            out_ref[section, k * TILE : (k + 1) * TILE] = proj_ref[:, k * LANES : (k + 1) * LANES]
         part = jnp.concatenate(
             [grad_ref[section * utterances + k].astype(wide) for k in range(utterances)], axis=0
         )
-        part = jnp.concatenate([part, jnp.zeros((part.shape[0], LANES), wide)], axis=1)
-        for tile in range(proj_at // TILE):
-            lane = 2 * tile * LANES
-            stacked = jnp.concatenate(
-                [part[:, lane : lane + LANES], part[:, lane + LANES : lane + 2 * LANES]], axis=0
-            )
-            out_ref[section, tile * TILE : (tile + 1) * TILE] = stacked.astype(narrow)
-        for k in range(2):
-            out_ref[section, proj_at + k * TILE : proj_at + (k + 1) * TILE] = proj_ref[
-                :, k * LANES : (k + 1) * LANES
+        for lane in range(0, width, 2 * LANES):
+            pieces = [
+                part[:, at : at + LANES] for at in range(lane, min(width, lane + 2 * LANES), LANES)
             ]
+            start = 2 * TILE + lane // LANES * (TILE // 2)
+            out_ref[section, start : start + len(pieces) * (TILE // 2)] = jnp.concatenate(
+                pieces, axis=0
+            ).astype(narrow)
 
 
 def bundle_kernel(place_ref, own_ref, other_ref, arrived_ref, out_ref):
     half = place_ref[1]
     rows = own_ref.shape[0]
-    start = arrived_ref.shape[1] - 2 * TILE
     for plane in range(out_ref.shape[0]):
         out_ref[plane, pl.ds(pl.multiple_of(half * rows, TILE), rows)] = own_ref[...]
         out_ref[plane, pl.ds(pl.multiple_of((1 - half) * rows, TILE), rows)] = other_ref[...]
         for section in range(arrived_ref.shape[0]):
             at = 2 * rows + section * 2 * TILE
-            out_ref[plane, at : at + 2 * TILE] = arrived_ref[section, start:]
+            out_ref[plane, at : at + 2 * TILE] = arrived_ref[section, : 2 * TILE]
 
 
 def position_order(frames):
@@ -134,10 +133,11 @@
     lax.fori_loop(0, row_tiles, step, 0)
 
 
-def early_kernel(input_ref, own_ref, grad_ref, taps_ref, cotangent_ref, part_ref, proj_ref, rows_ref):
+def early_kernel(input_ref, own_ref, grad_ref, shared_ref, part_ref, proj_ref, rows_ref):
     frames, width = rows_ref.shape
     sections = grad_ref.shape[0]
-    taps_ref[...] = matmul(position_order(frames), input_ref[...]).astype(narrow)
+    channels = input_ref.shape[1]
+    shared_ref[:, :channels] = matmul(position_order(frames), input_ref[...]).astype(narrow)
 
     run = frames // (2 * sections)
 
@@ -149,41 +149,50 @@
     eight = frames // sections
     for section in range(sections):
         for lane in range(width // LANES):
+            start = 2 * TILE + lane * eight
             if lane % 2 == 0:
-                stacked = grad_ref[section, lane // 2 * TILE : (lane // 2 + 1) * TILE].astype(wide)
+                count = min(2, width // LANES - lane)
+                stacked = grad_ref[section, start : start + count * eight].astype(wide)
             rows_ref[
                 section * eight : (section + 1) * eight, lane * LANES : (lane + 1) * LANES
             ] = stacked[(lane % 2) * eight : (lane % 2 + 1) * eight]
     grad_rows = matmul(
         one_hot((frames, frames), arrived_row), rows_ref[...].astype(narrow)
     ).astype(narrow)
-    cotangent_ref[...] = grad_rows
+    for k in range(4):
+        lanes = min(channels, width - k * channels)
+        shared_ref[k * frames : (k + 1) * frames, channels : channels + lanes] = grad_rows[
+            :, k * channels : k * channels + lanes
+        ]
+    shared_ref[3 * frames :, channels + lanes :] = jnp.zeros((frames, channels - lanes), narrow)
     place_proj(own_ref, proj_ref, width // sections // TILE, width // sections)
     part_ref[...] = matmul(grad_rows, proj_ref[...])
 
 
+def cotangents_of(shared_ref, width):
+    frames, channels = shared_ref.shape[0] // 4, shared_ref.shape[1] // 2
+    rows = jnp.concatenate(
+        [shared_ref[k * frames : (k + 1) * frames, channels:] for k in range(4)], axis=1
+    )
+    return rows[:, :width]
+
+
 def layer_kernel(
+    width,
     place_ref,
-    taps_ref,
+    shared_ref,
     own_ref,
     other_ref,
-    cotangent_ref,
     part_ref,
     gains_ref,
     biases_ref,
     six_ref,
-    dhid_ref,
-    kept_ref,
-    given_ref,
+    late_ref,
     seven_ref,
     proj_ref,
-    term_six_ref,
-    term_seven_ref,
-    term_proj_ref,
 ):
     core = place_ref[2]
-    channels = taps_ref.shape[1]
-    frames, width = cotangent_ref.shape
+    frames, channels = part_ref.shape[0], shared_ref.shape[1] // 2
     lane_tiles = channels // LANES
     planes = own_ref.shape[0]
     sections = (own_ref.shape[1] - 4 * lane_tiles) // 2
@@ -205,7 +214,7 @@
     lax.fori_loop(0, planes, place_tiles, 0)
 
     place_proj(other_ref, proj_ref, section_rows // TILE, section_rows)
-    tap_zero, tap_one = taps_ref[: 2 * frames], taps_ref[2 * frames :]
+    tap_zero, tap_one = shared_ref[: 2 * frames, :channels], shared_ref[2 * frames :, :channels]
     hid_six = matmul(tap_zero, six_ref[:channels]) + matmul(tap_one, six_ref[channels:])
     pre_six, part_six, scale_six = norm_forward(hid_six, gains_ref[0:1], biases_ref[0:1])
     act_six_f, deriv_six = gelu_parts(pre_six)
@@ -221,8 +230,7 @@
     )
     normed = pre_feat.astype(narrow)
 
-    grad_rows = cotangent_ref[...]
-    term_proj_ref[...] = matmul(normed, grad_rows, (0, 0))
+    grad_rows = cotangents_of(shared_ref, width)
     own_half, other_half = part_ref[...], matmul(grad_rows, proj_ref[...])
     first = core == 0
     grad_normed = jnp.concatenate(
@@ -231,8 +239,6 @@
     dact_seven = norm_backward(grad_normed, part_feat, scale_feat, gains_ref[2:3])
     dpre_seven = dact_seven * deriv_seven
     dhid_seven = norm_backward(dpre_seven, part_seven, scale_seven, gains_ref[1:2]).astype(narrow)
-    term_seven_ref[:channels] = matmul(act_zero, dhid_seven, (0, 0))
-    term_seven_ref[channels:] = matmul(act_one, dhid_seven, (0, 0))
     dact_six = jnp.concatenate(
         [
             matmul(dhid_seven, seven_ref[:channels], (1, 1)),
@@ -242,34 +248,6 @@
     )
     dpre_six = dact_six * deriv_six
     dhid_six = norm_backward(dpre_six, part_six, scale_six, gains_ref[0:1]).astype(narrow)
-    dhid_ref[...] = dhid_six
-    term_six_ref[:channels] = matmul(tap_zero, dhid_six, (0, 0))
-    term_six_ref[channels:] = matmul(tap_one, dhid_six, (0, 0))
-    half_rows = TILE // 2
-
-    def pack(plane, carry):
-        for target, index in ((kept_ref, core), (given_ref, 1 - core)):
-            proj_rows = []
-            for half in range(2):
-                group = (plane * 2 + half) * 2 + index
-                rows = pl.ds(pl.multiple_of(group * TILE, TILE), TILE)
-                for lane in range(lane_tiles):
-                    lanes = slice(lane * LANES, (lane + 1) * LANES)
-                    at = (half * lane_tiles + lane) * TILE
-                    target[plane, at : at + TILE] = term_six_ref[rows, lanes].astype(narrow)
-                    at += 2 * lane_tiles * TILE
-                    target[plane, at : at + TILE] = term_seven_ref[rows, lanes].astype(narrow)
-                proj_rows.append(
-                    term_proj_ref[pl.ds(pl.multiple_of(group * half_rows, half_rows), half_rows)]
-                )
-            proj_block = jnp.concatenate(proj_rows, axis=0).astype(narrow)
-            for lane in range(width // LANES):
-                at = (4 * lane_tiles + lane) * TILE
-                target[plane, at : at + TILE] = proj_block[:, lane * LANES : (lane + 1) * LANES]
-        return carry
-
-    lax.fori_loop(0, planes, pack, 0)
-
     def total(value):
         return jnp.sum(value, axis=0, keepdims=True)
 
@@ -284,23 +262,86 @@
         ],
         axis=0,
     )
+    late_ref[: 2 * frames] = dhid_six
+    late_ref[2 * frames : 4 * frames] = act_six
+    late_ref[4 * frames : 5 * frames] = dhid_seven
+    late_ref[5 * frames : 6 * frames] = normed
+    late_ref[6 * frames :] = jnp.concatenate(
+        [sums, jnp.zeros((TILE - sums.shape[0], channels), wide)], axis=0
+    ).astype(narrow)
+
+
+def terms_kernel(
+    width,
+    place_ref,
+    shared_ref,
+    shared_other_ref,
+    late_ref,
+    late_other_ref,
+    send_ref,
+    term_six_ref,
+    term_seven_ref,
+    term_proj_ref,
+):
+    core = place_ref[2]
+    frames, channels = shared_ref.shape[0] // 4, late_ref.shape[1]
+    lane_tiles = channels // LANES
+    planes = send_ref.shape[0]
+
+    def both(start, stop, left=shared_ref, right=shared_other_ref):
+        rows = slice(start * frames, stop * frames)
+        return jnp.concatenate([left[rows, :channels], right[rows, :channels]], axis=0)
+
+    def late(start, stop):
+        return both(start, stop, late_ref, late_other_ref)
+
+    dhid_six, dhid_seven, normed = late(0, 2), late(4, 5), late(5, 6)
+    term_six_ref[:channels] = matmul(both(0, 2), dhid_six, (0, 0))
+    term_six_ref[channels:] = matmul(both(2, 4), dhid_six, (0, 0))
+    term_seven_ref[:channels] = matmul(late(2, 3), dhid_seven, (0, 0))
+    term_seven_ref[channels:] = matmul(late(3, 4), dhid_seven, (0, 0))
+    grad_rows = jnp.concatenate(
+        [cotangents_of(shared_ref, width), cotangents_of(shared_other_ref, width)], axis=0
+    )
+    term_proj_ref[...] = matmul(normed, grad_rows, (0, 0))
+    half_rows = TILE // 2
+
+    def pack(plane, carry):
+        proj_rows = []
+        for half in range(2):
+            group = (plane * 2 + half) * 2 + core
+            rows = pl.ds(pl.multiple_of(group * TILE, TILE), TILE)
+            for lane in range(lane_tiles):
+                lanes = slice(lane * LANES, (lane + 1) * LANES)
+                at = (half * lane_tiles + lane) * TILE
+                send_ref[plane, at : at + TILE] = term_six_ref[rows, lanes].astype(narrow)
+                at += 2 * lane_tiles * TILE
+                send_ref[plane, at : at + TILE] = term_seven_ref[rows, lanes].astype(narrow)
+            proj_rows.append(
+                term_proj_ref[pl.ds(pl.multiple_of(group * half_rows, half_rows), half_rows)]
+            )
+        proj_block = jnp.concatenate(proj_rows, axis=0).astype(narrow)
+        for lane in range(width // LANES):
+            at = (4 * lane_tiles + lane) * TILE
+            send_ref[plane, at : at + TILE] = proj_block[:, lane * LANES : (lane + 1) * LANES]
+        return carry
+
+    lax.fori_loop(0, planes, pack, 0)
+    sums = (late_ref[6 * frames :].astype(wide) + late_other_ref[6 * frames :].astype(wide))[:6]
     sums = jnp.concatenate(
-        [sums[:, lane * LANES : (lane + 1) * LANES] for lane in range(lane_tiles)]
-        + [jnp.zeros((TILE // 2, LANES), wide)],
-        axis=0,
+        [sums[:, lane * LANES : (lane + 1) * LANES] for lane in range(lane_tiles)], axis=0
     ).astype(narrow)
     at = (4 * lane_tiles + width // LANES) * TILE
-    spread_sums = jnp.broadcast_to(sums[None], (planes,) + sums.shape)
-    kept_ref[:, at:] = spread_sums
-    given_ref[:, at:] = spread_sums
-
-
-def input_kernel(dhid_ref, six_ref, back_ref):
+    send_ref[:, at:] = jnp.broadcast_to(sums[None], (planes,) + sums.shape)
+
+
+def input_kernel(late_ref, six_ref, back_ref):
     channels = back_ref.shape[1]
+    dhid_six = late_ref[: back_ref.shape[0] // 2]
     back = jnp.concatenate(
         [
-            matmul(dhid_ref[...], six_ref[:channels], (1, 1)).astype(narrow),
-            matmul(dhid_ref[...], six_ref[channels:], (1, 1)).astype(narrow),
+            matmul(dhid_six, six_ref[:channels], (1, 1)).astype(narrow),
+            matmul(dhid_six, six_ref[channels:], (1, 1)).astype(narrow),
         ],
         axis=0,
     )
@@ -315,7 +356,8 @@
     total_ref[...] = running
     sections = out_ref.shape[0] // 2
     lane_tiles = sections // 2
-    proj_tiles = rows // TILE - 4 * lane_tiles - 2
+    sum_rows = 6 * lane_tiles
+    proj_tiles = (rows - sum_rows) // TILE - 4 * lane_tiles
     left = lax.broadcasted_iota(jnp.int32, (TILE, LANES), 1) < LANES // 2
     for half in range(2):
         for lane in range(lane_tiles):
@@ -345,7 +387,7 @@
             out_ref[half * sections + section, TILE : 2 * TILE] = jnp.concatenate(
                 [moved[rows_of, :LANES], moved[rows_of, LANES : 2 * LANES]], axis=0
             ).astype(narrow)
-    sums = total_ref[rows - 2 * TILE : rows - TILE // 2].astype(narrow)
+    sums = total_ref[rows - sum_rows :].astype(narrow)
     out_ref[:, 2 * TILE :] = jnp.broadcast_to(sums[None], (2 * sections,) + sums.shape)
 
 
@@ -380,11 +422,11 @@
         [lax.axis_index(("y", "x")), lax.axis_index("zh"), lax.axis_index("c"), lax.axis_index("s")]
     ).astype(jnp.int32)
 
-    tile_rows = 2 * (channels // LANES) * TILE
-    grad_tiles = (width // LANES + 1) // 2
+    lane_tiles = channels // LANES
+    tile_rows = 2 * lane_tiles * TILE
     convs = on_core(conv_kernel, shape((tile_rows, LANES), narrow), [], [conv_six, conv_seven])
     row_tiles = part_width // TILE
-    out_block = (sections, (grad_tiles + 2) * TILE, LANES)
+    out_block = (sections, 2 * TILE + width // LANES * (TILE // 2), LANES)
     outgoing = pl.pallas_call(
         pick_kernel,
         out_shape=shape(out_block, narrow),
@@ -418,32 +460,25 @@
     sibling = swap(gathered.reshape(-1, LANES), "c")
 
     tiles_shape = (planes, bundle.shape[1] // TILE, TILE, LANES)
-    send_rows = (4 * (channels // LANES) + width // LANES + 2) * TILE
-    taps, cotangents, part = on_core(
+    shared, part = on_core(
         early_kernel,
-        [
-            shape((4 * frames, channels), narrow),
-            shape((frames, width), narrow),
-            shape((frames, 2 * LANES), wide),
-        ],
+        [shape((4 * frames, 2 * channels), narrow), shape((frames, 2 * LANES), wide)],
         [],
         [layer_five.reshape(4 * frames, channels), gathered.reshape(tiles_shape), arrived],
         scratch=[pltpu.VMEM((width, 2 * LANES), narrow), pltpu.VMEM((frames, width), wide)],
     )
-    six_full, dhid_six, kept, given = on_core(
-        layer_kernel,
+    shared_other = swap(shared, "c")
+    six_full, late = on_core(
+        functools.partial(layer_kernel, width),
         [
             shape((2 * channels, channels), narrow),
-            shape((2 * frames, channels), narrow),
-            shape((planes, send_rows, LANES), narrow),
-            shape((planes, send_rows, LANES), narrow),
+            shape((6 * frames + TILE, channels), narrow),
         ],
         [place],
         [
-            taps,
+            shared,
             gathered.reshape(tiles_shape),
             sibling.reshape(tiles_shape),
-            cotangents,
             part,
             gains,
             biases,
@@ -451,17 +486,24 @@
         scratch=[
             pltpu.VMEM((2 * channels, channels), narrow),
             pltpu.VMEM((width, 2 * LANES), narrow),
+        ],
+        megabytes=16,
+    )
+    late_other = swap(late, "c")
+    back = on_core(input_kernel, shape((4 * frames, channels), narrow), [], [late, six_full])
+    send_rows = (4 * lane_tiles + width // LANES) * TILE + 6 * lane_tiles
+    chip = on_core(
+        functools.partial(terms_kernel, width),
+        shape((planes, send_rows, LANES), narrow),
+        [place],
+        [shared, shared_other, late, late_other],
+        scratch=[
             pltpu.VMEM((2 * channels, channels), wide),
             pltpu.VMEM((2 * channels, channels), wide),
             pltpu.VMEM((channels, width), wide),
         ],
-        megabytes=36,
-    )
-    back = on_core(
-        input_kernel, shape((4 * frames, channels), narrow), [], [dhid_six, six_full]
-    )
-    received = swap(given.reshape(-1, LANES), "c").reshape(given.shape)
-    chip = (kept.astype(wide) + received.astype(wide)).astype(narrow)
+        megabytes=24,
+    )
     plane_in = exchange(chip, ("y", "x"))
     line_out = on_core(
         plane_kernel,

time: 148 us -> 144 us (0.973)
  waiting for transfers between devices: 32.5 us -> 26.9 us
  starting transfers between devices: 35 us -> 37.7 us
    ppermute x2 -> x3, waiting for transfers between devices: 7.25 us -> 2.31 us  [swap(): return lax.ppermute(value, axis, [(0, 1), (1, 0)])]
    ppermute x2 -> x3, starting transfers between devices: 4.08 us -> 6.49 us  [swap(): return lax.ppermute(value, axis, [(0, 1), (1, 0)])]
    pallas_call x7 -> x8, Pallas kernels: 10.4 us -> 10.2 us  [on_core(): pl.pallas_call(kernel, out_shape=out_shape, in_specs=[pl.BlockSpec(memory...]
  transfers between devices with their start and end apart: 5 -> 6, of which waited for: 5 -> 5; matrix products, arithmetic and copies ran while one was open for 0% -> 0% of each run, Pallas kernels for 2% -> 4%
where the time goes in v5:
time: 144 us; the launch traced here: 143 us
  blocking collectives  62.9 us (44%)
  starting transfers between devices  37.7 us (26%)
  waiting for transfers between devices  26.9 us (19%)
  Pallas kernels  11.6 us (8%)
  local copies, waits for them, and re-layouts  3.34 us (2%)
    all_to_all x2, blocking collectives, exchange(): return lax.all_to_all(value, axes, 0, 0, tiled=True)  62.9 us
    all_to_all x2, starting transfers between devices, exchange(): return lax.all_to_all(value, axes, 0, 0, tiled=True)  23 us
    all_to_all x2, waiting for transfers between devices, exchange(): return lax.all_to_all(value, axes, 0, 0, tiled=True)  20.5 us
    pallas_call x8, Pallas kernels, on_core(): pl.pallas_call(kernel, out_shape=out_shape, in_specs=[pl.BlockSpec(memory...  10.2 us
    ppermute x1, starting transfers between devices, on_device(): other_convs = lax.ppermute(convs, ('zh', 's'), opposite)  8.21 us
    ppermute x3, starting transfers between devices, swap(): return lax.ppermute(value, axis, [(0, 1), (1, 0)])  6.49 us
    ppermute x1, waiting for transfers between devices, on_device(): other_convs = lax.ppermute(convs, ('zh', 's'), opposite)  4.08 us
    unnamed x14, local copies, waits for them, and re-layouts  3.34 us
  transfers between devices with their start and end apart: 6, of which 5 were waited for; matrix products, arithmetic and copies ran while one was open for 0% of the time, Pallas kernels for 4%

profile of v5, /device:TPU:32, one launch (start us, length us, event | category | flops | bytes accessed | tf_op | source)
XLA Modules:
  0.0 143.2 jit_solution(9756353147298008182)
XLA Ops:
  0.6 0.1 pad_add_fusion.place_ref
  0.7 0.0 copy-start.1
  0.7 0.9 copy-done.1
  1.7 0.0 copy-start.2
  1.7 0.9 copy-done.2
  2.6 1.3 shard_map.119
  3.9 12.6 %all-to-all-start = ((bf16[8,152,128]{2,1,0:T(8,128)(2,1)}), bf16[8,152,128]{2,1,0:T(8,128)(2,1)S(1)}, u32[]{:S(2)}, u32[]{:S(2)}) async-start(bf16[8,152,128]{2,1,0:T(8,128)(2,1)} %shard_map.119), calls=%async_computation | async-start | bytes 622592 | tf_op jit(solution)/shard_map/all_to_all | solution.py:53
  16.6 0.0 copy-start.3
  16.6 0.7 copy-done.3
  17.3 0.0 copy-start.4
  17.3 0.7 copy-done.4
  18.0 8.2 %collective-permute-start = (bf16[128,128]{1,0:T(8,128)(2,1)S(1)}, bf16[128,128]{1,0:T(8,128)(2,1)S(1)}, u32[]{:S(2)}, u32[]{:S(2)}) collective-permute-start(bf16[128,128]{1,0:T(8,128)(2,1)S(1)} %shard_map.118.own_ref), channel_id=1, source_target_pairs={{0,20},{1,21},{2,22},{3,23},{4,16},{5,17},{6,18},{7,19},{16,4},{17... | collective-permute-start | bytes 98312 | tf_op jit(solution)/shard_map/ppermute | solution.py:451
  26.2 4.1 %collective-permute-done.other_ref = bf16[128,128]{1,0:T(8,128)(2,1)S(1)} collective-permute-done((bf16[128,128]{1,0:T(8,128)(2,1)S(1)}, bf16[128,128]{1,0:T(8,128)(2,1)S(1)}, u32[]{:S(2)}, u32[]{:S(2)}) %collective-permute-start) | collective-permute-done | bytes 32800 | tf_op jit(solution)/shard_map/ppermute | solution.py:451
  30.3 5.2 %all-to-all-done.arrived_ref.grad_ref = bf16[8,152,128]{2,1,0:T(8,128)(2,1)S(1)} async-done(((bf16[8,152,128]{2,1,0:T(8,128)(2,1)}), bf16[8,152,128]{2,1,0:T(8,128)(2,1)S(1)}, u32[]{:S(2)}, u32[]{:S(2)}) %all-to-all-start) | async-done | bytes 311328 | tf_op jit(solution)/shard_map/all_to_all | solution.py:53
  35.5 0.8 shard_map.120
  36.4 0.0 copy-start
  36.4 30.9 %all_to_all.20 = bf16[16,512,128]{2,1,0:T(8,128)(2,1)S(1)} all-to-all(bf16[16,512,128]{2,1,0:T(8,128)(2,1)S(1)} %shard_map.120), channel_id=1, replica_groups=mesh['y'=4,'x'=4,'zh'=2,'c'=2,'s'=8] {'y','x'}, dimensions={0} | all-to-all | bytes 4194304 | tf_op jit(solution)/shard_map/all_to_all | solution.py:53
  67.2 0.0 copy-start.5
  67.2 0.0 copy-start.6
  67.2 2.0 %collective-permute-start.1 = (bf16[8192,128]{1,0:T(8,128)(2,1)S(1)}, bf16[8192,128]{1,0:T(8,128)(2,1)S(1)}, u32[]{:S(2)}, u32[]{:S(2)}) collective-permute-start(bf16[8192,128]{1,0:T(8,128)(2,1)S(1)} %bitcast.10), channel_id=1, source_target_pairs={{0,8},{8,0},{1,9},{9,1},{2,10},{10,2},{3,11},{11,3},{4,12},{12,4},... | collective-permute-start | bytes 6291464 | tf_op jit(solution)/shard_map/ppermute | solution.py:57
  69.3 0.0 copy-done
  69.3 1.0 shard_map.121
  70.2 2.4 %collective-permute-start.2 = (bf16[256,1024]{1,0:T(8,128)(2,1)S(1)}, bf16[256,1024]{1,0:T(8,128)(2,1)S(1)}, u32[]{:S(2)}, u32[]{:S(2)}) collective-permute-start(bf16[256,1024]{1,0:T(8,128)(2,1)S(1)} %get-tuple-element.15.shared_ref), channel_id=1, source_target_pairs={{0,8},{8,0},{1,9},{9,1},{2,10},{10,2},{3,11},{11,3},{4,12},{12,4},... | collective-permute-start | bytes 1572872 | tf_op jit(solution)/shard_map/ppermute | solution.py:57
  72.7 0.7 collective-permute-done.1
  73.4 0.0 copy-done.5
  73.4 0.0 copy-done.6
  73.4 3.2 %shard_map.122 = (bf16[1024,512]{1,0:T(8,128)(2,1)S(1)}, bf16[400,512]{1,0:T(8,128)(2,1)S(1)}) custom-call(s32[4]{0:T(128)S(1)} %pad_add_fusion.place_ref, bf16[256,1024]{1,0:T(8,128)(2,1)S(1)} %get-tuple-element.15.shared_ref, bf16[16,32,16,128]{3,2,1,0:T(8,128)(2,1)S(1)} %bitcast.12, bf16[16,32,16,128]{3,2,1,0:T(8,128)(2,1)S(1)} %bitcast.13, ...), custom_call_target="tpu_custom_call" | custom-call | tf_op jit(solution)/shard_map/pallas_call | solution.py:63
  76.6 2.0 %collective-permute-start.3 = (bf16[400,512]{1,0:T(8,128)(2,1)S(1)}, bf16[400,512]{1,0:T(8,128)(2,1)S(1)}, u32[]{:S(2)}, u32[]{:S(2)}) collective-permute-start(bf16[400,512]{1,0:T(8,128)(2,1)S(1)} %get-tuple-element.17.late_ref), channel_id=1, source_target_pairs={{0,8},{8,0},{1,9},{9,1},{2,10},{10,2},{3,11},{11,3},{4,12},{12,4},... | collective-permute-start | bytes 1228808 | tf_op jit(solution)/shard_map/ppermute | solution.py:57
  78.7 0.0 collective-permute-done.2.shared_other_ref
  78.7 1.6 %collective-permute-done.3.late_other_ref = bf16[400,512]{1,0:T(8,128)(2,1)S(1)} collective-permute-done((bf16[400,512]{1,0:T(8,128)(2,1)S(1)}, bf16[400,512]{1,0:T(8,128)(2,1)S(1)}, u32[]{:S(2)}, u32[]{:S(2)}) %collective-permute-start.3) | collective-permute-done | bytes 409632 | tf_op jit(solution)/shard_map/ppermute | solution.py:57
  80.3 2.1 %shard_map.124 = bf16[16,520,128]{2,1,0:T(8,128)(2,1)S(1)} custom-call(s32[4]{0:T(128)S(1)} %pad_add_fusion.place_ref, bf16[256,1024]{1,0:T(8,128)(2,1)S(1)} %get-tuple-element.15.shared_ref, bf16[256,1024]{1,0:T(8,128)(2,1)S(1)} %collective-permute-done.2.shared_other_ref, bf16[400,512]{1,0:T(8,128)(2,1)S(1)} %get-tuple-element.17.late_ref, ...), custom_call_target="tpu_custom_call" | custom-call | tf_op jit(solution)/shard_map/pallas_call | solution.py:63
  82.4 32.1 %all_to_all.21.arrived_ref = bf16[16,520,128]{2,1,0:T(8,128)(2,1)S(1)} all-to-all(bf16[16,520,128]{2,1,0:T(8,128)(2,1)S(1)} %shard_map.124), channel_id=1, replica_groups=mesh['y'=4,'x'=4,'zh'=2,'c'=2,'s'=8] {'y','x'}, dimensions={0} | all-to-all | bytes 4259840 | tf_op jit(solution)/shard_map/all_to_all | solution.py:53
  114.5 1.0 shard_map.125
  115.5 10.3 %all-to-all-start.3 = ((bf16[16,56,128]{2,1,0:T(8,128)(2,1)}), bf16[16,56,128]{2,1,0:T(8,128)(2,1)S(1)}, u32[]{:S(2)}, u32[]{:S(2)}) async-start(bf16[16,56,128]{2,1,0:T(8,128)(2,1)} %shard_map.125), calls=%async_computation.3 | async-start | bytes 458752 | tf_op jit(solution)/shard_map/all_to_all | solution.py:53
  125.8 1.4 shard_map.123
  127.2 15.3 %all-to-all-done.3.arrived_ref = bf16[16,56,128]{2,1,0:T(8,128)(2,1)S(1)} async-done(((bf16[16,56,128]{2,1,0:T(8,128)(2,1)}), bf16[16,56,128]{2,1,0:T(8,128)(2,1)S(1)}, u32[]{:S(2)}, u32[]{:S(2)}) %all-to-all-start.3) | async-done | bytes 229408 | tf_op jit(solution)/shard_map/all_to_all | solution.py:53
  142.5 0.7 shard_map.126
  (1 shorter events, 0.0 us)
Async XLA Ops:
  0.7 0.9 copy-start.1
  1.7 0.9 copy-start.2
  3.9 31.6 %all-to-all-start = ((bf16[8,152,128]{2,1,0:T(8,128)(2,1)}), bf16[8,152,128]{2,1,0:T(8,128)(2,1)S(1)}, u32[]{:S(2)}, u32[]{:S(2)}) async-start(bf16[8,152,128]{2,1,0:T(8,128)(2,1)} %shard_map.119), calls=%async_computation | async-start | bytes 622592 | tf_op jit(solution)/shard_map/all_to_all | solution.py:53
  16.6 0.7 copy-start.3
  17.3 0.7 copy-start.4
  18.0 12.3 %collective-permute-start = (bf16[128,128]{1,0:T(8,128)(2,1)S(1)}, bf16[128,128]{1,0:T(8,128)(2,1)S(1)}, u32[]{:S(2)}, u32[]{:S(2)}) collective-permute-start(bf16[128,128]{1,0:T(8,128)(2,1)S(1)} %shard_map.118.own_ref), channel_id=1, source_target_pairs={{0,20},{1,21},{2,22},{3,23},{4,16},{5,17},{6,18},{7,19},{16,4},{17... | collective-permute-start | bytes 98312 | tf_op jit(solution)/shard_map/ppermute | solution.py:451
  36.4 32.9 %copy-start = (bf16[2,128,512]{2,1,0:T(8,128)(2,1)S(1)}, bf16[2,128,512]{2,1,0:T(8,128)(2,1)}, u32[]{:S(2)}) copy-start(bf16[2,128,512]{2,1,0:T(8,128)(2,1)} %param.7) | copy-start | bytes 786436
  67.2 6.2 %copy-start.5 = (f32[3,512]{1,0:T(4,128)S(1)}, f32[3,512]{1,0:T(4,128)}, u32[]{:S(2)}) copy-start(f32[3,512]{1,0:T(4,128)} %gains_ref.1) | copy-start | bytes 18436
  67.2 6.2 %copy-start.6 = (f32[3,512]{1,0:T(4,128)S(1)}, f32[3,512]{1,0:T(4,128)}, u32[]{:S(2)}) copy-start(f32[3,512]{1,0:T(4,128)} %biases_ref.1) | copy-start | bytes 18436
  67.2 6.2 %collective-permute-start.1 = (bf16[8192,128]{1,0:T(8,128)(2,1)S(1)}, bf16[8192,128]{1,0:T(8,128)(2,1)S(1)}, u32[]{:S(2)}, u32[]{:S(2)}) collective-permute-start(bf16[8192,128]{1,0:T(8,128)(2,1)S(1)} %bitcast.10), channel_id=1, source_target_pairs={{0,8},{8,0},{1,9},{9,1},{2,10},{10,2},{3,11},{11,3},{4,12},{12,4},... | collective-permute-start | bytes 6291464 | tf_op jit(solution)/shard_map/ppermute | solution.py:57
  70.2 8.5 %collective-permute-start.2 = (bf16[256,1024]{1,0:T(8,128)(2,1)S(1)}, bf16[256,1024]{1,0:T(8,128)(2,1)S(1)}, u32[]{:S(2)}, u32[]{:S(2)}) collective-permute-start(bf16[256,1024]{1,0:T(8,128)(2,1)S(1)} %get-tuple-element.15.shared_ref), channel_id=1, source_target_pairs={{0,8},{8,0},{1,9},{9,1},{2,10},{10,2},{3,11},{11,3},{4,12},{12,4},... | collective-permute-start | bytes 1572872 | tf_op jit(solution)/shard_map/ppermute | solution.py:57
  76.6 3.6 %collective-permute-start.3 = (bf16[400,512]{1,0:T(8,128)(2,1)S(1)}, bf16[400,512]{1,0:T(8,128)(2,1)S(1)}, u32[]{:S(2)}, u32[]{:S(2)}) collective-permute-start(bf16[400,512]{1,0:T(8,128)(2,1)S(1)} %get-tuple-element.17.late_ref), channel_id=1, source_target_pairs={{0,8},{8,0},{1,9},{9,1},{2,10},{10,2},{3,11},{11,3},{4,12},{12,4},... | collective-permute-start | bytes 1228808 | tf_op jit(solution)/shard_map/ppermute | solution.py:57
  115.5 27.0 %all-to-all-start.3 = ((bf16[16,56,128]{2,1,0:T(8,128)(2,1)}), bf16[16,56,128]{2,1,0:T(8,128)(2,1)S(1)}, u32[]{:S(2)}, u32[]{:S(2)}) async-start(bf16[16,56,128]{2,1,0:T(8,128)(2,1)} %shard_map.125), calls=%async_computation.3 | async-start | bytes 458752 | tf_op jit(solution)/shard_map/all_to_all | solution.py:53

commit v6 on v5

--- a/solution.py
+++ b/solution.py
@@ -78,7 +78,18 @@
             conv_ref[at : at + TILE] = source[:, lane * LANES : (lane + 1) * LANES]
 
 
-def pick_kernel(place_ref, proj_ref, grad_ref, out_ref):
+def pick_kernel(place_ref, proj_hbm, grad_hbm, out_ref, proj_ref, grad_ref, done):
+    plane, core = place_ref[0], place_ref[2]
+    row = pl.multiple_of(jnp.minimum(plane, proj_hbm.shape[0] // TILE - 1) * TILE, TILE)
+    lane = pl.multiple_of(core * 2 * LANES, LANES)
+    grad_copy = pltpu.make_async_copy(grad_hbm, grad_ref, done.at[0])
+    proj_copy = pltpu.make_async_copy(
+        proj_hbm.at[pl.ds(row, TILE), pl.ds(lane, 2 * LANES)], proj_ref, done.at[1]
+    )
+    grad_copy.start()
+    proj_copy.start()
+    grad_copy.wait()
+    proj_copy.wait()
     sections = out_ref.shape[0]
     utterances = grad_ref.shape[0] // sections
     width = grad_ref.shape[2]
@@ -350,10 +361,12 @@
 
 def plane_kernel(arrived_ref, out_ref, total_ref):
     planes, rows = arrived_ref.shape[0], arrived_ref.shape[1]
-    running = arrived_ref[0].astype(wide)
-    for plane in range(1, planes):
-        running += arrived_ref[plane].astype(wide)
-    total_ref[...] = running
+    for start in range(0, rows, TILE):
+        at = slice(start, min(start + TILE, rows))
+        running = arrived_ref[0, at].astype(wide)
+        for plane in range(1, planes):
+            running += arrived_ref[plane, at].astype(wide)
+        total_ref[at] = running
     sections = out_ref.shape[0] // 2
     lane_tiles = sections // 2
     sum_rows = 6 * lane_tiles
@@ -425,23 +438,18 @@
     lane_tiles = channels // LANES
     tile_rows = 2 * lane_tiles * TILE
     convs = on_core(conv_kernel, shape((tile_rows, LANES), narrow), [], [conv_six, conv_seven])
-    row_tiles = part_width // TILE
-    out_block = (sections, 2 * TILE + width // LANES * (TILE // 2), LANES)
+    in_hbm = pl.BlockSpec(memory_space=pl.ANY)
     outgoing = pl.pallas_call(
         pick_kernel,
-        out_shape=shape(out_block, narrow),
-        grid_spec=pltpu.PrefetchScalarGridSpec(
-            num_scalar_prefetch=1,
-            grid=(1,),
-            in_specs=[
-                pl.BlockSpec(
-                    (TILE, 2 * LANES), lambda i, at: (jnp.minimum(at[0], row_tiles - 1), at[2])
-                ),
-                pl.BlockSpec(feature_grad.shape, lambda i, at: (0, 0, 0)),
-            ],
-            out_specs=pl.BlockSpec(out_block, lambda i, at: (0, 0, 0)),
-        ),
-        compiler_params=pltpu.CompilerParams(vmem_limit_bytes=8 * 1024 * 1024),
+        out_shape=shape((sections, 2 * TILE + width // LANES * (TILE // 2), LANES), narrow),
+        in_specs=[pl.BlockSpec(memory_space=pltpu.SMEM), in_hbm, in_hbm],
+        out_specs=pl.BlockSpec(memory_space=pltpu.VMEM),
+        scratch_shapes=[
+            pltpu.VMEM((TILE, 2 * LANES), narrow),
+            pltpu.VMEM(feature_grad.shape, narrow),
+            pltpu.SemaphoreType.DMA((2,)),
+        ],
+        compiler_params=pltpu.CompilerParams(vmem_limit_bytes=56 * 1024 * 1024),
     )(place, proj_weight.T, feature_grad)
     line = 2 * sections
     opposite = [
@@ -491,6 +499,7 @@
     )
     late_other = swap(late, "c")
     back = on_core(input_kernel, shape((4 * frames, channels), narrow), [], [late, six_full])
+    late, back = lax.optimization_barrier((late, back))
     send_rows = (4 * lane_tiles + width // LANES) * TILE + 6 * lane_tiles
     chip = on_core(
         functools.partial(terms_kernel, width),

time: 144 us -> 143 us (level)
  blocking collectives: 62.9 us -> 89.7 us
  waiting for transfers between devices: 26.9 us -> 10.2 us
  starting transfers between devices: 37.7 us -> 27.3 us
    all_to_all x2 -> x3, blocking collectives: 62.9 us -> 89.7 us  [exchange(): return lax.all_to_all(value, axes, 0, 0, tiled=True)]
    all_to_all x2 -> x1, waiting for transfers between devices: 20.5 us -> 5.22 us  [exchange(): return lax.all_to_all(value, axes, 0, 0, tiled=True)]
    all_to_all x2 -> x1, starting transfers between devices: 23 us -> 12.6 us  [exchange(): return lax.all_to_all(value, axes, 0, 0, tiled=True)]
  transfers between devices with their start and end apart: 6 -> 5, of which waited for: 5 -> 4; matrix products, arithmetic and copies ran while one was open for 0% -> 0% of each run, Pallas kernels for 4% -> 4%
where the time goes in v6:
time: 143 us
  blocking collectives  89.7 us (63%)
  starting transfers between devices  27.3 us (19%)
  Pallas kernels  12 us (8%)
  waiting for transfers between devices  10.2 us (7%)
  local copies, waits for them, and re-layouts  2.11 us (1%)
    all_to_all x3, blocking collectives, exchange(): return lax.all_to_all(value, axes, 0, 0, tiled=True)  89.7 us
    all_to_all x1, starting transfers between devices, exchange(): return lax.all_to_all(value, axes, 0, 0, tiled=True)  12.6 us
    pallas_call x8, Pallas kernels, on_core(): pl.pallas_call(kernel, out_shape=out_shape, in_specs=[pl.BlockSpec(memory...  9.56 us
    ppermute x1, starting transfers between devices, on_device(): other_convs = lax.ppermute(convs, ('zh', 's'), opposite)  8.21 us
    ppermute x3, starting transfers between devices, swap(): return lax.ppermute(value, axis, [(0, 1), (1, 0)])  6.49 us
    all_to_all x1, waiting for transfers between devices, exchange(): return lax.all_to_all(value, axes, 0, 0, tiled=True)  5.22 us
    ppermute x1, waiting for transfers between devices, on_device(): other_convs = lax.ppermute(convs, ('zh', 's'), opposite)  4.08 us
  transfers between devices with their start and end apart: 5, of which 4 were waited for; matrix products, arithmetic and copies ran while one was open for 0% of the time, Pallas kernels for 4%

profile of v6, /device:TPU:32, one launch (start us, length us, event | category | flops | bytes accessed | tf_op | source)
XLA Modules:
  0.0 142.7 jit_solution(14501786857119276471)
XLA Ops:
  0.6 0.6 pad_add_fusion.place_ref
  1.2 2.4 %shard_map.119 = bf16[8,152,128]{2,1,0:T(8,128)(2,1)} custom-call(s32[4]{0:T(128)} %pad_add_fusion.place_ref, bf16[240,512]{1,0:T(8,128)(2,1)} %bitcast.16, bf16[16,4,1920]{2,1,0:T(4,128)(2,1)} %grad_hbm.1), custom_call_target="tpu_custom_call" | custom-call | tf_op jit(solution)/shard_map/pallas_call | solution.py:442
  3.6 12.6 %all-to-all-start = ((bf16[8,152,128]{2,1,0:T(8,128)(2,1)}), bf16[8,152,128]{2,1,0:T(8,128)(2,1)S(1)}, u32[]{:S(2)}, u32[]{:S(2)}) async-start(bf16[8,152,128]{2,1,0:T(8,128)(2,1)} %shard_map.119), calls=%async_computation | async-start | bytes 622592 | tf_op jit(solution)/shard_map/all_to_all | solution.py:53
  16.3 0.0 copy-start.1
  16.3 0.7 copy-done.1
  17.0 0.0 copy-start.2
  17.0 0.7 copy-done.2
  17.7 8.2 %collective-permute-start = (bf16[128,128]{1,0:T(8,128)(2,1)S(1)}, bf16[128,128]{1,0:T(8,128)(2,1)S(1)}, u32[]{:S(2)}, u32[]{:S(2)}) collective-permute-start(bf16[128,128]{1,0:T(8,128)(2,1)S(1)} %shard_map.118.own_ref), channel_id=1, source_target_pairs={{0,20},{1,21},{2,22},{3,23},{4,16},{5,17},{6,18},{7,19},{16,4},{17... | collective-permute-start | bytes 98312 | tf_op jit(solution)/shard_map/ppermute | solution.py:459
  25.9 4.1 %collective-permute-done.other_ref = bf16[128,128]{1,0:T(8,128)(2,1)S(1)} collective-permute-done((bf16[128,128]{1,0:T(8,128)(2,1)S(1)}, bf16[128,128]{1,0:T(8,128)(2,1)S(1)}, u32[]{:S(2)}, u32[]{:S(2)}) %collective-permute-start) | collective-permute-done | bytes 32800 | tf_op jit(solution)/shard_map/ppermute | solution.py:459
  30.0 5.2 %all-to-all-done.arrived_ref.grad_ref = bf16[8,152,128]{2,1,0:T(8,128)(2,1)S(1)} async-done(((bf16[8,152,128]{2,1,0:T(8,128)(2,1)}), bf16[8,152,128]{2,1,0:T(8,128)(2,1)S(1)}, u32[]{:S(2)}, u32[]{:S(2)}) %all-to-all-start) | async-done | bytes 311328 | tf_op jit(solution)/shard_map/all_to_all | solution.py:53
  35.2 0.0 copy-start.3
  35.2 0.7 copy-done.3
  35.9 0.8 shard_map.120
  36.7 0.0 copy-start
  36.7 30.9 %all_to_all.20 = bf16[16,512,128]{2,1,0:T(8,128)(2,1)S(1)} all-to-all(bf16[16,512,128]{2,1,0:T(8,128)(2,1)S(1)} %shard_map.120), channel_id=1, replica_groups=mesh['y'=4,'x'=4,'zh'=2,'c'=2,'s'=8] {'y','x'}, dimensions={0} | all-to-all | bytes 4194304 | tf_op jit(solution)/shard_map/all_to_all | solution.py:53
  67.6 0.0 copy-start.4
  67.6 0.0 copy-start.5
  67.6 0.0 copy-start.6
  67.6 2.0 %collective-permute-start.1 = (bf16[8192,128]{1,0:T(8,128)(2,1)S(1)}, bf16[8192,128]{1,0:T(8,128)(2,1)S(1)}, u32[]{:S(2)}, u32[]{:S(2)}) collective-permute-start(bf16[8192,128]{1,0:T(8,128)(2,1)S(1)} %bitcast.10), channel_id=1, source_target_pairs={{0,8},{8,0},{1,9},{9,1},{2,10},{10,2},{3,11},{11,3},{4,12},{12,4},... | collective-permute-start | bytes 6291464 | tf_op jit(solution)/shard_map/ppermute | solution.py:57
  69.7 0.0 copy-done
  69.7 1.0 shard_map.121
  70.6 2.4 %collective-permute-start.2 = (bf16[256,1024]{1,0:T(8,128)(2,1)S(1)}, bf16[256,1024]{1,0:T(8,128)(2,1)S(1)}, u32[]{:S(2)}, u32[]{:S(2)}) collective-permute-start(bf16[256,1024]{1,0:T(8,128)(2,1)S(1)} %get-tuple-element.17.shared_ref), channel_id=1, source_target_pairs={{0,8},{8,0},{1,9},{9,1},{2,10},{10,2},{3,11},{11,3},{4,12},{12,4},... | collective-permute-start | bytes 1572872 | tf_op jit(solution)/shard_map/ppermute | solution.py:57
  73.0 0.7 collective-permute-done.1
  73.8 0.0 copy-done.4
  73.8 0.0 copy-done.5
  73.8 0.0 copy-done.6
  73.8 3.2 %shard_map.122 = (bf16[1024,512]{1,0:T(8,128)(2,1)S(1)}, bf16[400,512]{1,0:T(8,128)(2,1)S(1)}) custom-call(s32[4]{0:T(128)S(1)} %copy-done.4, bf16[256,1024]{1,0:T(8,128)(2,1)S(1)} %get-tuple-element.17.shared_ref, bf16[16,32,16,128]{3,2,1,0:T(8,128)(2,1)S(1)} %bitcast.12, bf16[16,32,16,128]{3,2,1,0:T(8,128)(2,1)S(1)} %bitcast.13, ...), custom_call_target="tpu_custom_call" | custom-call | tf_op jit(solution)/shard_map/pallas_call | solution.py:63
  77.0 2.0 %collective-permute-start.3 = (bf16[400,512]{1,0:T(8,128)(2,1)S(1)}, bf16[400,512]{1,0:T(8,128)(2,1)S(1)}, u32[]{:S(2)}, u32[]{:S(2)}) collective-permute-start(bf16[400,512]{1,0:T(8,128)(2,1)S(1)} %get-tuple-element.22.late_ref), channel_id=1, source_target_pairs={{0,8},{8,0},{1,9},{9,1},{2,10},{10,2},{3,11},{11,3},{4,12},{12,4},... | collective-permute-start | bytes 1228808 | tf_op jit(solution)/shard_map/ppermute | solution.py:57
  79.1 1.4 shard_map.123
  80.5 0.0 collective-permute-done.2.shared_other_ref
  80.5 0.2 collective-permute-done.3.late_other_ref
  80.7 2.1 %shard_map.124 = bf16[16,520,128]{2,1,0:T(8,128)(2,1)S(1)} custom-call(s32[4]{0:T(128)S(1)} %copy-done.4, bf16[256,1024]{1,0:T(8,128)(2,1)S(1)} %get-tuple-element.17.shared_ref, bf16[256,1024]{1,0:T(8,128)(2,1)S(1)} %collective-permute-done.2.shared_other_ref, bf16[400,512]{1,0:T(8,128)(2,1)S(1)} %get-tuple-element.22.late_ref, ...), custom_call_target="tpu_custom_call" | custom-call | tf_op jit(solution)/shard_map/pallas_call | solution.py:63
  82.8 32.1 %all_to_all.21.arrived_ref = bf16[16,520,128]{2,1,0:T(8,128)(2,1)S(1)} all-to-all(bf16[16,520,128]{2,1,0:T(8,128)(2,1)S(1)} %shard_map.124), channel_id=1, replica_groups=mesh['y'=4,'x'=4,'zh'=2,'c'=2,'s'=8] {'y','x'}, dimensions={0} | all-to-all | bytes 4259840 | tf_op jit(solution)/shard_map/all_to_all | solution.py:53
  114.9 0.3 shard_map.125
  115.2 26.7 %all_to_all.22.arrived_ref = bf16[16,56,128]{2,1,0:T(8,128)(2,1)S(1)} all-to-all(bf16[16,56,128]{2,1,0:T(8,128)(2,1)S(1)} %shard_map.125), channel_id=1, replica_groups=mesh['y'=4,'x'=4,'zh'=2,'c'=2,'s'=8] {'zh','s'}, dimensions={0} | all-to-all | bytes 458752 | tf_op jit(solution)/shard_map/all_to_all | solution.py:53
  142.0 0.7 shard_map.126
  (1 shorter events, 0.0 us)
Async XLA Ops:
  3.6 31.6 %all-to-all-start = ((bf16[8,152,128]{2,1,0:T(8,128)(2,1)}), bf16[8,152,128]{2,1,0:T(8,128)(2,1)S(1)}, u32[]{:S(2)}, u32[]{:S(2)}) async-start(bf16[8,152,128]{2,1,0:T(8,128)(2,1)} %shard_map.119), calls=%async_computation | async-start | bytes 622592 | tf_op jit(solution)/shard_map/all_to_all | solution.py:53
  16.3 0.7 copy-start.1
  17.0 0.7 copy-start.2
  17.7 12.3 %collective-permute-start = (bf16[128,128]{1,0:T(8,128)(2,1)S(1)}, bf16[128,128]{1,0:T(8,128)(2,1)S(1)}, u32[]{:S(2)}, u32[]{:S(2)}) collective-permute-start(bf16[128,128]{1,0:T(8,128)(2,1)S(1)} %shard_map.118.own_ref), channel_id=1, source_target_pairs={{0,20},{1,21},{2,22},{3,23},{4,16},{5,17},{6,18},{7,19},{16,4},{17... | collective-permute-start | bytes 98312 | tf_op jit(solution)/shard_map/ppermute | solution.py:459
  35.2 0.7 copy-start.3
  36.7 32.9 %copy-start = (bf16[2,128,512]{2,1,0:T(8,128)(2,1)S(1)}, bf16[2,128,512]{2,1,0:T(8,128)(2,1)}, u32[]{:S(2)}) copy-start(bf16[2,128,512]{2,1,0:T(8,128)(2,1)} %param.7) | copy-start | bytes 786436
  67.6 6.2 %copy-start.4 = (s32[4]{0:T(128)S(1)}, s32[4]{0:T(128)}, u32[]{:S(2)}) copy-start(s32[4]{0:T(128)} %pad_add_fusion.place_ref) | copy-start | bytes 52
  67.6 6.2 %copy-start.5 = (f32[3,512]{1,0:T(4,128)S(1)}, f32[3,512]{1,0:T(4,128)}, u32[]{:S(2)}) copy-start(f32[3,512]{1,0:T(4,128)} %gains_ref.1) | copy-start | bytes 18436
  67.6 6.2 %copy-start.6 = (f32[3,512]{1,0:T(4,128)S(1)}, f32[3,512]{1,0:T(4,128)}, u32[]{:S(2)}) copy-start(f32[3,512]{1,0:T(4,128)} %biases_ref.1) | copy-start | bytes 18436
  67.6 6.2 %collective-permute-start.1 = (bf16[8192,128]{1,0:T(8,128)(2,1)S(1)}, bf16[8192,128]{1,0:T(8,128)(2,1)S(1)}, u32[]{:S(2)}, u32[]{:S(2)}) collective-permute-start(bf16[8192,128]{1,0:T(8,128)(2,1)S(1)} %bitcast.10), channel_id=1, source_target_pairs={{0,8},{8,0},{1,9},{9,1},{2,10},{10,2},{3,11},{11,3},{4,12},{12,4},... | collective-permute-start | bytes 6291464 | tf_op jit(solution)/shard_map/ppermute | solution.py:57
  70.6 9.8 %collective-permute-start.2 = (bf16[256,1024]{1,0:T(8,128)(2,1)S(1)}, bf16[256,1024]{1,0:T(8,128)(2,1)S(1)}, u32[]{:S(2)}, u32[]{:S(2)}) collective-permute-start(bf16[256,1024]{1,0:T(8,128)(2,1)S(1)} %get-tuple-element.17.shared_ref), channel_id=1, source_target_pairs={{0,8},{8,0},{1,9},{9,1},{2,10},{10,2},{3,11},{11,3},{4,12},{12,4},... | collective-permute-start | bytes 1572872 | tf_op jit(solution)/shard_map/ppermute | solution.py:57
  77.0 3.6 %collective-permute-start.3 = (bf16[400,512]{1,0:T(8,128)(2,1)S(1)}, bf16[400,512]{1,0:T(8,128)(2,1)S(1)}, u32[]{:S(2)}, u32[]{:S(2)}) collective-permute-start(bf16[400,512]{1,0:T(8,128)(2,1)S(1)} %get-tuple-element.22.late_ref), channel_id=1, source_target_pairs={{0,8},{8,0},{1,9},{9,1},{2,10},{10,2},{3,11},{11,3},{4,12},{12,4},... | collective-permute-start | bytes 1228808 | tf_op jit(solution)/shard_map/ppermute | solution.py:57

commit v7 on v6

--- a/solution.py
+++ b/solution.py
@@ -57,17 +57,17 @@
     return lax.ppermute(value, axis, [(0, 1), (1, 0)])
 
 
-def on_core(kernel, out_shape, scalars, arrays, scratch=(), megabytes=8):
+def on_core(kernel, out_shape, arrays, scratch=(), megabytes=8):
     multiple = isinstance(out_shape, (list, tuple))
     vmem = pl.BlockSpec(memory_space=pltpu.VMEM)
     return pl.pallas_call(
         kernel,
         out_shape=out_shape,
-        in_specs=[pl.BlockSpec(memory_space=pltpu.SMEM)] * len(scalars) + [vmem] * len(arrays),
+        in_specs=[vmem] * len(arrays),
         out_specs=[vmem] * len(out_shape) if multiple else vmem,
         scratch_shapes=list(scratch),
         compiler_params=pltpu.CompilerParams(vmem_limit_bytes=megabytes * 1024 * 1024),
-    )(*scalars, *arrays)
+    )(*arrays)
 
 
 def conv_kernel(six_ref, seven_ref, conv_ref):
@@ -78,8 +78,8 @@
             conv_ref[at : at + TILE] = source[:, lane * LANES : (lane + 1) * LANES]
 
 
-def pick_kernel(place_ref, proj_hbm, grad_hbm, out_ref, proj_ref, grad_ref, done):
-    plane, core = place_ref[0], place_ref[2]
+def pick_kernel(proj_hbm, grad_hbm, out_ref, proj_ref, grad_ref, done):
+    plane, core = lax.axis_index(("y", "x")), lax.axis_index("c")
     row = pl.multiple_of(jnp.minimum(plane, proj_hbm.shape[0] // TILE - 1) * TILE, TILE)
     lane = pl.multiple_of(core * 2 * LANES, LANES)
     grad_copy = pltpu.make_async_copy(grad_hbm, grad_ref, done.at[0])
@@ -109,8 +109,8 @@
             ).astype(narrow)
 
 
-def bundle_kernel(place_ref, own_ref, other_ref, arrived_ref, out_ref):
-    half = place_ref[1]
+def bundle_kernel(own_ref, other_ref, arrived_ref, out_ref):
+    half = lax.axis_index("zh")
     rows = own_ref.shape[0]
     for plane in range(out_ref.shape[0]):
         out_ref[plane, pl.ds(pl.multiple_of(half * rows, TILE), rows)] = own_ref[...]
@@ -190,7 +190,6 @@
 
 def layer_kernel(
     width,
-    place_ref,
     shared_ref,
     own_ref,
     other_ref,
@@ -202,7 +201,7 @@
     seven_ref,
     proj_ref,
 ):
-    core = place_ref[2]
+    core = lax.axis_index("c")
     frames, channels = part_ref.shape[0], shared_ref.shape[1] // 2
     lane_tiles = channels // LANES
     planes = own_ref.shape[0]
@@ -284,7 +283,6 @@
 
 def terms_kernel(
     width,
-    place_ref,
     shared_ref,
     shared_other_ref,
     late_ref,
@@ -294,7 +292,7 @@
     term_seven_ref,
     term_proj_ref,
 ):
-    core = place_ref[2]
+    core = lax.axis_index("c")
     frames, channels = shared_ref.shape[0] // 4, late_ref.shape[1]
     lane_tiles = channels // LANES
     planes = send_ref.shape[0]
@@ -431,18 +429,15 @@
     planes = lax.axis_size(("y", "x"))
     frames = utt_local * positions // 4
     shape = jax.ShapeDtypeStruct
-    place = jnp.stack(
-        [lax.axis_index(("y", "x")), lax.axis_index("zh"), lax.axis_index("c"), lax.axis_index("s")]
-    ).astype(jnp.int32)
 
     lane_tiles = channels // LANES
     tile_rows = 2 * lane_tiles * TILE
-    convs = on_core(conv_kernel, shape((tile_rows, LANES), narrow), [], [conv_six, conv_seven])
+    convs = on_core(conv_kernel, shape((tile_rows, LANES), narrow), [conv_six, conv_seven])
     in_hbm = pl.BlockSpec(memory_space=pl.ANY)
     outgoing = pl.pallas_call(
         pick_kernel,
         out_shape=shape((sections, 2 * TILE + width // LANES * (TILE // 2), LANES), narrow),
-        in_specs=[pl.BlockSpec(memory_space=pltpu.SMEM), in_hbm, in_hbm],
+        in_specs=[in_hbm, in_hbm],
         out_specs=pl.BlockSpec(memory_space=pltpu.VMEM),
         scratch_shapes=[
             pltpu.VMEM((TILE, 2 * LANES), narrow),
@@ -450,7 +445,7 @@
             pltpu.SemaphoreType.DMA((2,)),
         ],
         compiler_params=pltpu.CompilerParams(vmem_limit_bytes=56 * 1024 * 1024),
-    )(place, proj_weight.T, feature_grad)
+    )(proj_weight.T, feature_grad)
     line = 2 * sections
     opposite = [
         (z, (1 - z // sections) * sections + (z % sections + sections // 2) % sections)
@@ -461,7 +456,6 @@
     bundle = on_core(
         bundle_kernel,
         shape((planes, 2 * tile_rows + sections * 2 * TILE, LANES), narrow),
-        [place],
         [convs, other_convs, arrived],
     )
     gathered = exchange(bundle, ("y", "x"))
@@ -471,7 +465,6 @@
     shared, part = on_core(
         early_kernel,
         [shape((4 * frames, 2 * channels), narrow), shape((frames, 2 * LANES), wide)],
-        [],
         [layer_five.reshape(4 * frames, channels), gathered.reshape(tiles_shape), arrived],
         scratch=[pltpu.VMEM((width, 2 * LANES), narrow), pltpu.VMEM((frames, width), wide)],
     )
@@ -482,7 +475,6 @@
             shape((2 * channels, channels), narrow),
             shape((6 * frames + TILE, channels), narrow),
         ],
-        [place],
         [
             shared,
             gathered.reshape(tiles_shape),
@@ -498,13 +490,12 @@
         megabytes=16,
     )
     late_other = swap(late, "c")
-    back = on_core(input_kernel, shape((4 * frames, channels), narrow), [], [late, six_full])
+    back = on_core(input_kernel, shape((4 * frames, channels), narrow), [late, six_full])
     late, back = lax.optimization_barrier((late, back))
     send_rows = (4 * lane_tiles + width // LANES) * TILE + 6 * lane_tiles
     chip = on_core(
         functools.partial(terms_kernel, width),
         shape((planes, send_rows, LANES), narrow),
-        [place],
         [shared, shared_other, late, late_other],
         scratch=[
             pltpu.VMEM((2 * channels, channels), wide),
@@ -517,7 +508,6 @@
     line_out = on_core(
         plane_kernel,
         shape((2 * sections, 3 * TILE + TILE // 2, LANES), narrow),
-        [],
         [plane_in],
         scratch=[pltpu.VMEM((send_rows, LANES), wide)],
     )
@@ -531,7 +521,6 @@
             shape((3, channels), wide),
             shape((3, channels), wide),
         ],
-        [],
         [line_in],
     )
     return (

time: 143 us -> 140 us (0.979)
  Pallas kernels: 12 us -> 9.62 us
    pallas_call x8, Pallas kernels: 9.56 us -> 7.88 us  [on_core(): pl.pallas_call(kernel, out_shape=out_shape, in_specs=[vmem] * len(arrays)...]
where the time goes in v7:
time: 140 us; the launch traced here: 139 us
  blocking collectives  89.7 us (64%)
  starting transfers between devices  27.3 us (20%)
  waiting for transfers between devices  10.2 us (7%)
  Pallas kernels  9.62 us (7%)
  local copies, waits for them, and re-layouts  1.45 us (1%)
    all_to_all x3, blocking collectives, exchange(): return lax.all_to_all(value, axes, 0, 0, tiled=True)  89.7 us
    all_to_all x1, starting transfers between devices, exchange(): return lax.all_to_all(value, axes, 0, 0, tiled=True)  12.6 us
    ppermute x1, starting transfers between devices, on_device(): other_convs = lax.ppermute(convs, ('zh', 's'), opposite)  8.21 us
    pallas_call x8, Pallas kernels, on_core(): pl.pallas_call(kernel, out_shape=out_shape, in_specs=[vmem] * len(arrays)...  7.88 us
    ppermute x3, starting transfers between devices, swap(): return lax.ppermute(value, axis, [(0, 1), (1, 0)])  6.5 us
    all_to_all x1, waiting for transfers between devices, exchange(): return lax.all_to_all(value, axes, 0, 0, tiled=True)  5.22 us
    ppermute x1, waiting for transfers between devices, on_device(): other_convs = lax.ppermute(convs, ('zh', 's'), opposite)  4.08 us
  transfers between devices with their start and end apart: 5, of which 4 were waited for; matrix products, arithmetic and copies ran while one was open for 0% of the time, Pallas kernels for 4%

profile of v7, /device:TPU:32, one launch (start us, length us, event | category | flops | bytes accessed | tf_op | source)
XLA Modules:
  0.0 139.1 jit_solution(5599920261609459545)
XLA Ops:
  0.6 1.7 %shard_map.119 = bf16[8,152,128]{2,1,0:T(8,128)(2,1)} custom-call(bf16[240,512]{1,0:T(8,128)(2,1)} %bitcast.12, bf16[16,4,1920]{2,1,0:T(4,128)(2,1)} %grad_hbm.1), custom_call_target="tpu_custom_call" | custom-call | tf_op jit(solution)/shard_map/pallas_call | solution.py:437
  2.4 12.6 %all-to-all-start = ((bf16[8,152,128]{2,1,0:T(8,128)(2,1)}), bf16[8,152,128]{2,1,0:T(8,128)(2,1)S(1)}, u32[]{:S(2)}, u32[]{:S(2)}) async-start(bf16[8,152,128]{2,1,0:T(8,128)(2,1)} %shard_map.119), calls=%async_computation | async-start | bytes 622592 | tf_op jit(solution)/shard_map/all_to_all | solution.py:53
  15.0 0.0 copy-start.1
  15.0 0.7 copy-done.1
  15.7 0.0 copy-start.2
  15.7 0.7 copy-done.2
  16.5 8.2 %collective-permute-start = (bf16[128,128]{1,0:T(8,128)(2,1)S(1)}, bf16[128,128]{1,0:T(8,128)(2,1)S(1)}, u32[]{:S(2)}, u32[]{:S(2)}) collective-permute-start(bf16[128,128]{1,0:T(8,128)(2,1)S(1)} %shard_map.118.own_ref), channel_id=1, source_target_pairs={{0,20},{1,21},{2,22},{3,23},{4,16},{5,17},{6,18},{7,19},{16,4},{17... | collective-permute-start | bytes 98312 | tf_op jit(solution)/shard_map/ppermute | solution.py:454
  24.7 4.1 %collective-permute-done.other_ref = bf16[128,128]{1,0:T(8,128)(2,1)S(1)} collective-permute-done((bf16[128,128]{1,0:T(8,128)(2,1)S(1)}, bf16[128,128]{1,0:T(8,128)(2,1)S(1)}, u32[]{:S(2)}, u32[]{:S(2)}) %collective-permute-start) | collective-permute-done | bytes 32800 | tf_op jit(solution)/shard_map/ppermute | solution.py:454
  28.8 5.2 %all-to-all-done.arrived_ref.grad_ref = bf16[8,152,128]{2,1,0:T(8,128)(2,1)S(1)} async-done(((bf16[8,152,128]{2,1,0:T(8,128)(2,1)}), bf16[8,152,128]{2,1,0:T(8,128)(2,1)S(1)}, u32[]{:S(2)}, u32[]{:S(2)}) %all-to-all-start) | async-done | bytes 311328 | tf_op jit(solution)/shard_map/all_to_all | solution.py:53
  34.0 0.3 shard_map.120
  34.2 0.0 copy-start
  34.3 30.9 %all_to_all.20 = bf16[16,512,128]{2,1,0:T(8,128)(2,1)S(1)} all-to-all(bf16[16,512,128]{2,1,0:T(8,128)(2,1)S(1)} %shard_map.120), channel_id=1, replica_groups=mesh['y'=4,'x'=4,'zh'=2,'c'=2,'s'=8] {'y','x'}, dimensions={0} | all-to-all | bytes 4194304 | tf_op jit(solution)/shard_map/all_to_all | solution.py:53
  65.1 0.0 copy-start.3
  65.1 0.0 copy-start.4
  65.1 2.0 %collective-permute-start.1 = (bf16[8192,128]{1,0:T(8,128)(2,1)S(1)}, bf16[8192,128]{1,0:T(8,128)(2,1)S(1)}, u32[]{:S(2)}, u32[]{:S(2)}) collective-permute-start(bf16[8192,128]{1,0:T(8,128)(2,1)S(1)} %bitcast.6), channel_id=1, source_target_pairs={{0,8},{8,0},{1,9},{9,1},{2,10},{10,2},{3,11},{11,3},{4,12},{12,4},... | collective-permute-start | bytes 6291464 | tf_op jit(solution)/shard_map/ppermute | solution.py:57
  67.2 0.0 copy-done
  67.2 1.0 shard_map.121
  68.1 2.4 %collective-permute-start.2 = (bf16[256,1024]{1,0:T(8,128)(2,1)S(1)}, bf16[256,1024]{1,0:T(8,128)(2,1)S(1)}, u32[]{:S(2)}, u32[]{:S(2)}) collective-permute-start(bf16[256,1024]{1,0:T(8,128)(2,1)S(1)} %get-tuple-element.17.shared_ref), channel_id=1, source_target_pairs={{0,8},{8,0},{1,9},{9,1},{2,10},{10,2},{3,11},{11,3},{4,12},{12,4},... | collective-permute-start | bytes 1572872 | tf_op jit(solution)/shard_map/ppermute | solution.py:57
  70.6 0.7 collective-permute-done.1
  71.3 0.0 copy-done.3
  71.3 0.0 copy-done.4
  71.3 2.7 %shard_map.122 = (bf16[1024,512]{1,0:T(8,128)(2,1)S(1)}, bf16[400,512]{1,0:T(8,128)(2,1)S(1)}) custom-call(bf16[256,1024]{1,0:T(8,128)(2,1)S(1)} %get-tuple-element.17.shared_ref, bf16[16,32,16,128]{3,2,1,0:T(8,128)(2,1)S(1)} %bitcast.8, bf16[16,32,16,128]{3,2,1,0:T(8,128)(2,1)S(1)} %bitcast.9, f32[64,256]{1,0:T(8,128)S(1)} %get-tuple-element.18.part_ref, ...), custom_call_target="tpu_custom_call" | custom-call | tf_op jit(solution)/shard_map/pallas_call | solution.py:63
  74.0 2.0 %collective-permute-start.3 = (bf16[400,512]{1,0:T(8,128)(2,1)S(1)}, bf16[400,512]{1,0:T(8,128)(2,1)S(1)}, u32[]{:S(2)}, u32[]{:S(2)}) collective-permute-start(bf16[400,512]{1,0:T(8,128)(2,1)S(1)} %get-tuple-element.22.late_ref), channel_id=1, source_target_pairs={{0,8},{8,0},{1,9},{9,1},{2,10},{10,2},{3,11},{11,3},{4,12},{12,4},... | collective-permute-start | bytes 1228808 | tf_op jit(solution)/shard_map/ppermute | solution.py:57
  76.0 1.4 shard_map.123
  77.4 0.0 collective-permute-done.2.shared_other_ref
  77.4 0.2 collective-permute-done.3.late_other_ref
  77.6 1.6 %shard_map.124 = bf16[16,520,128]{2,1,0:T(8,128)(2,1)S(1)} custom-call(bf16[256,1024]{1,0:T(8,128)(2,1)S(1)} %get-tuple-element.17.shared_ref, bf16[256,1024]{1,0:T(8,128)(2,1)S(1)} %collective-permute-done.2.shared_other_ref, bf16[400,512]{1,0:T(8,128)(2,1)S(1)} %get-tuple-element.22.late_ref, bf16[400,512]{1,0:T(8,128)(2,1)S(1)} %collective-permute-done.3.late_other_ref), custom_call_target="tpu_custom_call" | custom-call | tf_op jit(solution)/shard_map/pallas_call | solution.py:63
  79.2 32.1 %all_to_all.21.arrived_ref = bf16[16,520,128]{2,1,0:T(8,128)(2,1)S(1)} all-to-all(bf16[16,520,128]{2,1,0:T(8,128)(2,1)S(1)} %shard_map.124), channel_id=1, replica_groups=mesh['y'=4,'x'=4,'zh'=2,'c'=2,'s'=8] {'y','x'}, dimensions={0} | all-to-all | bytes 4259840 | tf_op jit(solution)/shard_map/all_to_all | solution.py:53
  111.3 0.3 shard_map.125
  111.6 26.7 %all_to_all.22.arrived_ref = bf16[16,56,128]{2,1,0:T(8,128)(2,1)S(1)} all-to-all(bf16[16,56,128]{2,1,0:T(8,128)(2,1)S(1)} %shard_map.125), channel_id=1, replica_groups=mesh['y'=4,'x'=4,'zh'=2,'c'=2,'s'=8] {'zh','s'}, dimensions={0} | all-to-all | bytes 458752 | tf_op jit(solution)/shard_map/all_to_all | solution.py:53
  138.4 0.7 shard_map.126
  (1 shorter events, 0.0 us)
Async XLA Ops:
  2.4 31.6 %all-to-all-start = ((bf16[8,152,128]{2,1,0:T(8,128)(2,1)}), bf16[8,152,128]{2,1,0:T(8,128)(2,1)S(1)}, u32[]{:S(2)}, u32[]{:S(2)}) async-start(bf16[8,152,128]{2,1,0:T(8,128)(2,1)} %shard_map.119), calls=%async_computation | async-start | bytes 622592 | tf_op jit(solution)/shard_map/all_to_all | solution.py:53
  15.0 0.7 copy-start.1
  15.7 0.7 copy-start.2
  16.5 12.3 %collective-permute-start = (bf16[128,128]{1,0:T(8,128)(2,1)S(1)}, bf16[128,128]{1,0:T(8,128)(2,1)S(1)}, u32[]{:S(2)}, u32[]{:S(2)}) collective-permute-start(bf16[128,128]{1,0:T(8,128)(2,1)S(1)} %shard_map.118.own_ref), channel_id=1, source_target_pairs={{0,20},{1,21},{2,22},{3,23},{4,16},{5,17},{6,18},{7,19},{16,4},{17... | collective-permute-start | bytes 98312 | tf_op jit(solution)/shard_map/ppermute | solution.py:454
  34.2 32.9 %copy-start = (bf16[2,128,512]{2,1,0:T(8,128)(2,1)S(1)}, bf16[2,128,512]{2,1,0:T(8,128)(2,1)}, u32[]{:S(2)}) copy-start(bf16[2,128,512]{2,1,0:T(8,128)(2,1)} %param.7) | copy-start | bytes 786436
  65.1 6.2 %copy-start.3 = (f32[3,512]{1,0:T(4,128)S(1)}, f32[3,512]{1,0:T(4,128)}, u32[]{:S(2)}) copy-start(f32[3,512]{1,0:T(4,128)} %gains_ref.1) | copy-start | bytes 18436
  65.1 6.2 %copy-start.4 = (f32[3,512]{1,0:T(4,128)S(1)}, f32[3,512]{1,0:T(4,128)}, u32[]{:S(2)}) copy-start(f32[3,512]{1,0:T(4,128)} %biases_ref.1) | copy-start | bytes 18436
  65.1 6.2 %collective-permute-start.1 = (bf16[8192,128]{1,0:T(8,128)(2,1)S(1)}, bf16[8192,128]{1,0:T(8,128)(2,1)S(1)}, u32[]{:S(2)}, u32[]{:S(2)}) collective-permute-start(bf16[8192,128]{1,0:T(8,128)(2,1)S(1)} %bitcast.6), channel_id=1, source_target_pairs={{0,8},{8,0},{1,9},{9,1},{2,10},{10,2},{3,11},{11,3},{4,12},{12,4},... | collective-permute-start | bytes 6291464 | tf_op jit(solution)/shard_map/ppermute | solution.py:57
  68.1 9.3 %collective-permute-start.2 = (bf16[256,1024]{1,0:T(8,128)(2,1)S(1)}, bf16[256,1024]{1,0:T(8,128)(2,1)S(1)}, u32[]{:S(2)}, u32[]{:S(2)}) collective-permute-start(bf16[256,1024]{1,0:T(8,128)(2,1)S(1)} %get-tuple-element.17.shared_ref), channel_id=1, source_target_pairs={{0,8},{8,0},{1,9},{9,1},{2,10},{10,2},{3,11},{11,3},{4,12},{12,4},... | collective-permute-start | bytes 1572872 | tf_op jit(solution)/shard_map/ppermute | solution.py:57
  74.0 3.6 %collective-permute-start.3 = (bf16[400,512]{1,0:T(8,128)(2,1)S(1)}, bf16[400,512]{1,0:T(8,128)(2,1)S(1)}, u32[]{:S(2)}, u32[]{:S(2)}) collective-permute-start(bf16[400,512]{1,0:T(8,128)(2,1)S(1)} %get-tuple-element.22.late_ref), channel_id=1, source_target_pairs={{0,8},{8,0},{1,9},{9,1},{2,10},{10,2},{3,11},{11,3},{4,12},{12,4},... | collective-permute-start | bytes 1228808 | tf_op jit(solution)/shard_map/ppermute | solution.py:57

commit v8 on v7

--- a/solution.py
+++ b/solution.py
@@ -103,10 +103,10 @@
             pieces = [
                 part[:, at : at + LANES] for at in range(lane, min(width, lane + 2 * LANES), LANES)
             ]
+            if len(pieces) == 1:
+                pieces.append(jnp.zeros(pieces[0].shape, wide))
             start = 2 * TILE + lane // LANES * (TILE // 2)
-            out_ref[section, start : start + len(pieces) * (TILE // 2)] = jnp.concatenate(
-                pieces, axis=0
-            ).astype(narrow)
+            out_ref[section, start : start + TILE] = jnp.concatenate(pieces, axis=0).astype(narrow)
 
 
 def bundle_kernel(own_ref, other_ref, arrived_ref, out_ref):
@@ -162,8 +162,7 @@
         for lane in range(width // LANES):
             start = 2 * TILE + lane * eight
             if lane % 2 == 0:
-                count = min(2, width // LANES - lane)
-                stacked = grad_ref[section, start : start + count * eight].astype(wide)
+                stacked = grad_ref[section, start : start + TILE].astype(wide)
             rows_ref[
                 section * eight : (section + 1) * eight, lane * LANES : (lane + 1) * LANES
             ] = stacked[(lane % 2) * eight : (lane % 2 + 1) * eight]
@@ -338,7 +337,9 @@
     lax.fori_loop(0, planes, pack, 0)
     sums = (late_ref[6 * frames :].astype(wide) + late_other_ref[6 * frames :].astype(wide))[:6]
     sums = jnp.concatenate(
-        [sums[:, lane * LANES : (lane + 1) * LANES] for lane in range(lane_tiles)], axis=0
+        [sums[:, lane * LANES : (lane + 1) * LANES] for lane in range(lane_tiles)]
+        + [jnp.zeros((TILE // 2, LANES), wide)],
+        axis=0,
     ).astype(narrow)
     at = (4 * lane_tiles + width // LANES) * TILE
     send_ref[:, at:] = jnp.broadcast_to(sums[None], (planes,) + sums.shape)
@@ -367,7 +368,7 @@
         total_ref[at] = running
     sections = out_ref.shape[0] // 2
     lane_tiles = sections // 2
-    sum_rows = 6 * lane_tiles
+    sum_rows = 2 * TILE
     proj_tiles = (rows - sum_rows) // TILE - 4 * lane_tiles
     left = lax.broadcasted_iota(jnp.int32, (TILE, LANES), 1) < LANES // 2
     for half in range(2):
@@ -436,7 +437,7 @@
     in_hbm = pl.BlockSpec(memory_space=pl.ANY)
     outgoing = pl.pallas_call(
         pick_kernel,
-        out_shape=shape((sections, 2 * TILE + width // LANES * (TILE // 2), LANES), narrow),
+        out_shape=shape((sections, 2 * TILE + (width // LANES + 1) // 2 * TILE, LANES), narrow),
         in_specs=[in_hbm, in_hbm],
         out_specs=pl.BlockSpec(memory_space=pltpu.VMEM),
         scratch_shapes=[
@@ -492,7 +493,7 @@
     late_other = swap(late, "c")
     back = on_core(input_kernel, shape((4 * frames, channels), narrow), [late, six_full])
     late, back = lax.optimization_barrier((late, back))
-    send_rows = (4 * lane_tiles + width // LANES) * TILE + 6 * lane_tiles
+    send_rows = (4 * lane_tiles + width // LANES + 2) * TILE
     chip = on_core(
         functools.partial(terms_kernel, width),
         shape((planes, send_rows, LANES), narrow),
@@ -507,7 +508,7 @@
     plane_in = exchange(chip, ("y", "x"))
     line_out = on_core(
         plane_kernel,
-        shape((2 * sections, 3 * TILE + TILE // 2, LANES), narrow),
+        shape((2 * sections, 4 * TILE, LANES), narrow),
         [plane_in],
         scratch=[pltpu.VMEM((send_rows, LANES), wide)],
     )

time: 140 us -> 141 us (level)
  no operation moved by 1% of the time
where the time goes in v8:
time: 141 us
  blocking collectives  90.8 us (64%)
  starting transfers between devices  27.3 us (19%)
  waiting for transfers between devices  10.9 us (8%)
  Pallas kernels  9.63 us (7%)
  local copies, waits for them, and re-layouts  1.45 us (1%)
    all_to_all x3, blocking collectives, exchange(): return lax.all_to_all(value, axes, 0, 0, tiled=True)  90.8 us
    all_to_all x1, starting transfers between devices, exchange(): return lax.all_to_all(value, axes, 0, 0, tiled=True)  12.6 us
    ppermute x1, starting transfers between devices, on_device(): other_convs = lax.ppermute(convs, ('zh', 's'), opposite)  8.21 us
    pallas_call x8, Pallas kernels, on_core(): pl.pallas_call(kernel, out_shape=out_shape, in_specs=[vmem] * len(arrays)...  7.89 us
    ppermute x3, starting transfers between devices, swap(): return lax.ppermute(value, axis, [(0, 1), (1, 0)])  6.49 us
    all_to_all x1, waiting for transfers between devices, exchange(): return lax.all_to_all(value, axes, 0, 0, tiled=True)  5.53 us
    ppermute x1, waiting for transfers between devices, on_device(): other_convs = lax.ppermute(convs, ('zh', 's'), opposite)  4.43 us
  transfers between devices with their start and end apart: 5, of which 4 were waited for; matrix products, arithmetic and copies ran while one was open for 0% of the time, Pallas kernels for 4%

profile of v8, /device:TPU:32, one launch (start us, length us, event | category | flops | bytes accessed | tf_op | source)
XLA Modules:
  0.0 140.8 jit_solution(17304074718181615214)
XLA Ops:
  0.6 1.7 %shard_map.119 = bf16[8,160,128]{2,1,0:T(8,128)(2,1)} custom-call(bf16[240,512]{1,0:T(8,128)(2,1)} %bitcast.12, bf16[16,4,1920]{2,1,0:T(4,128)(2,1)} %grad_hbm.1), custom_call_target="tpu_custom_call" | custom-call | tf_op jit(solution)/shard_map/pallas_call | solution.py:438
  2.4 12.6 %all-to-all-start = ((bf16[8,160,128]{2,1,0:T(8,128)(2,1)}), bf16[8,160,128]{2,1,0:T(8,128)(2,1)S(1)}, u32[]{:S(2)}, u32[]{:S(2)}) async-start(bf16[8,160,128]{2,1,0:T(8,128)(2,1)} %shard_map.119), calls=%async_computation | async-start | bytes 655360 | tf_op jit(solution)/shard_map/all_to_all | solution.py:53
  15.0 0.0 copy-start.1
  15.0 0.7 copy-done.1
  15.7 0.0 copy-start.2
  15.7 0.7 copy-done.2
  16.5 8.2 %collective-permute-start = (bf16[128,128]{1,0:T(8,128)(2,1)S(1)}, bf16[128,128]{1,0:T(8,128)(2,1)S(1)}, u32[]{:S(2)}, u32[]{:S(2)}) collective-permute-start(bf16[128,128]{1,0:T(8,128)(2,1)S(1)} %shard_map.118.own_ref), channel_id=1, source_target_pairs={{0,20},{1,21},{2,22},{3,23},{4,16},{5,17},{6,18},{7,19},{16,4},{17... | collective-permute-start | bytes 98312 | tf_op jit(solution)/shard_map/ppermute | solution.py:455
  24.7 4.4 %collective-permute-done.other_ref = bf16[128,128]{1,0:T(8,128)(2,1)S(1)} collective-permute-done((bf16[128,128]{1,0:T(8,128)(2,1)S(1)}, bf16[128,128]{1,0:T(8,128)(2,1)S(1)}, u32[]{:S(2)}, u32[]{:S(2)}) %collective-permute-start) | collective-permute-done | bytes 32800 | tf_op jit(solution)/shard_map/ppermute | solution.py:455
  29.1 5.5 %all-to-all-done.arrived_ref.grad_ref = bf16[8,160,128]{2,1,0:T(8,128)(2,1)S(1)} async-done(((bf16[8,160,128]{2,1,0:T(8,128)(2,1)}), bf16[8,160,128]{2,1,0:T(8,128)(2,1)S(1)}, u32[]{:S(2)}, u32[]{:S(2)}) %all-to-all-start) | async-done | bytes 327712 | tf_op jit(solution)/shard_map/all_to_all | solution.py:53
  34.6 0.3 shard_map.120
  34.9 0.0 copy-start
  34.9 31.1 %all_to_all.20 = bf16[16,512,128]{2,1,0:T(8,128)(2,1)S(1)} all-to-all(bf16[16,512,128]{2,1,0:T(8,128)(2,1)S(1)} %shard_map.120), channel_id=1, replica_groups=mesh['y'=4,'x'=4,'zh'=2,'c'=2,'s'=8] {'y','x'}, dimensions={0} | all-to-all | bytes 4194304 | tf_op jit(solution)/shard_map/all_to_all | solution.py:53
  66.0 0.0 copy-start.3
  66.0 0.0 copy-start.4
  66.0 2.0 %collective-permute-start.1 = (bf16[8192,128]{1,0:T(8,128)(2,1)S(1)}, bf16[8192,128]{1,0:T(8,128)(2,1)S(1)}, u32[]{:S(2)}, u32[]{:S(2)}) collective-permute-start(bf16[8192,128]{1,0:T(8,128)(2,1)S(1)} %bitcast.6), channel_id=1, source_target_pairs={{0,8},{8,0},{1,9},{9,1},{2,10},{10,2},{3,11},{11,3},{4,12},{12,4},... | collective-permute-start | bytes 6291464 | tf_op jit(solution)/shard_map/ppermute | solution.py:57
  68.0 0.0 copy-done
  68.0 1.0 shard_map.121
  69.0 2.4 %collective-permute-start.2 = (bf16[256,1024]{1,0:T(8,128)(2,1)S(1)}, bf16[256,1024]{1,0:T(8,128)(2,1)S(1)}, u32[]{:S(2)}, u32[]{:S(2)}) collective-permute-start(bf16[256,1024]{1,0:T(8,128)(2,1)S(1)} %get-tuple-element.17.shared_ref), channel_id=1, source_target_pairs={{0,8},{8,0},{1,9},{9,1},{2,10},{10,2},{3,11},{11,3},{4,12},{12,4},... | collective-permute-start | bytes 1572872 | tf_op jit(solution)/shard_map/ppermute | solution.py:57
  71.4 0.7 collective-permute-done.1
  72.2 0.0 copy-done.3
  72.2 0.0 copy-done.4
  72.2 2.7 %shard_map.122 = (bf16[1024,512]{1,0:T(8,128)(2,1)S(1)}, bf16[400,512]{1,0:T(8,128)(2,1)S(1)}) custom-call(bf16[256,1024]{1,0:T(8,128)(2,1)S(1)} %get-tuple-element.17.shared_ref, bf16[16,32,16,128]{3,2,1,0:T(8,128)(2,1)S(1)} %bitcast.8, bf16[16,32,16,128]{3,2,1,0:T(8,128)(2,1)S(1)} %bitcast.9, f32[64,256]{1,0:T(8,128)S(1)} %get-tuple-element.18.part_ref, ...), custom_call_target="tpu_custom_call" | custom-call | tf_op jit(solution)/shard_map/pallas_call | solution.py:63
  74.8 2.0 %collective-permute-start.3 = (bf16[400,512]{1,0:T(8,128)(2,1)S(1)}, bf16[400,512]{1,0:T(8,128)(2,1)S(1)}, u32[]{:S(2)}, u32[]{:S(2)}) collective-permute-start(bf16[400,512]{1,0:T(8,128)(2,1)S(1)} %get-tuple-element.22.late_ref), channel_id=1, source_target_pairs={{0,8},{8,0},{1,9},{9,1},{2,10},{10,2},{3,11},{11,3},{4,12},{12,4},... | collective-permute-start | bytes 1228808 | tf_op jit(solution)/shard_map/ppermute | solution.py:57
  76.9 1.4 shard_map.123
  78.3 0.0 collective-permute-done.2.shared_other_ref
  78.3 0.2 collective-permute-done.3.late_other_ref
  78.5 1.6 %shard_map.124 = bf16[16,528,128]{2,1,0:T(8,128)(2,1)S(1)} custom-call(bf16[256,1024]{1,0:T(8,128)(2,1)S(1)} %get-tuple-element.17.shared_ref, bf16[256,1024]{1,0:T(8,128)(2,1)S(1)} %collective-permute-done.2.shared_other_ref, bf16[400,512]{1,0:T(8,128)(2,1)S(1)} %get-tuple-element.22.late_ref, bf16[400,512]{1,0:T(8,128)(2,1)S(1)} %collective-permute-done.3.late_other_ref), custom_call_target="tpu_custom_call" | custom-call | tf_op jit(solution)/shard_map/pallas_call | solution.py:63
  80.1 32.3 %all_to_all.21.arrived_ref = bf16[16,528,128]{2,1,0:T(8,128)(2,1)S(1)} all-to-all(bf16[16,528,128]{2,1,0:T(8,128)(2,1)S(1)} %shard_map.124), channel_id=1, replica_groups=mesh['y'=4,'x'=4,'zh'=2,'c'=2,'s'=8] {'y','x'}, dimensions={0} | all-to-all | bytes 4325376 | tf_op jit(solution)/shard_map/all_to_all | solution.py:53
  112.4 0.3 shard_map.125
  112.7 27.4 %all_to_all.22.arrived_ref = bf16[16,64,128]{2,1,0:T(8,128)(2,1)S(1)} all-to-all(bf16[16,64,128]{2,1,0:T(8,128)(2,1)S(1)} %shard_map.125), channel_id=1, replica_groups=mesh['y'=4,'x'=4,'zh'=2,'c'=2,'s'=8] {'zh','s'}, dimensions={0} | all-to-all | bytes 524288 | tf_op jit(solution)/shard_map/all_to_all | solution.py:53
  140.1 0.7 shard_map.126
  (1 shorter events, 0.0 us)
Async XLA Ops:
  2.4 32.3 %all-to-all-start = ((bf16[8,160,128]{2,1,0:T(8,128)(2,1)}), bf16[8,160,128]{2,1,0:T(8,128)(2,1)S(1)}, u32[]{:S(2)}, u32[]{:S(2)}) async-start(bf16[8,160,128]{2,1,0:T(8,128)(2,1)} %shard_map.119), calls=%async_computation | async-start | bytes 655360 | tf_op jit(solution)/shard_map/all_to_all | solution.py:53
  15.0 0.7 copy-start.1
  15.7 0.7 copy-start.2
  16.5 12.6 %collective-permute-start = (bf16[128,128]{1,0:T(8,128)(2,1)S(1)}, bf16[128,128]{1,0:T(8,128)(2,1)S(1)}, u32[]{:S(2)}, u32[]{:S(2)}) collective-permute-start(bf16[128,128]{1,0:T(8,128)(2,1)S(1)} %shard_map.118.own_ref), channel_id=1, source_target_pairs={{0,20},{1,21},{2,22},{3,23},{4,16},{5,17},{6,18},{7,19},{16,4},{17... | collective-permute-start | bytes 98312 | tf_op jit(solution)/shard_map/ppermute | solution.py:455
  34.9 33.1 %copy-start = (bf16[2,128,512]{2,1,0:T(8,128)(2,1)S(1)}, bf16[2,128,512]{2,1,0:T(8,128)(2,1)}, u32[]{:S(2)}) copy-start(bf16[2,128,512]{2,1,0:T(8,128)(2,1)} %param.7) | copy-start | bytes 786436
  66.0 6.2 %copy-start.3 = (f32[3,512]{1,0:T(4,128)S(1)}, f32[3,512]{1,0:T(4,128)}, u32[]{:S(2)}) copy-start(f32[3,512]{1,0:T(4,128)} %gains_ref.1) | copy-start | bytes 18436
  66.0 6.2 %copy-start.4 = (f32[3,512]{1,0:T(4,128)S(1)}, f32[3,512]{1,0:T(4,128)}, u32[]{:S(2)}) copy-start(f32[3,512]{1,0:T(4,128)} %biases_ref.1) | copy-start | bytes 18436
  66.0 6.2 %collective-permute-start.1 = (bf16[8192,128]{1,0:T(8,128)(2,1)S(1)}, bf16[8192,128]{1,0:T(8,128)(2,1)S(1)}, u32[]{:S(2)}, u32[]{:S(2)}) collective-permute-start(bf16[8192,128]{1,0:T(8,128)(2,1)S(1)} %bitcast.6), channel_id=1, source_target_pairs={{0,8},{8,0},{1,9},{9,1},{2,10},{10,2},{3,11},{11,3},{4,12},{12,4},... | collective-permute-start | bytes 6291464 | tf_op jit(solution)/shard_map/ppermute | solution.py:57
  69.0 9.3 %collective-permute-start.2 = (bf16[256,1024]{1,0:T(8,128)(2,1)S(1)}, bf16[256,1024]{1,0:T(8,128)(2,1)S(1)}, u32[]{:S(2)}, u32[]{:S(2)}) collective-permute-start(bf16[256,1024]{1,0:T(8,128)(2,1)S(1)} %get-tuple-element.17.shared_ref), channel_id=1, source_target_pairs={{0,8},{8,0},{1,9},{9,1},{2,10},{10,2},{3,11},{11,3},{4,12},{12,4},... | collective-permute-start | bytes 1572872 | tf_op jit(solution)/shard_map/ppermute | solution.py:57
  74.8 3.6 %collective-permute-start.3 = (bf16[400,512]{1,0:T(8,128)(2,1)S(1)}, bf16[400,512]{1,0:T(8,128)(2,1)S(1)}, u32[]{:S(2)}, u32[]{:S(2)}) collective-permute-start(bf16[400,512]{1,0:T(8,128)(2,1)S(1)} %get-tuple-element.22.late_ref), channel_id=1, source_target_pairs={{0,8},{8,0},{1,9},{9,1},{2,10},{10,2},{3,11},{11,3},{4,12},{12,4},... | collective-permute-start | bytes 1228808 | tf_op jit(solution)/shard_map/ppermute | solution.py:57

commit v9 on v7

--- a/solution.py
+++ b/solution.py
@@ -288,9 +288,6 @@
     late_ref,
     late_other_ref,
     send_ref,
-    term_six_ref,
-    term_seven_ref,
-    term_proj_ref,
 ):
     core = lax.axis_index("c")
     frames, channels = shared_ref.shape[0] // 4, late_ref.shape[1]
@@ -304,38 +301,37 @@
     def late(start, stop):
         return both(start, stop, late_ref, late_other_ref)
 
+    def own_columns(rows, group):
+        chosen = one_hot(
+            (channels // 2, channels), lambda j: (j // group * 2 + core) * group + j % group
+        )
+        return matmul(rows, chosen, (1, 1)).astype(narrow)
+
     dhid_six, dhid_seven, normed = late(0, 2), late(4, 5), late(5, 6)
-    term_six_ref[:channels] = matmul(both(0, 2), dhid_six, (0, 0))
-    term_six_ref[channels:] = matmul(both(2, 4), dhid_six, (0, 0))
-    term_seven_ref[:channels] = matmul(late(2, 3), dhid_seven, (0, 0))
-    term_seven_ref[channels:] = matmul(late(3, 4), dhid_seven, (0, 0))
+    for tap in range(2):
+        first = tap * planes // 2
+        rows_six = own_columns(both(2 * tap, 2 * tap + 2), TILE)
+        rows_seven = own_columns(late(2 + tap, 3 + tap), TILE)
+        for start, term in (
+            (0, matmul(rows_six, dhid_six, (0, 0)).astype(narrow)),
+            (2 * lane_tiles, matmul(rows_seven, dhid_seven, (0, 0)).astype(narrow)),
+        ):
+            for group in range(planes):
+                for lane in range(lane_tiles):
+                    at = (start + group % 2 * lane_tiles + lane) * TILE
+                    send_ref[first + group // 2, at : at + TILE] = term[
+                        group * TILE : (group + 1) * TILE, lane * LANES : (lane + 1) * LANES
+                    ]
     grad_rows = jnp.concatenate(
         [cotangents_of(shared_ref, width), cotangents_of(shared_other_ref, width)], axis=0
     )
-    term_proj_ref[...] = matmul(normed, grad_rows, (0, 0))
-    half_rows = TILE // 2
-
-    def pack(plane, carry):
-        proj_rows = []
-        for half in range(2):
-            group = (plane * 2 + half) * 2 + core
-            rows = pl.ds(pl.multiple_of(group * TILE, TILE), TILE)
-            for lane in range(lane_tiles):
-                lanes = slice(lane * LANES, (lane + 1) * LANES)
-                at = (half * lane_tiles + lane) * TILE
-                send_ref[plane, at : at + TILE] = term_six_ref[rows, lanes].astype(narrow)
-                at += 2 * lane_tiles * TILE
-                send_ref[plane, at : at + TILE] = term_seven_ref[rows, lanes].astype(narrow)
-            proj_rows.append(
-                term_proj_ref[pl.ds(pl.multiple_of(group * half_rows, half_rows), half_rows)]
-            )
-        proj_block = jnp.concatenate(proj_rows, axis=0).astype(narrow)
+    term = matmul(own_columns(normed, TILE // 2), grad_rows, (0, 0)).astype(narrow)
+    for plane in range(planes):
         for lane in range(width // LANES):
             at = (4 * lane_tiles + lane) * TILE
-            send_ref[plane, at : at + TILE] = proj_block[:, lane * LANES : (lane + 1) * LANES]
-        return carry
-
-    lax.fori_loop(0, planes, pack, 0)
+            send_ref[plane, at : at + TILE] = term[
+                plane * TILE : (plane + 1) * TILE, lane * LANES : (lane + 1) * LANES
+            ]
     sums = (late_ref[6 * frames :].astype(wide) + late_other_ref[6 * frames :].astype(wide))[:6]
     sums = jnp.concatenate(
         [sums[:, lane * LANES : (lane + 1) * LANES] for lane in range(lane_tiles)], axis=0
@@ -497,11 +493,6 @@
         functools.partial(terms_kernel, width),
         shape((planes, send_rows, LANES), narrow),
         [shared, shared_other, late, late_other],
-        scratch=[
-            pltpu.VMEM((2 * channels, channels), wide),
-            pltpu.VMEM((2 * channels, channels), wide),
-            pltpu.VMEM((channels, width), wide),
-        ],
         megabytes=24,
     )
     plane_in = exchange(chip, ("y", "x"))

time: 140 us -> 140 us (level)
  no operation moved by 1% of the time
where the time goes in v9:
time: 140 us; the launch traced here: 139 us
  blocking collectives  89.7 us (64%)
  starting transfers between devices  27.3 us (20%)
  waiting for transfers between devices  10.2 us (7%)
  Pallas kernels  9.76 us (7%)
  local copies, waits for them, and re-layouts  1.45 us (1%)
    all_to_all x3, blocking collectives, exchange(): return lax.all_to_all(value, axes, 0, 0, tiled=True)  89.7 us
    all_to_all x1, starting transfers between devices, exchange(): return lax.all_to_all(value, axes, 0, 0, tiled=True)  12.6 us
    ppermute x1, starting transfers between devices, on_device(): other_convs = lax.ppermute(convs, ('zh', 's'), opposite)  8.21 us
    pallas_call x8, Pallas kernels, on_core(): pl.pallas_call(kernel, out_shape=out_shape, in_specs=[vmem] * len(arrays)...  8.02 us
    ppermute x3, starting transfers between devices, swap(): return lax.ppermute(value, axis, [(0, 1), (1, 0)])  6.5 us
    all_to_all x1, waiting for transfers between devices, exchange(): return lax.all_to_all(value, axes, 0, 0, tiled=True)  5.22 us
    ppermute x1, waiting for transfers between devices, on_device(): other_convs = lax.ppermute(convs, ('zh', 's'), opposite)  4.08 us
  transfers between devices with their start and end apart: 5, of which 4 were waited for; matrix products, arithmetic and copies ran while one was open for 0% of the time, Pallas kernels for 4%

profile of v9, /device:TPU:32, one launch (start us, length us, event | category | flops | bytes accessed | tf_op | source)
XLA Modules:
  0.0 139.2 jit_solution(18231668597366261891)
XLA Ops:
  0.6 1.7 %shard_map.119 = bf16[8,152,128]{2,1,0:T(8,128)(2,1)} custom-call(bf16[240,512]{1,0:T(8,128)(2,1)} %bitcast.12, bf16[16,4,1920]{2,1,0:T(4,128)(2,1)} %grad_hbm.1), custom_call_target="tpu_custom_call" | custom-call | tf_op jit(solution)/shard_map/pallas_call | solution.py:433
  2.4 12.6 %all-to-all-start = ((bf16[8,152,128]{2,1,0:T(8,128)(2,1)}), bf16[8,152,128]{2,1,0:T(8,128)(2,1)S(1)}, u32[]{:S(2)}, u32[]{:S(2)}) async-start(bf16[8,152,128]{2,1,0:T(8,128)(2,1)} %shard_map.119), calls=%async_computation | async-start | bytes 622592 | tf_op jit(solution)/shard_map/all_to_all | solution.py:53
  15.0 0.0 copy-start.1
  15.0 0.7 copy-done.1
  15.7 0.0 copy-start.2
  15.7 0.7 copy-done.2
  16.5 8.2 %collective-permute-start = (bf16[128,128]{1,0:T(8,128)(2,1)S(1)}, bf16[128,128]{1,0:T(8,128)(2,1)S(1)}, u32[]{:S(2)}, u32[]{:S(2)}) collective-permute-start(bf16[128,128]{1,0:T(8,128)(2,1)S(1)} %shard_map.118.own_ref), channel_id=1, source_target_pairs={{0,20},{1,21},{2,22},{3,23},{4,16},{5,17},{6,18},{7,19},{16,4},{17... | collective-permute-start | bytes 98312 | tf_op jit(solution)/shard_map/ppermute | solution.py:450
  24.7 4.1 %collective-permute-done.other_ref = bf16[128,128]{1,0:T(8,128)(2,1)S(1)} collective-permute-done((bf16[128,128]{1,0:T(8,128)(2,1)S(1)}, bf16[128,128]{1,0:T(8,128)(2,1)S(1)}, u32[]{:S(2)}, u32[]{:S(2)}) %collective-permute-start) | collective-permute-done | bytes 32800 | tf_op jit(solution)/shard_map/ppermute | solution.py:450
  28.8 5.2 %all-to-all-done.arrived_ref.grad_ref = bf16[8,152,128]{2,1,0:T(8,128)(2,1)S(1)} async-done(((bf16[8,152,128]{2,1,0:T(8,128)(2,1)}), bf16[8,152,128]{2,1,0:T(8,128)(2,1)S(1)}, u32[]{:S(2)}, u32[]{:S(2)}) %all-to-all-start) | async-done | bytes 311328 | tf_op jit(solution)/shard_map/all_to_all | solution.py:53
  34.0 0.3 shard_map.120
  34.2 0.0 copy-start
  34.3 30.9 %all_to_all.20 = bf16[16,512,128]{2,1,0:T(8,128)(2,1)S(1)} all-to-all(bf16[16,512,128]{2,1,0:T(8,128)(2,1)S(1)} %shard_map.120), channel_id=1, replica_groups=mesh['y'=4,'x'=4,'zh'=2,'c'=2,'s'=8] {'y','x'}, dimensions={0} | all-to-all | bytes 4194304 | tf_op jit(solution)/shard_map/all_to_all | solution.py:53
  65.1 0.0 copy-start.3
  65.1 0.0 copy-start.4
  65.1 2.0 %collective-permute-start.1 = (bf16[8192,128]{1,0:T(8,128)(2,1)S(1)}, bf16[8192,128]{1,0:T(8,128)(2,1)S(1)}, u32[]{:S(2)}, u32[]{:S(2)}) collective-permute-start(bf16[8192,128]{1,0:T(8,128)(2,1)S(1)} %bitcast.6), channel_id=1, source_target_pairs={{0,8},{8,0},{1,9},{9,1},{2,10},{10,2},{3,11},{11,3},{4,12},{12,4},... | collective-permute-start | bytes 6291464 | tf_op jit(solution)/shard_map/ppermute | solution.py:57
  67.2 0.0 copy-done
  67.2 1.0 shard_map.121
  68.1 2.4 %collective-permute-start.2 = (bf16[256,1024]{1,0:T(8,128)(2,1)S(1)}, bf16[256,1024]{1,0:T(8,128)(2,1)S(1)}, u32[]{:S(2)}, u32[]{:S(2)}) collective-permute-start(bf16[256,1024]{1,0:T(8,128)(2,1)S(1)} %get-tuple-element.17.shared_ref), channel_id=1, source_target_pairs={{0,8},{8,0},{1,9},{9,1},{2,10},{10,2},{3,11},{11,3},{4,12},{12,4},... | collective-permute-start | bytes 1572872 | tf_op jit(solution)/shard_map/ppermute | solution.py:57
  70.6 0.7 collective-permute-done.1
  71.3 0.0 copy-done.3
  71.3 0.0 copy-done.4
  71.3 2.7 %shard_map.122 = (bf16[1024,512]{1,0:T(8,128)(2,1)S(1)}, bf16[400,512]{1,0:T(8,128)(2,1)S(1)}) custom-call(bf16[256,1024]{1,0:T(8,128)(2,1)S(1)} %get-tuple-element.17.shared_ref, bf16[16,32,16,128]{3,2,1,0:T(8,128)(2,1)S(1)} %bitcast.8, bf16[16,32,16,128]{3,2,1,0:T(8,128)(2,1)S(1)} %bitcast.9, f32[64,256]{1,0:T(8,128)S(1)} %get-tuple-element.18.part_ref, ...), custom_call_target="tpu_custom_call" | custom-call | tf_op jit(solution)/shard_map/pallas_call | solution.py:63
  74.0 2.0 %collective-permute-start.3 = (bf16[400,512]{1,0:T(8,128)(2,1)S(1)}, bf16[400,512]{1,0:T(8,128)(2,1)S(1)}, u32[]{:S(2)}, u32[]{:S(2)}) collective-permute-start(bf16[400,512]{1,0:T(8,128)(2,1)S(1)} %get-tuple-element.22.late_ref), channel_id=1, source_target_pairs={{0,8},{8,0},{1,9},{9,1},{2,10},{10,2},{3,11},{11,3},{4,12},{12,4},... | collective-permute-start | bytes 1228808 | tf_op jit(solution)/shard_map/ppermute | solution.py:57
  76.0 1.4 shard_map.123
  77.4 0.0 collective-permute-done.2.shared_other_ref
  77.4 0.2 collective-permute-done.3.late_other_ref
  77.6 1.7 %shard_map.124 = bf16[16,520,128]{2,1,0:T(8,128)(2,1)S(1)} custom-call(bf16[256,1024]{1,0:T(8,128)(2,1)S(1)} %get-tuple-element.17.shared_ref, bf16[256,1024]{1,0:T(8,128)(2,1)S(1)} %collective-permute-done.2.shared_other_ref, bf16[400,512]{1,0:T(8,128)(2,1)S(1)} %get-tuple-element.22.late_ref, bf16[400,512]{1,0:T(8,128)(2,1)S(1)} %collective-permute-done.3.late_other_ref), custom_call_target="tpu_custom_call" | custom-call | tf_op jit(solution)/shard_map/pallas_call | solution.py:63
  79.3 32.1 %all_to_all.21.arrived_ref = bf16[16,520,128]{2,1,0:T(8,128)(2,1)S(1)} all-to-all(bf16[16,520,128]{2,1,0:T(8,128)(2,1)S(1)} %shard_map.124), channel_id=1, replica_groups=mesh['y'=4,'x'=4,'zh'=2,'c'=2,'s'=8] {'y','x'}, dimensions={0} | all-to-all | bytes 4259840 | tf_op jit(solution)/shard_map/all_to_all | solution.py:53
  111.4 0.3 shard_map.125
  111.8 26.8 %all_to_all.22.arrived_ref = bf16[16,56,128]{2,1,0:T(8,128)(2,1)S(1)} all-to-all(bf16[16,56,128]{2,1,0:T(8,128)(2,1)S(1)} %shard_map.125), channel_id=1, replica_groups=mesh['y'=4,'x'=4,'zh'=2,'c'=2,'s'=8] {'zh','s'}, dimensions={0} | all-to-all | bytes 458752 | tf_op jit(solution)/shard_map/all_to_all | solution.py:53
  138.5 0.7 shard_map.126
  (1 shorter events, 0.0 us)
Async XLA Ops:
  2.4 31.6 %all-to-all-start = ((bf16[8,152,128]{2,1,0:T(8,128)(2,1)}), bf16[8,152,128]{2,1,0:T(8,128)(2,1)S(1)}, u32[]{:S(2)}, u32[]{:S(2)}) async-start(bf16[8,152,128]{2,1,0:T(8,128)(2,1)} %shard_map.119), calls=%async_computation | async-start | bytes 622592 | tf_op jit(solution)/shard_map/all_to_all | solution.py:53
  15.0 0.7 copy-start.1
  15.7 0.7 copy-start.2
  16.5 12.3 %collective-permute-start = (bf16[128,128]{1,0:T(8,128)(2,1)S(1)}, bf16[128,128]{1,0:T(8,128)(2,1)S(1)}, u32[]{:S(2)}, u32[]{:S(2)}) collective-permute-start(bf16[128,128]{1,0:T(8,128)(2,1)S(1)} %shard_map.118.own_ref), channel_id=1, source_target_pairs={{0,20},{1,21},{2,22},{3,23},{4,16},{5,17},{6,18},{7,19},{16,4},{17... | collective-permute-start | bytes 98312 | tf_op jit(solution)/shard_map/ppermute | solution.py:450
  34.2 32.9 %copy-start = (bf16[2,128,512]{2,1,0:T(8,128)(2,1)S(1)}, bf16[2,128,512]{2,1,0:T(8,128)(2,1)}, u32[]{:S(2)}) copy-start(bf16[2,128,512]{2,1,0:T(8,128)(2,1)} %param.7) | copy-start | bytes 786436
  65.1 6.2 %copy-start.3 = (f32[3,512]{1,0:T(4,128)S(1)}, f32[3,512]{1,0:T(4,128)}, u32[]{:S(2)}) copy-start(f32[3,512]{1,0:T(4,128)} %gains_ref.1) | copy-start | bytes 18436
  65.1 6.2 %copy-start.4 = (f32[3,512]{1,0:T(4,128)S(1)}, f32[3,512]{1,0:T(4,128)}, u32[]{:S(2)}) copy-start(f32[3,512]{1,0:T(4,128)} %biases_ref.1) | copy-start | bytes 18436
  65.1 6.2 %collective-permute-start.1 = (bf16[8192,128]{1,0:T(8,128)(2,1)S(1)}, bf16[8192,128]{1,0:T(8,128)(2,1)S(1)}, u32[]{:S(2)}, u32[]{:S(2)}) collective-permute-start(bf16[8192,128]{1,0:T(8,128)(2,1)S(1)} %bitcast.6), channel_id=1, source_target_pairs={{0,8},{8,0},{1,9},{9,1},{2,10},{10,2},{3,11},{11,3},{4,12},{12,4},... | collective-permute-start | bytes 6291464 | tf_op jit(solution)/shard_map/ppermute | solution.py:57
  68.1 9.3 %collective-permute-start.2 = (bf16[256,1024]{1,0:T(8,128)(2,1)S(1)}, bf16[256,1024]{1,0:T(8,128)(2,1)S(1)}, u32[]{:S(2)}, u32[]{:S(2)}) collective-permute-start(bf16[256,1024]{1,0:T(8,128)(2,1)S(1)} %get-tuple-element.17.shared_ref), channel_id=1, source_target_pairs={{0,8},{8,0},{1,9},{9,1},{2,10},{10,2},{3,11},{11,3},{4,12},{12,4},... | collective-permute-start | bytes 1572872 | tf_op jit(solution)/shard_map/ppermute | solution.py:57
  74.0 3.6 %collective-permute-start.3 = (bf16[400,512]{1,0:T(8,128)(2,1)S(1)}, bf16[400,512]{1,0:T(8,128)(2,1)S(1)}, u32[]{:S(2)}, u32[]{:S(2)}) collective-permute-start(bf16[400,512]{1,0:T(8,128)(2,1)S(1)} %get-tuple-element.22.late_ref), channel_id=1, source_target_pairs={{0,8},{8,0},{1,9},{9,1},{2,10},{10,2},{3,11},{11,3},{4,12},{12,4},... | collective-permute-start | bytes 1228808 | tf_op jit(solution)/shard_map/ppermute | solution.py:57

commit v10 on v9

--- a/solution.py
+++ b/solution.py
@@ -313,15 +313,15 @@
         rows_six = own_columns(both(2 * tap, 2 * tap + 2), TILE)
         rows_seven = own_columns(late(2 + tap, 3 + tap), TILE)
         for start, term in (
-            (0, matmul(rows_six, dhid_six, (0, 0)).astype(narrow)),
-            (2 * lane_tiles, matmul(rows_seven, dhid_seven, (0, 0)).astype(narrow)),
+            (0, matmul(rows_six, dhid_six, (0, 0))),
+            (2 * lane_tiles, matmul(rows_seven, dhid_seven, (0, 0))),
         ):
             for group in range(planes):
                 for lane in range(lane_tiles):
                     at = (start + group % 2 * lane_tiles + lane) * TILE
                     send_ref[first + group // 2, at : at + TILE] = term[
                         group * TILE : (group + 1) * TILE, lane * LANES : (lane + 1) * LANES
-                    ]
+                    ].astype(narrow)
     grad_rows = jnp.concatenate(
         [cotangents_of(shared_ref, width), cotangents_of(shared_other_ref, width)], axis=0
     )

time: 140 us -> 140 us (level)
  no operation moved by 1% of the time
where the time goes in v10:
time: 140 us; the launch traced here: 139 us
  blocking collectives  89.7 us (64%)
  starting transfers between devices  27.3 us (20%)
  waiting for transfers between devices  10.2 us (7%)
  Pallas kernels  9.76 us (7%)
  local copies, waits for them, and re-layouts  1.45 us (1%)
    all_to_all x3, blocking collectives, exchange(): return lax.all_to_all(value, axes, 0, 0, tiled=True)  89.7 us
    all_to_all x1, starting transfers between devices, exchange(): return lax.all_to_all(value, axes, 0, 0, tiled=True)  12.6 us
    ppermute x1, starting transfers between devices, on_device(): other_convs = lax.ppermute(convs, ('zh', 's'), opposite)  8.21 us
    pallas_call x8, Pallas kernels, on_core(): pl.pallas_call(kernel, out_shape=out_shape, in_specs=[vmem] * len(arrays)...  8.02 us
    ppermute x3, starting transfers between devices, swap(): return lax.ppermute(value, axis, [(0, 1), (1, 0)])  6.5 us
    all_to_all x1, waiting for transfers between devices, exchange(): return lax.all_to_all(value, axes, 0, 0, tiled=True)  5.22 us
    ppermute x1, waiting for transfers between devices, on_device(): other_convs = lax.ppermute(convs, ('zh', 's'), opposite)  4.08 us
  transfers between devices with their start and end apart: 5, of which 4 were waited for; matrix products, arithmetic and copies ran while one was open for 0% of the time, Pallas kernels for 4%

profile of v10, /device:TPU:32, one launch (start us, length us, event | category | flops | bytes accessed | tf_op | source)
XLA Modules:
  0.0 139.2 jit_solution(18231668597366261891)
XLA Ops:
  0.6 1.7 %shard_map.119 = bf16[8,152,128]{2,1,0:T(8,128)(2,1)} custom-call(bf16[240,512]{1,0:T(8,128)(2,1)} %bitcast.12, bf16[16,4,1920]{2,1,0:T(4,128)(2,1)} %grad_hbm.1), custom_call_target="tpu_custom_call" | custom-call | tf_op jit(solution)/shard_map/pallas_call | solution.py:433
  2.4 12.6 %all-to-all-start = ((bf16[8,152,128]{2,1,0:T(8,128)(2,1)}), bf16[8,152,128]{2,1,0:T(8,128)(2,1)S(1)}, u32[]{:S(2)}, u32[]{:S(2)}) async-start(bf16[8,152,128]{2,1,0:T(8,128)(2,1)} %shard_map.119), calls=%async_computation | async-start | bytes 622592 | tf_op jit(solution)/shard_map/all_to_all | solution.py:53
  15.0 0.0 copy-start.1
  15.0 0.7 copy-done.1
  15.7 0.0 copy-start.2
  15.7 0.7 copy-done.2
  16.5 8.2 %collective-permute-start = (bf16[128,128]{1,0:T(8,128)(2,1)S(1)}, bf16[128,128]{1,0:T(8,128)(2,1)S(1)}, u32[]{:S(2)}, u32[]{:S(2)}) collective-permute-start(bf16[128,128]{1,0:T(8,128)(2,1)S(1)} %shard_map.118.own_ref), channel_id=1, source_target_pairs={{0,20},{1,21},{2,22},{3,23},{4,16},{5,17},{6,18},{7,19},{16,4},{17... | collective-permute-start | bytes 98312 | tf_op jit(solution)/shard_map/ppermute | solution.py:450
  24.7 4.1 %collective-permute-done.other_ref = bf16[128,128]{1,0:T(8,128)(2,1)S(1)} collective-permute-done((bf16[128,128]{1,0:T(8,128)(2,1)S(1)}, bf16[128,128]{1,0:T(8,128)(2,1)S(1)}, u32[]{:S(2)}, u32[]{:S(2)}) %collective-permute-start) | collective-permute-done | bytes 32800 | tf_op jit(solution)/shard_map/ppermute | solution.py:450
  28.8 5.2 %all-to-all-done.arrived_ref.grad_ref = bf16[8,152,128]{2,1,0:T(8,128)(2,1)S(1)} async-done(((bf16[8,152,128]{2,1,0:T(8,128)(2,1)}), bf16[8,152,128]{2,1,0:T(8,128)(2,1)S(1)}, u32[]{:S(2)}, u32[]{:S(2)}) %all-to-all-start) | async-done | bytes 311328 | tf_op jit(solution)/shard_map/all_to_all | solution.py:53
  34.0 0.3 shard_map.120
  34.2 0.0 copy-start
  34.3 30.9 %all_to_all.20 = bf16[16,512,128]{2,1,0:T(8,128)(2,1)S(1)} all-to-all(bf16[16,512,128]{2,1,0:T(8,128)(2,1)S(1)} %shard_map.120), channel_id=1, replica_groups=mesh['y'=4,'x'=4,'zh'=2,'c'=2,'s'=8] {'y','x'}, dimensions={0} | all-to-all | bytes 4194304 | tf_op jit(solution)/shard_map/all_to_all | solution.py:53
  65.1 0.0 copy-start.3
  65.1 0.0 copy-start.4
  65.1 2.0 %collective-permute-start.1 = (bf16[8192,128]{1,0:T(8,128)(2,1)S(1)}, bf16[8192,128]{1,0:T(8,128)(2,1)S(1)}, u32[]{:S(2)}, u32[]{:S(2)}) collective-permute-start(bf16[8192,128]{1,0:T(8,128)(2,1)S(1)} %bitcast.6), channel_id=1, source_target_pairs={{0,8},{8,0},{1,9},{9,1},{2,10},{10,2},{3,11},{11,3},{4,12},{12,4},... | collective-permute-start | bytes 6291464 | tf_op jit(solution)/shard_map/ppermute | solution.py:57
  67.2 0.0 copy-done
  67.2 1.0 shard_map.121
  68.1 2.4 %collective-permute-start.2 = (bf16[256,1024]{1,0:T(8,128)(2,1)S(1)}, bf16[256,1024]{1,0:T(8,128)(2,1)S(1)}, u32[]{:S(2)}, u32[]{:S(2)}) collective-permute-start(bf16[256,1024]{1,0:T(8,128)(2,1)S(1)} %get-tuple-element.17.shared_ref), channel_id=1, source_target_pairs={{0,8},{8,0},{1,9},{9,1},{2,10},{10,2},{3,11},{11,3},{4,12},{12,4},... | collective-permute-start | bytes 1572872 | tf_op jit(solution)/shard_map/ppermute | solution.py:57
  70.6 0.7 collective-permute-done.1
  71.3 0.0 copy-done.3
  71.3 0.0 copy-done.4
  71.3 2.7 %shard_map.122 = (bf16[1024,512]{1,0:T(8,128)(2,1)S(1)}, bf16[400,512]{1,0:T(8,128)(2,1)S(1)}) custom-call(bf16[256,1024]{1,0:T(8,128)(2,1)S(1)} %get-tuple-element.17.shared_ref, bf16[16,32,16,128]{3,2,1,0:T(8,128)(2,1)S(1)} %bitcast.8, bf16[16,32,16,128]{3,2,1,0:T(8,128)(2,1)S(1)} %bitcast.9, f32[64,256]{1,0:T(8,128)S(1)} %get-tuple-element.18.part_ref, ...), custom_call_target="tpu_custom_call" | custom-call | tf_op jit(solution)/shard_map/pallas_call | solution.py:63
  74.0 2.0 %collective-permute-start.3 = (bf16[400,512]{1,0:T(8,128)(2,1)S(1)}, bf16[400,512]{1,0:T(8,128)(2,1)S(1)}, u32[]{:S(2)}, u32[]{:S(2)}) collective-permute-start(bf16[400,512]{1,0:T(8,128)(2,1)S(1)} %get-tuple-element.22.late_ref), channel_id=1, source_target_pairs={{0,8},{8,0},{1,9},{9,1},{2,10},{10,2},{3,11},{11,3},{4,12},{12,4},... | collective-permute-start | bytes 1228808 | tf_op jit(solution)/shard_map/ppermute | solution.py:57
  76.0 1.4 shard_map.123
  77.4 0.0 collective-permute-done.2.shared_other_ref
  77.4 0.2 collective-permute-done.3.late_other_ref
  77.6 1.7 %shard_map.124 = bf16[16,520,128]{2,1,0:T(8,128)(2,1)S(1)} custom-call(bf16[256,1024]{1,0:T(8,128)(2,1)S(1)} %get-tuple-element.17.shared_ref, bf16[256,1024]{1,0:T(8,128)(2,1)S(1)} %collective-permute-done.2.shared_other_ref, bf16[400,512]{1,0:T(8,128)(2,1)S(1)} %get-tuple-element.22.late_ref, bf16[400,512]{1,0:T(8,128)(2,1)S(1)} %collective-permute-done.3.late_other_ref), custom_call_target="tpu_custom_call" | custom-call | tf_op jit(solution)/shard_map/pallas_call | solution.py:63
  79.3 32.1 %all_to_all.21.arrived_ref = bf16[16,520,128]{2,1,0:T(8,128)(2,1)S(1)} all-to-all(bf16[16,520,128]{2,1,0:T(8,128)(2,1)S(1)} %shard_map.124), channel_id=1, replica_groups=mesh['y'=4,'x'=4,'zh'=2,'c'=2,'s'=8] {'y','x'}, dimensions={0} | all-to-all | bytes 4259840 | tf_op jit(solution)/shard_map/all_to_all | solution.py:53
  111.4 0.3 shard_map.125
  111.8 26.8 %all_to_all.22.arrived_ref = bf16[16,56,128]{2,1,0:T(8,128)(2,1)S(1)} all-to-all(bf16[16,56,128]{2,1,0:T(8,128)(2,1)S(1)} %shard_map.125), channel_id=1, replica_groups=mesh['y'=4,'x'=4,'zh'=2,'c'=2,'s'=8] {'zh','s'}, dimensions={0} | all-to-all | bytes 458752 | tf_op jit(solution)/shard_map/all_to_all | solution.py:53
  138.5 0.7 shard_map.126
  (1 shorter events, 0.0 us)
Async XLA Ops:
  2.4 31.6 %all-to-all-start = ((bf16[8,152,128]{2,1,0:T(8,128)(2,1)}), bf16[8,152,128]{2,1,0:T(8,128)(2,1)S(1)}, u32[]{:S(2)}, u32[]{:S(2)}) async-start(bf16[8,152,128]{2,1,0:T(8,128)(2,1)} %shard_map.119), calls=%async_computation | async-start | bytes 622592 | tf_op jit(solution)/shard_map/all_to_all | solution.py:53
  15.0 0.7 copy-start.1
  15.7 0.7 copy-start.2
  16.5 12.3 %collective-permute-start = (bf16[128,128]{1,0:T(8,128)(2,1)S(1)}, bf16[128,128]{1,0:T(8,128)(2,1)S(1)}, u32[]{:S(2)}, u32[]{:S(2)}) collective-permute-start(bf16[128,128]{1,0:T(8,128)(2,1)S(1)} %shard_map.118.own_ref), channel_id=1, source_target_pairs={{0,20},{1,21},{2,22},{3,23},{4,16},{5,17},{6,18},{7,19},{16,4},{17... | collective-permute-start | bytes 98312 | tf_op jit(solution)/shard_map/ppermute | solution.py:450
  34.2 32.9 %copy-start = (bf16[2,128,512]{2,1,0:T(8,128)(2,1)S(1)}, bf16[2,128,512]{2,1,0:T(8,128)(2,1)}, u32[]{:S(2)}) copy-start(bf16[2,128,512]{2,1,0:T(8,128)(2,1)} %param.7) | copy-start | bytes 786436
  65.1 6.2 %copy-start.3 = (f32[3,512]{1,0:T(4,128)S(1)}, f32[3,512]{1,0:T(4,128)}, u32[]{:S(2)}) copy-start(f32[3,512]{1,0:T(4,128)} %gains_ref.1) | copy-start | bytes 18436
  65.1 6.2 %copy-start.4 = (f32[3,512]{1,0:T(4,128)S(1)}, f32[3,512]{1,0:T(4,128)}, u32[]{:S(2)}) copy-start(f32[3,512]{1,0:T(4,128)} %biases_ref.1) | copy-start | bytes 18436
  65.1 6.2 %collective-permute-start.1 = (bf16[8192,128]{1,0:T(8,128)(2,1)S(1)}, bf16[8192,128]{1,0:T(8,128)(2,1)S(1)}, u32[]{:S(2)}, u32[]{:S(2)}) collective-permute-start(bf16[8192,128]{1,0:T(8,128)(2,1)S(1)} %bitcast.6), channel_id=1, source_target_pairs={{0,8},{8,0},{1,9},{9,1},{2,10},{10,2},{3,11},{11,3},{4,12},{12,4},... | collective-permute-start | bytes 6291464 | tf_op jit(solution)/shard_map/ppermute | solution.py:57
  68.1 9.3 %collective-permute-start.2 = (bf16[256,1024]{1,0:T(8,128)(2,1)S(1)}, bf16[256,1024]{1,0:T(8,128)(2,1)S(1)}, u32[]{:S(2)}, u32[]{:S(2)}) collective-permute-start(bf16[256,1024]{1,0:T(8,128)(2,1)S(1)} %get-tuple-element.17.shared_ref), channel_id=1, source_target_pairs={{0,8},{8,0},{1,9},{9,1},{2,10},{10,2},{3,11},{11,3},{4,12},{12,4},... | collective-permute-start | bytes 1572872 | tf_op jit(solution)/shard_map/ppermute | solution.py:57
  74.0 3.6 %collective-permute-start.3 = (bf16[400,512]{1,0:T(8,128)(2,1)S(1)}, bf16[400,512]{1,0:T(8,128)(2,1)S(1)}, u32[]{:S(2)}, u32[]{:S(2)}) collective-permute-start(bf16[400,512]{1,0:T(8,128)(2,1)S(1)} %get-tuple-element.22.late_ref), channel_id=1, source_target_pairs={{0,8},{8,0},{1,9},{9,1},{2,10},{10,2},{3,11},{11,3},{4,12},{12,4},... | collective-permute-start | bytes 1228808 | tf_op jit(solution)/shard_map/ppermute | solution.py:57
